TPU v7x, 256 devices: a whole 4x4x8 slice. The times are simulated.
256 devices in a mesh: cfg: 2 (over x_lo), gx: 16 (over x_hi, y, core), gy: 8 (over z).
Axes of the slice: x: 4 (x_hi: 2, x_lo: 2; x = x_hi * 2 + x_lo), y: 4, z: 8, core: 2. Of those that a mesh axis runs over, the one named last changes fastest.
Arguments:
- latent: float32 [64, 128, 32, 128], P('gx', 'gy'), may hold values from -6 to 6
- sample_noise: bfloat16 [2, 64, 128, 32, 128], P(None, 'gx', 'gy'), may hold values from -6 to 6
- cond_field: bfloat16 [64, 128, 8, 128], P('gx', 'gy'), may hold values from -6 to 6
- timesteps: int32 [3], replicated, may hold values from 301 to 599, as said below
- spatial_weight: bfloat16 [3, 3, 128, 32], replicated, may hold values from -0.375 to 0.375
- cond_weight: bfloat16 [128, 8], replicated, may hold values from -2 to 2
- temporal_weight: bfloat16 [3, 32, 128], replicated, may hold values from -0.3125 to 0.3125
Outputs:
- sampled: float32 [64, 128, 32, 128], P('gx', 'gy')
Inputs may be any that keep to these rules, and one draw needn't show every extreme that they name: `timesteps`: strictly falling, the first is 599, each later one 60 to 149 below the one before.
All inputs are finite; a program needn't handle non-finite values.
Results may differ from a plain program's by a relative error of at most 0.012.
Values may be sent and summed in bfloat16 or wider, within the bound.
No kernel may reach another device: no remote copies, remote signals or barrier semaphores. Data moves between devices by JAX's collectives and lax.ppermute only.
A program may use at most 128 MiB of HBM per device.

v0:
```python
import jax
import jax.numpy as jnp
from jax import lax
from jax.sharding import PartitionSpec as P

STEPS = 2


GUIDANCE = 3.0
DDIM_ETA = 0.5


def padded_2(block, sides, width):
    for axis, dim in sides:
        count = lax.axis_size(axis)
        forward = [(i, i + 1) for i in range(count - 1)]
        backward = [(target, source) for source, target in forward]
        low = lax.ppermute(
            lax.slice_in_dim(block, block.shape[dim] - width, None, axis=dim), axis, forward
        )
        high = lax.ppermute(lax.slice_in_dim(block, 0, width, axis=dim), axis, backward)
        block = jnp.concatenate([low, block, high], axis=dim)
    return block


def partner(block, axis, stride):
    count = lax.axis_size(axis)
    route = []
    for low in range(count):
        high = low | 1 << stride
        if high != low and high < count:
            route += [(low, high), (high, low)]
    return lax.ppermute(block, axis, route)


def alpha_table():
    positions = jnp.arange(1000, dtype=jnp.int32)
    beta_values = 0.0001 + (0.02 - 0.0001) * positions.astype(jnp.float32) / 999.0
    return (positions, jnp.exp(jnp.cumsum(jnp.log(1.0 - beta_values))))


def lookup(positions, table, when):
    return jnp.sum(jnp.where(positions == when, table, jnp.float32(0.0)))


def ddim_update(current, guided, fresh_noise, alpha_now, alpha_next):
    clean_estimate = (current - jnp.sqrt(1.0 - alpha_now) * guided) / jnp.sqrt(alpha_now)
    noise_scale = (
        DDIM_ETA
        * jnp.sqrt((1.0 - alpha_next) / (1.0 - alpha_now))
        * jnp.sqrt(1.0 - alpha_now / alpha_next)
    )
    return (
        jnp.sqrt(alpha_next) * clean_estimate
        + jnp.sqrt(1.0 - alpha_next - noise_scale * noise_scale) * guided
        + noise_scale * fresh_noise.astype(jnp.float32)
    )


def spatial(padded, row_count, spatial_weight):
    col_count = padded.shape[1] - 2
    summed = None
    for row_off in range(3):
        for col_off in range(3):
            term = jnp.einsum(
                "xyct,fc->xyft",
                padded[row_off : row_off + row_count, col_off : col_off + col_count],
                spatial_weight[row_off, col_off],
                preferred_element_type=jnp.float32,
            )
            summed = term if summed is None else summed + term
    return summed


def finish(summed, normed, temporal_weight):
    hidden = jax.nn.silu(summed).astype(jnp.bfloat16)
    length = hidden.shape[-1]
    shifted = jnp.pad(hidden, ((0, 0), (0, 0), (0, 0), (1, 1)))
    output_sum = normed
    for tap_index in range(3):
        output_sum = output_sum + jnp.einsum(
            "xyft,cf->xyct",
            shifted[:, :, :, tap_index : tap_index + length],
            temporal_weight[tap_index],
            preferred_element_type=jnp.float32,
        )
    return output_sum.astype(jnp.bfloat16)


def guide(eps_cond, eps_free):
    free_value = eps_free.astype(jnp.float32)
    return free_value + GUIDANCE * (eps_cond.astype(jnp.float32) - free_value)


def normalize(current):
    return current * lax.rsqrt(jnp.mean(current * current, axis=(2, 3), keepdims=True) + 1e-05)


def on_device(
    latent, sample_noise, cond_field, timesteps, spatial_weight, cond_weight, temporal_weight
):
    positions, table = alpha_table()
    branch = lax.axis_index("cfg")
    row_total = latent.shape[0]
    current = latent
    for step_index in range(STEPS):
        alpha_now = lookup(positions, table, timesteps[step_index])
        alpha_next = lookup(positions, table, timesteps[step_index + 1])
        normed = normalize(current)
        act = jax.nn.silu(normed).astype(jnp.bfloat16)
        padded = padded_2(act, (("gx", 0), ("gy", 1)), 1)
        summed = spatial(padded, row_total, spatial_weight)
        cond_term = jnp.einsum(
            "xykt,fk->xyft", cond_field, cond_weight, preferred_element_type=jnp.float32
        )
        cond_flag = (branch == 0).astype(jnp.float32)
        own_eps = finish(summed + cond_flag * cond_term, normed, temporal_weight)
        partner_eps = partner(own_eps, "cfg", 0)
        eps_cond = jnp.where(branch == 0, own_eps, partner_eps)
        eps_free = jnp.where(branch == 0, partner_eps, own_eps)
        current = ddim_update(
            current, guide(eps_cond, eps_free), sample_noise[step_index], alpha_now, alpha_next
        )
    return current


def solution(mesh):
    in_specs = (
        P("gx", "gy", None, None),
        P(None, "gx", "gy", None, None),
        P("gx", "gy", None, None),
        P(),
        P(),
        P(),
        P(),
    )
    out_specs = P("gx", "gy", None, None)
    return jax.shard_map(
        on_device, mesh=mesh, in_specs=in_specs, out_specs=out_specs, check_vma=False
    )
```

profile of v0, /device:TPU:121, one launch (start us, length us, event | category | flops | bytes accessed | tf_op | source)
XLA Modules:
  0.0 136.3 jit_solution(11183112686050090140)
XLA Ops:
  0.0 0.0 copy-start
  0.0 1.5 %multiply_reduce_fusion.1 = f32[4,16]{1,0:T(4,128)S(1)} fusion(f32[4,16,32,128]{3,2,1,0:T(8,128)} %param.7), kind=kLoop, calls=%fused_computation.41 | loop fusion | flops 524224 | bytes 1048832 | tf_op jit(solution)/shard_map/reduce_sum | solution.py:96
  1.5 1.6 %multiply_convert_fusion.3 = bf16[4,16,32,128]{3,2,1,0:T(8,128)(2,1)S(1)} fusion(f32[4,16,32,128]{3,2,1,0:T(8,128)} %param.7, f32[4,16]{1,0:T(4,128)S(1)} %add_rsqrt_fusion.1), kind=kLoop, calls=%fused_computation.40 | loop fusion | flops 1572864 | bytes 1573120 | tf_op jit(solution)/shard_map/convert_element_type | solution.py:110
  3.1 4.9 %collective-permute-start = (bf16[1,16,32,128]{3,2,1,0:T(8,128)(2,1)S(1)}, bf16[1,16,32,128]{3,2,1,0:T(8,128)(2,1)S(1)}, u32[]{:S(2)}, u32[]{:S(2)}) collective-permute-start(bf16[1,16,32,128]{3,2,1,0:T(8,128)(2,1)S(1)} %get-tuple-element.16), channel_id=1, source_target_pairs={{0,8},{8,16},{16,24},{24,32},{32,40},{40,48},{48,56},{56,64},{64,7... | collective-permute-start | bytes 393224 | tf_op jit(solution)/shard_map/ppermute | solution.py:18
  8.0 0.0 copy-start.12
  8.0 1.9 %collective-permute-start.1 = (bf16[1,16,32,128]{3,2,1,0:T(8,128)(2,1)S(1)}, bf16[1,16,32,128]{3,2,1,0:T(8,128)(2,1)S(1)}, u32[]{:S(2)}, u32[]{:S(2)}) collective-permute-start(bf16[1,16,32,128]{3,2,1,0:T(8,128)(2,1)S(1)} %get-tuple-element.17), channel_id=1, source_target_pairs={{8,0},{16,8},{24,16},{32,24},{40,32},{48,40},{56,48},{64,56},{72,6... | collective-permute-start | bytes 393224 | tf_op jit(solution)/shard_map/ppermute | solution.py:21
  10.0 2.7 %fusion.92 = f32[4,16,128,128]{3,2,1,0:T(8,128)} fusion(bf16[4,16,32,128]{3,2,1,0:T(8,128)(2,1)S(1)} %multiply_convert_fusion.3, bf16[3,3,128,32]{2,3,1,0:T(8,128)(2,1)S(1)} %copy-done.9), kind=kOutput, calls=%fused_computation.90 | convolution fusion | flops 67108864 | bytes 4726784 | tf_op jit(solution)/shard_map/xyct,fc->xyft/dot_general | solution.py:65
  12.7 2.9 %fusion.132 = f32[128,4,16,128]{0,3,2,1:T(8,128)} fusion(bf16[4,16,8,128]{3,2,1,0:T(8,128)(2,1)S(1)} %copy-done, bf16[128,8]{0,1:T(8,128)(2,1)S(1)} %copy-done.12), kind=kOutput, calls=%fused_computation.141 | convolution fusion | flops 16777216 | bytes 4327424 | tf_op jit(solution)/shard_map/xykt,fk->xyft/dot_general | solution.py:113
  15.6 0.3 reduce-window.9
  15.9 0.1 slice.177
  16.0 0.0 collective-permute-done
  16.0 1.9 %collective-permute-done.1 = bf16[1,16,32,128]{3,2,1,0:T(8,128)(2,1)S(1)} collective-permute-done((bf16[1,16,32,128]{3,2,1,0:T(8,128)(2,1)S(1)}, bf16[1,16,32,128]{3,2,1,0:T(8,128)(2,1)S(1)}, u32[]{:S(2)}, u32[]{:S(2)}) %collective-permute-start.1) | collective-permute-done | bytes 131104 | tf_op jit(solution)/shard_map/ppermute | solution.py:21
  17.9 1.9 %collective-permute-start.3 = (bf16[6,1,32,128]{3,2,1,0:T(8,128)(2,1)S(1)}, bf16[6,1,32,128]{3,2,1,0:T(8,128)(2,1)S(1)}, u32[]{:S(2)}, u32[]{:S(2)}) collective-permute-start(bf16[6,1,32,128]{3,2,1,0:T(8,128)(2,1)S(1)} %get-tuple-element.12), channel_id=1, source_target_pairs={{1,0},{2,1},{3,2},{4,3},{5,4},{6,5},{7,6},{9,8},{10,9},{11,10},{12... | collective-permute-start | bytes 147464 | tf_op jit(solution)/shard_map/ppermute | solution.py:21
  19.9 4.8 %collective-permute-start.2 = (bf16[6,1,32,128]{3,2,1,0:T(8,128)(2,1)S(1)}, bf16[6,1,32,128]{3,2,1,0:T(8,128)(2,1)S(1)}, u32[]{:S(2)}, u32[]{:S(2)}) collective-permute-start(bf16[6,1,32,128]{3,2,1,0:T(8,128)(2,1)S(1)} %get-tuple-element.13), channel_id=1, source_target_pairs={{0,1},{1,2},{2,3},{3,4},{4,5},{5,6},{6,7},{8,9},{9,10},{10,11},{11... | collective-permute-start | bytes 147464 | tf_op jit(solution)/shard_map/ppermute | solution.py:18
  24.6 2.8 %fusion.50 = f32[4,16,128,128]{3,2,1,0:T(8,128)} fusion(bf16[4,16,32,128]{3,2,1,0:T(8,128)(2,1)S(1)} %multiply_convert_fusion.3, bf16[1,16,32,128]{3,2,1,0:T(8,128)(2,1)S(1)} %collective-permute-done, bf16[3,3,128,32]{2,3,1,0:T(8,128)(2,1)S(1)} %copy-done.9), kind=kOutput, calls=%fused_computation.46 | convolution fusion | flops 68419584 | bytes 4857856 | tf_op jit(solution)/shard_map/xyct,fc->xyft/dot_general | solution.py:65
  27.4 2.7 %fusion.54 = f32[4,16,128,128]{3,2,1,0:T(8,128)} fusion(bf16[1,16,32,128]{3,2,1,0:T(8,128)(2,1)S(1)} %collective-permute-done.1, bf16[4,16,32,128]{3,2,1,0:T(8,128)(2,1)S(1)} %multiply_convert_fusion.3, bf16[3,3,128,32]{2,3,1,0:T(8,128)(2,1)S(1)} %copy-done.9), kind=kOutput, calls=%fused_computation.50 | convolution fusion | flops 68419584 | bytes 4857856 | tf_op jit(solution)/shard_map/xyct,fc->xyft/dot_general | solution.py:65
  30.2 0.0 collective-permute-done.2
  30.2 2.7 %fusion.106 = f32[4,16,128,128]{3,2,1,0:T(8,128)} fusion(bf16[3,3,128,32]{2,3,1,0:T(8,128)(2,1)S(1)} %copy-done.9, bf16[1,16,32,128]{3,2,1,0:T(8,128)(2,1)S(1)} %collective-permute-done.1, bf16[4,16,32,128]{3,2,1,0:T(8,128)(2,1)S(1)} %multiply_convert_fusion.3, bf16[1,16,32,128]{3,2,1,0:T(8,128)(2,1)S(1)} %collective-permute-done, ...), kind=kOutput, calls=%fused_computation.104 | convolution fusion | flops 70451200 | bytes 5038080 | tf_op jit(solution)/shard_map/xyct,fc->xyft/dot_general | solution.py:65
  32.9 2.7 %fusion.84 = f32[4,16,128,128]{3,2,1,0:T(8,128)} fusion(bf16[3,3,128,32]{2,3,1,0:T(8,128)(2,1)S(1)} %copy-done.9, bf16[1,16,32,128]{3,2,1,0:T(8,128)(2,1)S(1)} %collective-permute-done.1, bf16[4,16,32,128]{3,2,1,0:T(8,128)(2,1)S(1)} %multiply_convert_fusion.3, bf16[1,16,32,128]{3,2,1,0:T(8,128)(2,1)S(1)} %collective-permute-done, ...), kind=kOutput, calls=%fused_computation.82 | convolution fusion | flops 70451200 | bytes 5038080 | tf_op jit(solution)/shard_map/xyct,fc->xyft/dot_general | solution.py:65
  35.6 0.0 collective-permute-done.3
  35.6 2.7 %fusion.100 = f32[4,16,128,128]{3,2,1,0:T(8,128)} fusion(bf16[3,3,128,32]{2,3,1,0:T(8,128)(2,1)S(1)} %copy-done.9, bf16[6,1,32,128]{3,2,1,0:T(8,128)(2,1)S(1)} %collective-permute-done.3, bf16[1,16,32,128]{3,2,1,0:T(8,128)(2,1)S(1)} %collective-permute-done.1, bf16[4,16,32,128]{3,2,1,0:T(8,128)(2,1)S(1)} %multiply_convert_fusion.3, ...), kind=kOutput, calls=%fused_computation.98 | convolution fusion | flops 70451200 | bytes 5038080 | tf_op jit(solution)/shard_map/xyct,fc->xyft/dot_general | solution.py:65
  38.3 2.7 %fusion.88 = f32[4,16,128,128]{3,2,1,0:T(8,128)} fusion(bf16[3,3,128,32]{2,3,1,0:T(8,128)(2,1)S(1)} %copy-done.9, bf16[6,1,32,128]{3,2,1,0:T(8,128)(2,1)S(1)} %collective-permute-done.3, bf16[1,16,32,128]{3,2,1,0:T(8,128)(2,1)S(1)} %collective-permute-done.1, bf16[4,16,32,128]{3,2,1,0:T(8,128)(2,1)S(1)} %multiply_convert_fusion.3, ...), kind=kOutput, calls=%fused_computation.86 | convolution fusion | flops 70451200 | bytes 5038080 | tf_op jit(solution)/shard_map/xyct,fc->xyft/dot_general | solution.py:65
  41.0 2.7 %fusion.96 = f32[4,16,128,128]{3,2,1,0:T(8,128)} fusion(bf16[3,3,128,32]{2,3,1,0:T(8,128)(2,1)S(1)} %copy-done.9, bf16[1,16,32,128]{3,2,1,0:T(8,128)(2,1)S(1)} %collective-permute-done.1, bf16[4,16,32,128]{3,2,1,0:T(8,128)(2,1)S(1)} %multiply_convert_fusion.3, bf16[1,16,32,128]{3,2,1,0:T(8,128)(2,1)S(1)} %collective-permute-done, ...), kind=kOutput, calls=%fused_computation.94 | convolution fusion | flops 70451200 | bytes 5038080 | tf_op jit(solution)/shard_map/xyct,fc->xyft/dot_general | solution.py:65
  43.8 0.6 copy-done.2
  44.4 12.4 %multiply_convert_fusion.1 = bf16[4,16,128,128]{2,3,1,0:T(8,128)(2,1)S(1)} fusion(f32[4,16,128,128]{3,2,1,0:T(8,128)} %fusion.54, f32[4,16,128,128]{3,2,1,0:T(8,128)} %fusion.84, f32[4,16,128,128]{3,2,1,0:T(8,128)} %fusion.88, f32[4,16,128,128]{3,2,1,0:T(8,128)} %fusion.92, f32[4,16,128,128]{3,2,1,0:T(8,128)} %fusion.96, f32[4,16,128,128]{3,2,1,0:T(8,128)} %fusion.100, ...), kind=kOutput, calls=%fused_computation.3 | convolution fusion | flops 86179840 | bytes 40689668 | tf_op jit(solution)/shard_map/xyct,fc->xyft/dot_general | solution.py:65
  56.8 0.0 copy-done.10
  56.8 0.8 convolution_bitcast_fusion.1
  57.7 0.8 fusion.24
  58.5 0.4 copy-done.4
  58.9 0.9 fusion.45
  59.8 0.6 collective-permute-start.4
  60.4 0.1 slice_reduce_fusion
  60.5 0.6 fusion.144
  61.1 0.1 add_bitcast_fusion
  61.2 2.5 %select_reduce_fusion.2 = (f32[]{:T(128)}, f32[]{:T(128)}, f32[]{:T(128)}) fusion(f32[1024]{0:T(1024)S(1)} %add_bitcast_fusion, s32[]{:T(128)} %bitcast, s32[]{:T(128)} %bitcast.3, s32[]{:T(128)} %bitcast.4), kind=kLoop, calls=%fused_computation.135 | loop fusion | flops 8997 | bytes 4024 | tf_op jit(solution)/shard_map/reduce_sum | solution.py:43
  67.5 4.6 %collective-permute-done.4 = bf16[4,16,32,128]{3,2,1,0:T(8,128)(2,1)S(1)} collective-permute-done((bf16[4,16,32,128]{3,2,1,0:T(8,128)(2,1)S(1)}, bf16[4,16,32,128]{3,2,1,0:T(8,128)(2,1)S(1)}, u32[]{:S(2)}, u32[]{:S(2)}) %collective-permute-start.4) | collective-permute-done | bytes 524320 | tf_op jit(solution)/shard_map/ppermute | solution.py:33
  72.1 0.8 multiply_reduce_fusion
  72.9 0.4 multiply_convert_fusion.2
  73.2 3.5 %collective-permute-start.5 = (bf16[1,16,32,128]{3,2,1,0:T(8,128)(2,1)S(1)}, bf16[1,16,32,128]{3,2,1,0:T(8,128)(2,1)S(1)}, u32[]{:S(2)}, u32[]{:S(2)}) collective-permute-start(bf16[1,16,32,128]{3,2,1,0:T(8,128)(2,1)S(1)} %get-tuple-element.14), channel_id=1, source_target_pairs={{0,8},{8,16},{16,24},{24,32},{32,40},{40,48},{48,56},{56,64},{64,7... | collective-permute-start | bytes 393224 | tf_op jit(solution)/shard_map/ppermute | solution.py:18
  76.7 0.0 copy-done.5
  76.8 1.9 %collective-permute-start.6 = (bf16[1,16,32,128]{3,2,1,0:T(8,128)(2,1)S(1)}, bf16[1,16,32,128]{3,2,1,0:T(8,128)(2,1)S(1)}, u32[]{:S(2)}, u32[]{:S(2)}) collective-permute-start(bf16[1,16,32,128]{3,2,1,0:T(8,128)(2,1)S(1)} %get-tuple-element.15), channel_id=1, source_target_pairs={{8,0},{16,8},{24,16},{32,24},{40,32},{48,40},{56,48},{64,56},{72,6... | collective-permute-start | bytes 393224 | tf_op jit(solution)/shard_map/ppermute | solution.py:21
  78.7 0.8 fusion.90
  79.4 0.0 collective-permute-done.5
  79.5 7.2 %collective-permute-done.6 = bf16[1,16,32,128]{3,2,1,0:T(8,128)(2,1)S(1)} collective-permute-done((bf16[1,16,32,128]{3,2,1,0:T(8,128)(2,1)S(1)}, bf16[1,16,32,128]{3,2,1,0:T(8,128)(2,1)S(1)}, u32[]{:S(2)}, u32[]{:S(2)}) %collective-permute-start.6) | collective-permute-done | bytes 131104 | tf_op jit(solution)/shard_map/ppermute | solution.py:21
  86.7 3.4 %collective-permute-start.7 = (bf16[6,1,32,128]{3,2,1,0:T(8,128)(2,1)S(1)}, bf16[6,1,32,128]{3,2,1,0:T(8,128)(2,1)S(1)}, u32[]{:S(2)}, u32[]{:S(2)}) collective-permute-start(bf16[6,1,32,128]{3,2,1,0:T(8,128)(2,1)S(1)} %get-tuple-element.11), channel_id=1, source_target_pairs={{0,1},{1,2},{2,3},{3,4},{4,5},{5,6},{6,7},{8,9},{9,10},{10,11},{11... | collective-permute-start | bytes 147464 | tf_op jit(solution)/shard_map/ppermute | solution.py:18
  90.0 1.9 %collective-permute-start.8 = (bf16[6,1,32,128]{3,2,1,0:T(8,128)(2,1)S(1)}, bf16[6,1,32,128]{3,2,1,0:T(8,128)(2,1)S(1)}, u32[]{:S(2)}, u32[]{:S(2)}) collective-permute-start(bf16[6,1,32,128]{3,2,1,0:T(8,128)(2,1)S(1)} %get-tuple-element.10), channel_id=1, source_target_pairs={{1,0},{2,1},{3,2},{4,3},{5,4},{6,5},{7,6},{9,8},{10,9},{11,10},{12... | collective-permute-start | bytes 147464 | tf_op jit(solution)/shard_map/ppermute | solution.py:21
  92.0 2.7 %fusion.58 = f32[4,16,128,128]{3,2,1,0:T(8,128)} fusion(bf16[4,16,32,128]{3,2,1,0:T(8,128)(2,1)S(1)} %multiply_convert_fusion.2, bf16[1,16,32,128]{3,2,1,0:T(8,128)(2,1)S(1)} %collective-permute-done.5, bf16[3,3,128,32]{2,3,1,0:T(8,128)(2,1)S(1)} %copy-done.9), kind=kOutput, calls=%fused_computation.54 | convolution fusion | flops 68419584 | bytes 4857856 | tf_op jit(solution)/shard_map/xyct,fc->xyft/dot_general | solution.py:65
  94.7 2.7 %fusion.62 = f32[4,16,128,128]{3,2,1,0:T(8,128)} fusion(bf16[1,16,32,128]{3,2,1,0:T(8,128)(2,1)S(1)} %collective-permute-done.6, bf16[4,16,32,128]{3,2,1,0:T(8,128)(2,1)S(1)} %multiply_convert_fusion.2, bf16[3,3,128,32]{2,3,1,0:T(8,128)(2,1)S(1)} %copy-done.9), kind=kOutput, calls=%fused_computation.58 | convolution fusion | flops 68419584 | bytes 4857856 | tf_op jit(solution)/shard_map/xyct,fc->xyft/dot_general | solution.py:65
  97.4 0.0 collective-permute-done.7
  97.4 2.7 %fusion.104 = f32[4,16,128,128]{3,2,1,0:T(8,128)} fusion(bf16[3,3,128,32]{2,3,1,0:T(8,128)(2,1)S(1)} %copy-done.9, bf16[1,16,32,128]{3,2,1,0:T(8,128)(2,1)S(1)} %collective-permute-done.6, bf16[4,16,32,128]{3,2,1,0:T(8,128)(2,1)S(1)} %multiply_convert_fusion.2, bf16[1,16,32,128]{3,2,1,0:T(8,128)(2,1)S(1)} %collective-permute-done.5, ...), kind=kOutput, calls=%fused_computation.102 | convolution fusion | flops 70451200 | bytes 5038080 | tf_op jit(solution)/shard_map/xyct,fc->xyft/dot_general | solution.py:65
  100.1 2.7 %fusion.94 = f32[4,16,128,128]{3,2,1,0:T(8,128)} fusion(bf16[3,3,128,32]{2,3,1,0:T(8,128)(2,1)S(1)} %copy-done.9, bf16[1,16,32,128]{3,2,1,0:T(8,128)(2,1)S(1)} %collective-permute-done.6, bf16[4,16,32,128]{3,2,1,0:T(8,128)(2,1)S(1)} %multiply_convert_fusion.2, bf16[1,16,32,128]{3,2,1,0:T(8,128)(2,1)S(1)} %collective-permute-done.5, ...), kind=kOutput, calls=%fused_computation.92 | convolution fusion | flops 70451200 | bytes 5038080 | tf_op jit(solution)/shard_map/xyct,fc->xyft/dot_general | solution.py:65
  102.8 0.0 collective-permute-done.8
  102.8 2.7 %fusion.98 = f32[4,16,128,128]{3,2,1,0:T(8,128)} fusion(bf16[3,3,128,32]{2,3,1,0:T(8,128)(2,1)S(1)} %copy-done.9, bf16[6,1,32,128]{3,2,1,0:T(8,128)(2,1)S(1)} %collective-permute-done.8, bf16[1,16,32,128]{3,2,1,0:T(8,128)(2,1)S(1)} %collective-permute-done.6, bf16[4,16,32,128]{3,2,1,0:T(8,128)(2,1)S(1)} %multiply_convert_fusion.2, ...), kind=kOutput, calls=%fused_computation.96 | convolution fusion | flops 70451200 | bytes 5038080 | tf_op jit(solution)/shard_map/xyct,fc->xyft/dot_general | solution.py:65
  105.6 2.7 %fusion.86 = f32[4,16,128,128]{3,2,1,0:T(8,128)} fusion(bf16[3,3,128,32]{2,3,1,0:T(8,128)(2,1)S(1)} %copy-done.9, bf16[6,1,32,128]{3,2,1,0:T(8,128)(2,1)S(1)} %collective-permute-done.8, bf16[1,16,32,128]{3,2,1,0:T(8,128)(2,1)S(1)} %collective-permute-done.6, bf16[4,16,32,128]{3,2,1,0:T(8,128)(2,1)S(1)} %multiply_convert_fusion.2, ...), kind=kOutput, calls=%fused_computation.84 | convolution fusion | flops 70451200 | bytes 5038080 | tf_op jit(solution)/shard_map/xyct,fc->xyft/dot_general | solution.py:65
  108.3 2.7 %fusion.82 = f32[4,16,128,128]{3,2,1,0:T(8,128)} fusion(bf16[3,3,128,32]{2,3,1,0:T(8,128)(2,1)S(1)} %copy-done.9, bf16[1,16,32,128]{3,2,1,0:T(8,128)(2,1)S(1)} %collective-permute-done.6, bf16[4,16,32,128]{3,2,1,0:T(8,128)(2,1)S(1)} %multiply_convert_fusion.2, bf16[1,16,32,128]{3,2,1,0:T(8,128)(2,1)S(1)} %collective-permute-done.5, ...), kind=kOutput, calls=%fused_computation.80 | convolution fusion | flops 70451200 | bytes 5038080 | tf_op jit(solution)/shard_map/xyct,fc->xyft/dot_general | solution.py:65
  111.0 0.6 copy-done.3
  111.7 11.2 %multiply_convert_fusion = bf16[4,16,128,128]{2,3,1,0:T(8,128)(2,1)S(1)} fusion(f32[4,16,128,128]{3,2,1,0:T(8,128)} %fusion.62, f32[4,16,128,128]{3,2,1,0:T(8,128)} %fusion.82, f32[4,16,128,128]{3,2,1,0:T(8,128)} %fusion.86, f32[4,16,128,128]{3,2,1,0:T(8,128)S(1)} %fusion.90, f32[4,16,128,128]{3,2,1,0:T(8,128)} %fusion.94, f32[4,16,128,128]{3,2,1,0:T(8,128)} %fusion.98, ...), kind=kOutput, calls=%fused_computation.2 | convolution fusion | flops 86179840 | bytes 40689668 | tf_op jit(solution)/shard_map/xyct,fc->xyft/dot_general | solution.py:65
  122.9 0.8 convolution_bitcast_fusion
  123.7 0.8 fusion.39
  124.5 0.4 copy-done.6
  124.9 0.9 fusion.42
  125.8 0.4 collective-permute-start.9
  128.9 5.9 %collective-permute-done.9 = bf16[4,16,32,128]{3,2,1,0:T(8,128)(2,1)S(1)} collective-permute-done((bf16[4,16,32,128]{3,2,1,0:T(8,128)(2,1)S(1)}, bf16[4,16,32,128]{3,2,1,0:T(8,128)(2,1)S(1)}, u32[]{:S(2)}, u32[]{:S(2)}) %collective-permute-start.9) | collective-permute-done | bytes 524320 | tf_op jit(solution)/shard_map/ppermute | solution.py:33
  134.8 1.5 %bitcast_add_fusion.2 = f32[4,16,32,128]{3,2,1,0:T(8,128)} fusion(f32[4,16,32,128]{3,2,1,0:T(8,128)S(1)} %copy-done.6, bf16[2,4,16,32,128]{4,3,2,1,0:T(8,128)(2,1)S(1)} %copy-done.8, f32[]{:T(128)S(6)} %mul.159, f32[]{:T(128)S(6)} %sqrt.44, bf16[4,16,32,128]{3,2,1,0:T(8,128)(2,1)S(1)} %fusion.42, bf16[4,16,32,128]{3,2,1,0:T(8,128)(2,1)S(1)} %collective-permute-done.9, ...), kind=kLoop, calls=%fused_computation.36 | loop fusion | flops 4194304 | bytes 3670037 | tf_op jit(solution)/shard_map/add | solution.py:54
  (27 shorter events, 0.2 us)
Async XLA Ops:
  0.0 12.7 %copy-start = (bf16[4,16,8,128]{3,2,1,0:T(8,128)(2,1)S(1)}, bf16[4,16,8,128]{3,2,1,0:T(8,128)(2,1)}, u32[]{:S(2)}) copy-start(bf16[4,16,8,128]{3,2,1,0:T(8,128)(2,1)} %param.9) | copy-start | bytes 393220
  0.0 9.9 %copy-start.9 = (bf16[3,3,128,32]{2,3,1,0:T(8,128)(2,1)S(1)}, bf16[3,3,128,32]{2,3,1,0:T(8,128)(2,1)}, u32[]{:S(2)}) copy-start(bf16[3,3,128,32]{2,3,1,0:T(8,128)(2,1)} %param.11) | copy-start | bytes 221188
  3.1 12.9 %collective-permute-start = (bf16[1,16,32,128]{3,2,1,0:T(8,128)(2,1)S(1)}, bf16[1,16,32,128]{3,2,1,0:T(8,128)(2,1)S(1)}, u32[]{:S(2)}, u32[]{:S(2)}) collective-permute-start(bf16[1,16,32,128]{3,2,1,0:T(8,128)(2,1)S(1)} %get-tuple-element.16), channel_id=1, source_target_pairs={{0,8},{8,16},{16,24},{24,32},{32,40},{40,48},{48,56},{56,64},{64,7... | collective-permute-start | bytes 393224 | tf_op jit(solution)/shard_map/ppermute | solution.py:18
  8.0 4.7 %copy-start.12 = (bf16[128,8]{0,1:T(8,128)(2,1)S(1)}, bf16[128,8]{0,1:T(8,128)(2,1)}, u32[]{:S(2)}) copy-start(bf16[128,8]{0,1:T(8,128)(2,1)} %param.12) | copy-start | bytes 6148
  8.0 9.9 %collective-permute-start.1 = (bf16[1,16,32,128]{3,2,1,0:T(8,128)(2,1)S(1)}, bf16[1,16,32,128]{3,2,1,0:T(8,128)(2,1)S(1)}, u32[]{:S(2)}, u32[]{:S(2)}) collective-permute-start(bf16[1,16,32,128]{3,2,1,0:T(8,128)(2,1)S(1)} %get-tuple-element.17), channel_id=1, source_target_pairs={{8,0},{16,8},{24,16},{32,24},{40,32},{48,40},{56,48},{64,56},{72,6... | collective-permute-start | bytes 393224 | tf_op jit(solution)/shard_map/ppermute | solution.py:21
  17.9 17.6 %collective-permute-start.3 = (bf16[6,1,32,128]{3,2,1,0:T(8,128)(2,1)S(1)}, bf16[6,1,32,128]{3,2,1,0:T(8,128)(2,1)S(1)}, u32[]{:S(2)}, u32[]{:S(2)}) collective-permute-start(bf16[6,1,32,128]{3,2,1,0:T(8,128)(2,1)S(1)} %get-tuple-element.12), channel_id=1, source_target_pairs={{1,0},{2,1},{3,2},{4,3},{5,4},{6,5},{7,6},{9,8},{10,9},{11,10},{12... | collective-permute-start | bytes 147464 | tf_op jit(solution)/shard_map/ppermute | solution.py:21
  19.9 10.3 %collective-permute-start.2 = (bf16[6,1,32,128]{3,2,1,0:T(8,128)(2,1)S(1)}, bf16[6,1,32,128]{3,2,1,0:T(8,128)(2,1)S(1)}, u32[]{:S(2)}, u32[]{:S(2)}) collective-permute-start(bf16[6,1,32,128]{3,2,1,0:T(8,128)(2,1)S(1)} %get-tuple-element.13), channel_id=1, source_target_pairs={{0,1},{1,2},{2,3},{3,4},{4,5},{5,6},{6,7},{8,9},{9,10},{10,11},{11... | collective-permute-start | bytes 147464 | tf_op jit(solution)/shard_map/ppermute | solution.py:18
  41.0 3.4 %copy-start.2 = (f32[128,4,16,128]{0,3,2,1:T(8,128)S(1)}, f32[128,4,16,128]{0,3,2,1:T(8,128)}, u32[]{:S(2)}) copy-start(f32[128,4,16,128]{0,3,2,1:T(8,128)} %fusion.132) | copy-start | bytes 12582916
  44.4 12.4 %copy-start.10 = (bf16[3,32,128]{2,1,0:T(8,128)(2,1)S(1)}, bf16[3,32,128]{2,1,0:T(8,128)(2,1)}, u32[]{:S(2)}) copy-start(bf16[3,32,128]{2,1,0:T(8,128)(2,1)} %param.13) | copy-start | bytes 73732
  57.7 1.2 copy-start.4
  58.9 1.6 %copy-start.11 = (s32[3]{0:T(128)S(1)}, s32[3]{0:T(128)}, u32[]{:S(2)}) copy-start(s32[3]{0:T(128)} %param.10) | copy-start | bytes 40
  58.9 13.2 %copy-start.7 = (bf16[2,4,16,32,128]{4,3,2,1,0:T(8,128)(2,1)S(1)}, bf16[2,4,16,32,128]{4,3,2,1,0:T(8,128)(2,1)}, u32[]{:S(2)}) copy-start(bf16[2,4,16,32,128]{4,3,2,1,0:T(8,128)(2,1)} %param.8) | copy-start | bytes 3145732
  59.8 12.3 %collective-permute-start.4 = (bf16[4,16,32,128]{3,2,1,0:T(8,128)(2,1)S(1)}, bf16[4,16,32,128]{3,2,1,0:T(8,128)(2,1)S(1)}, u32[]{:S(2)}, u32[]{:S(2)}) collective-permute-start(bf16[4,16,32,128]{3,2,1,0:T(8,128)(2,1)S(1)} %fusion.45), channel_id=1, source_target_pairs={{0,128},{128,0},{1,129},{129,1},{2,130},{130,2},{3,131},{131,3},{4... | collective-permute-start | bytes 1572872 | tf_op jit(solution)/shard_map/ppermute | solution.py:33
  72.8 3.9 %copy-start.5 = (f32[4,16,32,128]{3,2,1,0:T(8,128)}, f32[4,16,32,128]{3,2,1,0:T(8,128)S(1)}, u32[]{:S(2)}) copy-start(f32[4,16,32,128]{3,2,1,0:T(8,128)S(1)} %get-tuple-element.9) | copy-start | bytes 3145732
  73.2 6.2 %collective-permute-start.5 = (bf16[1,16,32,128]{3,2,1,0:T(8,128)(2,1)S(1)}, bf16[1,16,32,128]{3,2,1,0:T(8,128)(2,1)S(1)}, u32[]{:S(2)}, u32[]{:S(2)}) collective-permute-start(bf16[1,16,32,128]{3,2,1,0:T(8,128)(2,1)S(1)} %get-tuple-element.14), channel_id=1, source_target_pairs={{0,8},{8,16},{16,24},{24,32},{32,40},{40,48},{48,56},{56,64},{64,7... | collective-permute-start | bytes 393224 | tf_op jit(solution)/shard_map/ppermute | solution.py:18
  76.8 9.9 %collective-permute-start.6 = (bf16[1,16,32,128]{3,2,1,0:T(8,128)(2,1)S(1)}, bf16[1,16,32,128]{3,2,1,0:T(8,128)(2,1)S(1)}, u32[]{:S(2)}, u32[]{:S(2)}) collective-permute-start(bf16[1,16,32,128]{3,2,1,0:T(8,128)(2,1)S(1)} %get-tuple-element.15), channel_id=1, source_target_pairs={{8,0},{16,8},{24,16},{32,24},{40,32},{48,40},{56,48},{64,56},{72,6... | collective-permute-start | bytes 393224 | tf_op jit(solution)/shard_map/ppermute | solution.py:21
  86.7 10.7 %collective-permute-start.7 = (bf16[6,1,32,128]{3,2,1,0:T(8,128)(2,1)S(1)}, bf16[6,1,32,128]{3,2,1,0:T(8,128)(2,1)S(1)}, u32[]{:S(2)}, u32[]{:S(2)}) collective-permute-start(bf16[6,1,32,128]{3,2,1,0:T(8,128)(2,1)S(1)} %get-tuple-element.11), channel_id=1, source_target_pairs={{0,1},{1,2},{2,3},{3,4},{4,5},{5,6},{6,7},{8,9},{9,10},{10,11},{11... | collective-permute-start | bytes 147464 | tf_op jit(solution)/shard_map/ppermute | solution.py:18
  90.0 12.8 %collective-permute-start.8 = (bf16[6,1,32,128]{3,2,1,0:T(8,128)(2,1)S(1)}, bf16[6,1,32,128]{3,2,1,0:T(8,128)(2,1)S(1)}, u32[]{:S(2)}, u32[]{:S(2)}) collective-permute-start(bf16[6,1,32,128]{3,2,1,0:T(8,128)(2,1)S(1)} %get-tuple-element.10), channel_id=1, source_target_pairs={{1,0},{2,1},{3,2},{4,3},{5,4},{6,5},{7,6},{9,8},{10,9},{11,10},{12... | collective-permute-start | bytes 147464 | tf_op jit(solution)/shard_map/ppermute | solution.py:21
  108.3 3.4 %copy-start.3 = (f32[128,4,16,128]{0,3,2,1:T(8,128)S(1)}, f32[128,4,16,128]{0,3,2,1:T(8,128)}, u32[]{:S(2)}) copy-start(f32[128,4,16,128]{0,3,2,1:T(8,128)} %fusion.132) | copy-start | bytes 12582916
  123.7 1.2 copy-start.6
  124.9 9.9 %copy-start.8 = (bf16[2,4,16,32,128]{4,3,2,1,0:T(8,128)(2,1)S(1)}, bf16[2,4,16,32,128]{4,3,2,1,0:T(8,128)(2,1)}, u32[]{:S(2)}) copy-start(bf16[2,4,16,32,128]{4,3,2,1,0:T(8,128)(2,1)} %param.8) | copy-start | bytes 3145732
  124.9 11.4 %copy-start.1 = (bf16[4,16,8,128]{3,2,1,0:T(8,128)(2,1)S(1)}, bf16[4,16,8,128]{3,2,1,0:T(8,128)(2,1)}, u32[]{:S(2)}) copy-start(bf16[4,16,8,128]{3,2,1,0:T(8,128)(2,1)} %param.9) | copy-start | bytes 393220
  125.8 9.0 %collective-permute-start.9 = (bf16[4,16,32,128]{3,2,1,0:T(8,128)(2,1)S(1)}, bf16[4,16,32,128]{3,2,1,0:T(8,128)(2,1)S(1)}, u32[]{:S(2)}, u32[]{:S(2)}) collective-permute-start(bf16[4,16,32,128]{3,2,1,0:T(8,128)(2,1)S(1)} %fusion.42), channel_id=1, source_target_pairs={{0,128},{128,0},{1,129},{129,1},{2,130},{130,2},{3,131},{131,3},{4... | collective-permute-start | bytes 1572872 | tf_op jit(solution)/shard_map/ppermute | solution.py:33
where the time goes:
time: 138 us; the launch traced here: 136 us
  matrix products  73.2 us (53%)
  starting transfers between devices  25.1 us (18%)
  waiting for transfers between devices  19.6 us (14%)
  other arithmetic  8.62 us (6%)
  between operations  6.76 us (5%)
  local copies, waits for them, and re-layouts  2.99 us (2%)
    dot_general x18, matrix products, spatial(): jnp.einsum('xyct,fc->xyft', padded[row_off:row_off + row_count, col_off:c...  65.3 us
    ppermute x4, starting transfers between devices, padded_2(): lax.ppermute(lax.slice_in_dim(block, block.shape[dim] - width, None, axis...  16.5 us
    ppermute x2, waiting for transfers between devices, partner(): return lax.ppermute(block, axis, route)  10.5 us
    ppermute x4, waiting for transfers between devices, padded_2(): lax.ppermute(lax.slice_in_dim(block, 0, width, axis=dim), axis, backward)  9.15 us
    ppermute x4, starting transfers between devices, padded_2(): lax.ppermute(lax.slice_in_dim(block, 0, width, axis=dim), axis, backward)  7.68 us
    dot_general x6, matrix products, finish(): jnp.einsum('xyft,cf->xyct', shifted[:, :, :, tap_index:tap_index + length...  5.07 us
    dot_general x1, matrix products, on_device(): jnp.einsum('xykt,fk->xyft', cond_field, cond_weight, preferred_element_ty...  2.88 us
  transfers between devices with their start and end apart: 10, of which 4 were waited for; matrix products, arithmetic and copies ran while one was open for 23% of the time, Pallas kernels for 0%

commit v1 on v0

v1 whole, which is shorter than its diff:
```python
import jax
import jax.numpy as jnp
from jax import lax
from jax.experimental import pallas as pl
from jax.experimental.pallas import tpu as pltpu
from jax.sharding import PartitionSpec as P

F32 = jnp.float32
BF16 = jnp.bfloat16
AXES = ("cfg", "gx", "gy")
NCFG, NGX, NGY = 2, 16, 8
ROWS, COLS, C, FF, CK, NT = 4, 16, 32, 128, 8, 128
YROWS = 2 * C + C + 2 * CK
XROWS = 2 * COLS * C + COLS * C + COLS * CK
DROWS = 8 * C + 2 * C + 2 * CK


def linear(cfg, gx, gy):
    return (cfg * NGX + gx) * NGY + gy


def swaps_x(parity):
    pairs = []
    for cfg in range(NCFG):
        for gy in range(NGY):
            for gx in range(parity, NGX - 1, 2):
                other = 1 - cfg if gx == NGX // 2 - 1 else cfg
                a, b = linear(cfg, gx, gy), linear(other, gx + 1, gy)
                pairs += [(a, b), (b, a)]
    return pairs


def swaps_y(parity):
    pairs = []
    for cfg in range(NCFG):
        for gx in range(NGX):
            for gy in range(parity, NGY - 1, 2):
                a, b = linear(cfg, gx, gy), linear(cfg, gx, gy + 1)
                pairs += [(a, b), (b, a)]
    return pairs


def vmem():
    return pl.BlockSpec(memory_space=pltpu.VMEM)


def smem():
    return pl.BlockSpec(memory_space=pltpu.SMEM)


def join16(*parts):
    return jnp.concatenate([p.astype(F32) for p in parts], axis=0).astype(BF16)


def pack_kernel(place, lat, noise, cond, ya, yb, xa, xb):
    def pack_y(out, high):
        lo, inner = (COLS - 2, COLS - 1) if high else (0, 0)
        for r in range(ROWS):
            out[r, 0 : 2 * C, :] = lat[r, lo : lo + 2].reshape(2 * C, NT).astype(BF16)
            out[r, 2 * C : 3 * C, :] = noise[0, r, inner]
            cell = cond[r, inner * CK : (inner + 1) * CK, :]
            out[r, 3 * C :, :] = join16(cell, cell)

    def pack_x(out, high):
        lo, inner = (ROWS - 2, ROWS - 1) if high else (0, 0)
        n = COLS * C
        for i in range(2):
            out[i * n : (i + 1) * n, :] = lat[lo + i].reshape(n, NT).astype(BF16)
        out[2 * n : 3 * n, :] = noise[0, inner].reshape(n, NT)
        out[3 * n :, :] = cond[inner]

    for parity in range(2):

        @pl.when(place[1] == parity)
        def _():
            pack_y(ya, parity == 0)
            pack_y(yb, parity == 1)

    for parity in range(2):

        @pl.when(place[0] == parity)
        def _():
            pack_x(xa, parity == 0)
            pack_x(xb, parity == 1)


def pack(place, lat, noise, cond):
    y = jax.ShapeDtypeStruct((ROWS, YROWS, NT), BF16)
    x = jax.ShapeDtypeStruct((XROWS, NT), BF16)
    return pl.pallas_call(
        pack_kernel,
        out_shape=(y, y, x, x),
        in_specs=[smem(), vmem(), vmem(), vmem()],
        out_specs=(vmem(),) * 4,
        compiler_params=pltpu.CompilerParams(vmem_limit_bytes=16 << 20),
        cost_estimate=pl.CostEstimate(flops=1 << 18, bytes_accessed=3 << 20, transcendentals=0),
        name="pack_faces",
    )(place, lat, noise, cond)


def corner_kernel(place, ya, yb, da, db):
    def pack_corner(out, low, high, top):
        lo, inner = (ROWS - 2, ROWS - 1) if top else (0, 0)
        for i in range(2):
            out[4 * C * i : 4 * C * i + 2 * C, :] = low[lo + i, 0 : 2 * C, :]
            out[4 * C * i + 2 * C : 4 * C * i + 4 * C, :] = high[lo + i, 0 : 2 * C, :]
        out[8 * C : 9 * C, :] = low[inner, 2 * C : 3 * C, :]
        out[9 * C : 10 * C, :] = high[inner, 2 * C : 3 * C, :]
        first = low[inner, 3 * C :, :].astype(F32)[0:CK]
        second = high[inner, 3 * C :, :].astype(F32)[0:CK]
        out[10 * C :, :] = join16(first, second)

    for px in range(2):
        for py in range(2):

            @pl.when((place[0] == px) & (place[1] == py))
            def _():
                low, high = (yb, ya) if py == 0 else (ya, yb)
                pack_corner(da, low, high, px == 0)
                pack_corner(db, low, high, px == 1)


def pack_corners(place, ya, yb):
    d = jax.ShapeDtypeStruct((DROWS, NT), BF16)
    return pl.pallas_call(
        corner_kernel,
        out_shape=(d, d),
        in_specs=[smem(), vmem(), vmem()],
        out_specs=(vmem(),) * 2,
        compiler_params=pltpu.CompilerParams(vmem_limit_bytes=16 << 20),
        cost_estimate=pl.CostEstimate(flops=1 << 12, bytes_accessed=1 << 18, transcendentals=0),
        name="pack_corners",
    )(place, ya, yb)


def weights_kernel(spatial, cond, temporal, wide, wide_cond, wide_temporal):
    blank = jnp.zeros((FF, C), F32)
    for dx in range(3):
        taps = [spatial[dx, dy].astype(F32) for dy in range(3)]
        wide[0:FF, dx * 4 * C : (dx + 1) * 4 * C] = jnp.concatenate(taps + [blank], axis=1).astype(BF16)
        wide[FF:, dx * 4 * C : (dx + 1) * 4 * C] = jnp.concatenate([blank] + taps, axis=1).astype(BF16)
    small = cond[...].astype(F32)
    none = jnp.zeros((FF, CK), F32)
    wide_cond[0:FF, :] = jnp.concatenate([small, none], axis=1).astype(BF16)
    wide_cond[FF:, :] = jnp.concatenate([none, small], axis=1).astype(BF16)
    wide_temporal[...] = jnp.zeros(wide_temporal.shape, BF16)
    wide_temporal[0 : 3 * C, 0:FF] = temporal[...].reshape(3 * C, FF)
    wide_temporal[3 * C :, FF:] = temporal[...].reshape(3 * C, FF)


def widen(spatial, cond, temporal):
    return pl.pallas_call(
        weights_kernel,
        out_shape=(
            jax.ShapeDtypeStruct((2 * FF, 12 * C), BF16),
            jax.ShapeDtypeStruct((2 * FF, 2 * CK), BF16),
            jax.ShapeDtypeStruct((6 * C, 2 * FF), BF16),
        ),
        in_specs=[vmem()] * 3,
        out_specs=(vmem(),) * 3,
        compiler_params=pltpu.CompilerParams(vmem_limit_bytes=16 << 20),
        cost_estimate=pl.CostEstimate(flops=1 << 18, bytes_accessed=1 << 20, transcendentals=0),
        name="widen_weights",
    )(spatial, cond, temporal)


def log_alpha(when):
    shape = (8, 128)
    position = lax.broadcasted_iota(jnp.int32, shape, 0) * 128 + lax.broadcasted_iota(jnp.int32, shape, 1)
    beta = 0.0001 + (0.02 - 0.0001) * position.astype(F32) / 999.0
    logs = jnp.log(1.0 - jnp.minimum(beta, 0.5))
    return jnp.sum(jnp.where(position <= when, logs, 0.0))


def coefficients(now, later):
    a = jnp.exp(jnp.full((1, NT), log_alpha(now), F32))
    p = jnp.exp(jnp.full((1, NT), log_alpha(later), F32))
    sigma = 0.5 * jnp.sqrt((1.0 - p) / (1.0 - a)) * jnp.sqrt(1.0 - a / p)
    keep = jnp.sqrt(p) / jnp.sqrt(a)
    move = jnp.sqrt(1.0 - p - sigma * sigma) - keep * jnp.sqrt(1.0 - a)
    return keep, move, sigma


def silu(v):
    half = 0.5 * v
    return half + half * jnp.tanh(half)


def normalize(x):
    mean = jnp.sum(jnp.sum(x * x, axis=1, keepdims=True), axis=2, keepdims=True) * (1.0 / (C * NT))
    return x * lax.rsqrt(mean + 1e-05)


def block(act, row, cond_rows, pairs, wide, wide_cond, wide_temporal):
    windows = [
        jnp.concatenate([act[row + dx, 2 * C * p : 2 * C * p + 4 * C, :] for dx in range(3)], axis=0)
        for p in pairs
    ]
    fields = [cond_rows(p) for p in pairs]
    rhs = jnp.concatenate(windows, axis=1) if len(pairs) > 1 else windows[0]
    field = jnp.concatenate(fields, axis=1) if len(pairs) > 1 else fields[0]
    free = jnp.dot(wide[...], rhs, preferred_element_type=F32)
    with_cond = free + jnp.dot(wide_cond[...], field, preferred_element_type=F32)
    hidden = (3.0 * silu(with_cond) - 2.0 * silu(free)).astype(BF16)
    taps = jnp.dot(wide_temporal[...], hidden, preferred_element_type=F32)
    time = lax.broadcasted_iota(jnp.int32, (C, NT), 1)
    sums = []
    for q in range(len(pairs)):
        for o in range(2):
            t = taps[3 * C * o : 3 * C * (o + 1), NT * q : NT * (q + 1)]
            before = jnp.where(time == 0, 0.0, pltpu.roll(t[0:C], 1, 1))
            after = jnp.where(time == NT - 1, 0.0, pltpu.roll(t[2 * C :], NT - 1, 1))
            sums.append(before + t[C : 2 * C] + after)
    return sums


def main_kernel(
    place, steps, lat, noise, cond, ya, yb, xa, xb, da, db, wide, wide_cond, wide_temporal,
    out, act, base, condx, act2,
):
    keep, move, sigma = coefficients(steps[0], steps[1])
    even_x, even_y = place[0] == 0, place[1] == 0

    def side(even, a, b, high):
        return jnp.where(even, a, b) if high else jnp.where(even, b, a)

    def prepare(e, x, fresh, field):
        normed = normalize(x)
        act[e] = silu(normed).astype(BF16).reshape(20 * C, NT)
        if fresh is not None:
            value = keep * x[1:19] + move * normed[1:19] + sigma * fresh
            base[e - 1] = value.reshape(18 * C, NT)
            condx[e - 1] = field

    def cells(v):
        return v.astype(F32).reshape(-1, C, NT)

    for r in range(ROWS):
        low = side(even_y, ya[r], yb[r], False)
        high = side(even_y, ya[r], yb[r], True)
        x = jnp.concatenate([cells(low[0 : 2 * C]), lat[r], cells(high[0 : 2 * C])], axis=0)
        fresh = jnp.concatenate(
            [cells(low[2 * C : 3 * C]), noise[0, r].astype(F32), cells(high[2 * C : 3 * C])], axis=0
        )
        field = join16(low.astype(F32)[3 * C : 3 * C + CK], cond[r], high.astype(F32)[3 * C : 3 * C + CK])
        prepare(r + 2, x, fresh, field)
    n = COLS * C
    for top in (False, True):
        face = lambda lo, hi: side(even_x, xa[lo:hi, :], xb[lo:hi, :], top)
        corner = lambda lo, hi: side(even_x, da[lo:hi, :], db[lo:hi, :], top)
        for i in range(2):
            x = jnp.concatenate(
                [
                    cells(corner(4 * C * i, 4 * C * i + 2 * C)),
                    cells(face(i * n, (i + 1) * n)),
                    cells(corner(4 * C * i + 2 * C, 4 * C * i + 4 * C)),
                ],
                axis=0,
            )
            fresh = field = None
            if i == (0 if top else 1):
                fresh = jnp.concatenate(
                    [
                        cells(corner(8 * C, 9 * C)),
                        cells(face(2 * n, 3 * n)),
                        cells(corner(9 * C, 10 * C)),
                    ],
                    axis=0,
                )
                ends = corner(10 * C, 10 * C + 2 * CK).astype(F32)
                field = join16(ends[0:CK], face(3 * n, 3 * n + COLS * CK), ends[CK:])
            prepare((6 if top else 0) + i, x, fresh, field)

    def first(e, carry):
        for lo in range(0, 9, 2):
            pairs = list(range(lo, min(lo + 2, 9)))
            sums = block(
                act, e, lambda p: condx[e, 2 * CK * p : 2 * CK * (p + 1), :], pairs, wide, wide_cond, wide_temporal
            )
            for i, s in enumerate(sums):
                at = pl.ds((2 * lo + i) * C, C)
                base[e, at, :] = base[e, at, :] + move * s
        return carry

    lax.fori_loop(0, 6, first, 0)

    keep2, move2, sigma2 = coefficients(steps[1], steps[2])
    left = jnp.where(place[3] == 0, 0.0, 1.0)
    right = jnp.where(place[3] == NGY - 1, 0.0, 1.0)
    for e in range(6):
        x = base[e].reshape(18, C, NT)
        normed = normalize(x)
        value = silu(normed)
        value = jnp.concatenate([value[0:1] * left, value[1:17], value[17:18] * right], axis=0)
        if e == 0:
            value = value * jnp.where(place[2] == 0, 0.0, 1.0)
        if e == 5:
            value = value * jnp.where(place[2] == NGX - 1, 0.0, 1.0)
        act2[e] = value.astype(BF16).reshape(18 * C, NT)
        if 0 < e < 5:
            out[e - 1] = keep2 * x[1:17] + move2 * normed[1:17] + sigma2 * noise[1, e - 1].astype(F32)

    def second(r, carry):
        for lo in range(0, 8, 2):
            sums = block(
                act2, r, lambda p: cond[r, 2 * CK * p : 2 * CK * (p + 1), :], [lo, lo + 1],
                wide, wide_cond, wide_temporal,
            )
            for i, s in enumerate(sums):
                out[r, 2 * lo + i] = out[r, 2 * lo + i] + move2 * s
        return carry

    lax.fori_loop(0, ROWS, second, 0)


def sample(place, steps, lat, noise, cond, halos, weights):
    return pl.pallas_call(
        main_kernel,
        out_shape=jax.ShapeDtypeStruct((ROWS, COLS, C, NT), F32),
        in_specs=[smem(), smem()] + [vmem()] * 12,
        out_specs=vmem(),
        scratch_shapes=[
            pltpu.VMEM((8, 20 * C, NT), BF16),
            pltpu.VMEM((6, 18 * C, NT), F32),
            pltpu.VMEM((6, 18 * CK, NT), BF16),
            pltpu.VMEM((6, 18 * C, NT), BF16),
        ],
        compiler_params=pltpu.CompilerParams(vmem_limit_bytes=40 << 20),
        cost_estimate=pl.CostEstimate(flops=2 << 30, bytes_accessed=5 << 20, transcendentals=5 << 20),
        name="sample_slab",
    )(place, steps, lat, noise, cond, *halos, *weights)


def on_device(latent, sample_noise, cond_field, timesteps, spatial_weight, cond_weight, temporal_weight):
    gx, gy = lax.axis_index("gx"), lax.axis_index("gy")
    place = jnp.stack([gx % 2, gy % 2, gx, gy]).astype(jnp.int32)
    cond = cond_field.reshape(ROWS, COLS * CK, NT)
    ya, yb, xa, xb = pack(place, latent, sample_noise, cond)
    ya = lax.ppermute(ya, AXES, swaps_y(0))
    yb = lax.ppermute(yb, AXES, swaps_y(1))
    xa = lax.ppermute(xa, AXES, swaps_x(0))
    xb = lax.ppermute(xb, AXES, swaps_x(1))
    weights = widen(spatial_weight, cond_weight, temporal_weight)
    da, db = pack_corners(place, ya, yb)
    da = lax.ppermute(da, AXES, swaps_x(0))
    db = lax.ppermute(db, AXES, swaps_x(1))
    return sample(place, timesteps, latent, sample_noise, cond, (ya, yb, xa, xb, da, db), weights)


def solution(mesh):
    in_specs = (
        P("gx", "gy", None, None),
        P(None, "gx", "gy", None, None),
        P("gx", "gy", None, None),
        P(),
        P(),
        P(),
        P(),
    )
    return jax.shard_map(
        on_device, mesh=mesh, in_specs=in_specs, out_specs=P("gx", "gy", None, None), check_vma=False
    )
```

time: 138 us -> 51.9 us (0.38)
  the two profiles are of different devices: /device:TPU:121 before, /device:TPU:134 now
where the time goes in v1:
time: 51.9 us; the launch traced here: 51.6 us
  Pallas kernels  24.2 us (47%)
  starting transfers between devices  11.6 us (22%)
  waiting for transfers between devices  10.4 us (20%)
  local copies, waits for them, and re-layouts  5.23 us (10%)
    pallas_call x1, Pallas kernels, sample(): pl.pallas_call(main_kernel, out_shape=jax.ShapeDtypeStruct((ROWS, COLS, C...  21.3 us
    unnamed x20, local copies, waits for them, and re-layouts  5.23 us
    ppermute x1, starting transfers between devices, on_device(): xb = lax.ppermute(xb, AXES, swaps_x(1))  4.94 us
    ppermute x1, waiting for transfers between devices, on_device(): db = lax.ppermute(db, AXES, swaps_x(1))  4.43 us
    ppermute x1, waiting for transfers between devices, on_device(): yb = lax.ppermute(yb, AXES, swaps_y(1))  4.11 us
    ppermute x1, starting transfers between devices, on_device(): db = lax.ppermute(db, AXES, swaps_x(1))  3.64 us
    ppermute x1, starting transfers between devices, on_device(): yb = lax.ppermute(yb, AXES, swaps_y(1))  1.91 us
    ppermute x1, waiting for transfers between devices, on_device(): ya = lax.ppermute(ya, AXES, swaps_y(0))  1.86 us
  transfers between devices with their start and end apart: 6, of which 3 were waited for; matrix products, arithmetic and copies ran while one was open for 2% of the time, Pallas kernels for 3%

profile of v1, /device:TPU:134, one launch (start us, length us, event | category | flops | bytes accessed | tf_op | source)
XLA Modules:
  0.0 51.6 jit_solution(2118706942803269631)
XLA Ops:
  0.0 0.1 pad_add_fusion.place
  0.1 0.0 copy-start
  0.1 1.2 %copy-done = f32[4,16,32,128]{3,2,1,0:T(8,128)S(1)} copy-done((f32[4,16,32,128]{3,2,1,0:T(8,128)S(1)}, f32[4,16,32,128]{3,2,1,0:T(8,128)}, u32[]{:S(2)}) %copy-start) | copy-done | bytes 1048600
  1.3 0.0 copy-start.2
  1.3 1.2 %copy-done.2 = bf16[2,4,16,32,128]{4,3,2,1,0:T(8,128)(2,1)S(1)} copy-done((bf16[2,4,16,32,128]{4,3,2,1,0:T(8,128)(2,1)S(1)}, bf16[2,4,16,32,128]{4,3,2,1,0:T(8,128)(2,1)}, u32[]{:S(2)}) %copy-start.2) | copy-done | bytes 1048600
  2.5 0.0 copy-start.4
  2.5 0.9 %copy-done.4 = bf16[4,16,8,128]{3,2,1,0:T(8,128)(2,1)S(1)} copy-done((bf16[4,16,8,128]{3,2,1,0:T(8,128)(2,1)S(1)}, bf16[4,16,8,128]{3,2,1,0:T(8,128)(2,1)}, u32[]{:S(2)}) %copy-start.4) | copy-done | bytes 131096
  3.4 0.0 copy-start.1
  3.4 0.0 copy-start.3
  3.4 1.4 %pack_faces.1 = (bf16[4,112,128]{2,1,0:T(8,128)(2,1)S(1)}, bf16[4,112,128]{2,1,0:T(8,128)(2,1)S(1)}, bf16[1664,128]{1,0:T(8,128)(2,1)}, bf16[1664,128]{1,0:T(8,128)(2,1)S(1)}) custom-call(s32[4]{0:T(128)S(1)} %pad_add_fusion.place, f32[4,16,32,128]{3,2,1,0:T(8,128)S(1)} %copy-done, bf16[2,4,16,32,128]{4,3,2,1,0:T(8,128)(2,1)S(1)} %copy-done.2, ...), custom_call_target="tpu_custom_call" | custom-call | flops 262144 | bytes 3145728 | tf_op jit(solution)/shard_map/pack_faces/pallas_call | solution.py:90
  4.9 0.0 collective-permute-start.2
  4.9 4.9 %collective-permute-start.3 = (bf16[1664,128]{1,0:T(8,128)(2,1)S(1)}, bf16[1664,128]{1,0:T(8,128)(2,1)}, u32[]{:S(2)}, u32[]{:S(2)}) collective-permute-start(bf16[1664,128]{1,0:T(8,128)(2,1)S(1)} %get-tuple-element.17), channel_id=1, source_target_pairs={{8,16},{16,8},{24,32},{32,24},{40,48},{48,40},{56,192},{192,56},{7... | collective-permute-start | bytes 1277960 | tf_op jit(solution)/shard_map/ppermute | solution.py:342
  9.8 1.1 %collective-permute-start = (bf16[4,112,128]{2,1,0:T(8,128)(2,1)S(1)}, bf16[4,112,128]{2,1,0:T(8,128)(2,1)S(1)}, u32[]{:S(2)}, u32[]{:S(2)}) collective-permute-start(bf16[4,112,128]{2,1,0:T(8,128)(2,1)S(1)} %get-tuple-element.14), channel_id=1, source_target_pairs={{0,1},{1,0},{2,3},{3,2},{4,5},{5,4},{6,7},{7,6},{8,9},{9,8},{10,11... | collective-permute-start | bytes 344072 | tf_op jit(solution)/shard_map/ppermute | solution.py:339
  10.9 1.9 %collective-permute-start.1 = (bf16[4,112,128]{2,1,0:T(8,128)(2,1)S(1)}, bf16[4,112,128]{2,1,0:T(8,128)(2,1)S(1)}, u32[]{:S(2)}, u32[]{:S(2)}) collective-permute-start(bf16[4,112,128]{2,1,0:T(8,128)(2,1)S(1)} %get-tuple-element.15), channel_id=1, source_target_pairs={{1,2},{2,1},{3,4},{4,3},{5,6},{6,5},{9,10},{10,9},{11,12},{12,11},... | collective-permute-start | bytes 344072 | tf_op jit(solution)/shard_map/ppermute | solution.py:340
  12.8 1.9 %collective-permute-done.ya = bf16[4,112,128]{2,1,0:T(8,128)(2,1)S(1)} collective-permute-done((bf16[4,112,128]{2,1,0:T(8,128)(2,1)S(1)}, bf16[4,112,128]{2,1,0:T(8,128)(2,1)S(1)}, u32[]{:S(2)}, u32[]{:S(2)}) %collective-permute-start) | collective-permute-done | bytes 114720 | tf_op jit(solution)/shard_map/ppermute | solution.py:339
  14.7 4.1 %collective-permute-done.1.yb = bf16[4,112,128]{2,1,0:T(8,128)(2,1)S(1)} collective-permute-done((bf16[4,112,128]{2,1,0:T(8,128)(2,1)S(1)}, bf16[4,112,128]{2,1,0:T(8,128)(2,1)S(1)}, u32[]{:S(2)}, u32[]{:S(2)}) %collective-permute-start.1) | collective-permute-done | bytes 114720 | tf_op jit(solution)/shard_map/ppermute | solution.py:340
  18.8 1.3 %pack_corners.1 = (bf16[336,128]{1,0:T(8,128)(2,1)}, bf16[336,128]{1,0:T(8,128)(2,1)}) custom-call(s32[4]{0:T(128)S(1)} %pad_add_fusion.place, bf16[4,112,128]{2,1,0:T(8,128)(2,1)S(1)} %collective-permute-done.ya, bf16[4,112,128]{2,1,0:T(8,128)(2,1)S(1)} %collective-permute-done.1.yb), custom_call_target="tpu_custom_call" | custom-call | flops 4096 | bytes 262144 | tf_op jit(solution)/shard_map/pack_corners/pallas_call | solution.py:125
  20.1 0.0 copy-start.8
  20.1 0.0 collective-permute-start.4
  20.1 3.6 %collective-permute-start.5 = (bf16[336,128]{1,0:T(8,128)(2,1)}, bf16[336,128]{1,0:T(8,128)(2,1)}, u32[]{:S(2)}, u32[]{:S(2)}) collective-permute-start(bf16[336,128]{1,0:T(8,128)(2,1)} %get-tuple-element.19), channel_id=1, source_target_pairs={{8,16},{16,8},{24,32},{32,24},{40,48},{48,40},{56,192},{192,56},{7... | collective-permute-start | bytes 258056 | tf_op jit(solution)/shard_map/ppermute | solution.py:346
  23.7 0.0 copy-done.8
  23.7 0.1 copy.9.cond
  23.8 0.0 copy-start.6
  23.8 1.1 %copy.8.spatial = bf16[3,3,128,32]{3,2,1,0:T(8,128)(2,1)S(1)} copy(bf16[3,3,128,32]{2,3,1,0:T(8,128)(2,1)} %param.11) | data formatting | bytes 147456 | tf_op args[4]
  24.9 0.0 copy-done.6
  25.0 0.0 copy-start.5
  25.0 0.2 widen_weights.1
  25.2 0.0 collective-permute-done.4.da
  25.2 4.4 %collective-permute-done.5.db = bf16[336,128]{1,0:T(8,128)(2,1)} collective-permute-done((bf16[336,128]{1,0:T(8,128)(2,1)}, bf16[336,128]{1,0:T(8,128)(2,1)}, u32[]{:S(2)}, u32[]{:S(2)}) %collective-permute-start.5) | collective-permute-done | bytes 86048 | tf_op jit(solution)/shard_map/ppermute | solution.py:346
  29.6 0.0 collective-permute-done.2.xa
  29.6 0.0 collective-permute-done.3.xb
  29.6 0.0 copy-start.7
  29.6 0.0 copy-done.1
  29.6 0.0 copy-done.3
  29.6 0.0 copy-done.5
  29.7 0.6 %copy-done.7 = s32[3]{0:T(128)S(1)} copy-done((s32[3]{0:T(128)S(1)}, s32[3]{0:T(128)}, u32[]{:S(2)}) %copy-start.7) | copy-done | bytes 36
  30.3 21.3 %sample_slab.1 = f32[4,16,32,128]{3,2,1,0:T(8,128)} custom-call(s32[4]{0:T(128)S(1)} %pad_add_fusion.place, s32[3]{0:T(128)S(1)} %copy-done.7, f32[4,16,32,128]{3,2,1,0:T(8,128)S(1)} %copy-done.1, bf16[2,4,16,32,128]{4,3,2,1,0:T(8,128)(2,1)S(1)} %copy-done.3, bf16[4,128,128]{2,1,0:T(8,128)(2,1)S(1)} %bitcast.6, ...), custom_call_target="tpu_custom_call" | custom-call | flops 2147483648 | bytes 5242880 | tf_op jit(solution)/shard_map/sample_slab/pallas_call | solution.py:317
Async XLA Ops:
  0.1 1.2 %copy-start = (f32[4,16,32,128]{3,2,1,0:T(8,128)S(1)}, f32[4,16,32,128]{3,2,1,0:T(8,128)}, u32[]{:S(2)}) copy-start(f32[4,16,32,128]{3,2,1,0:T(8,128)} %lat.3) | copy-start | bytes 3145732
  1.3 1.2 %copy-start.2 = (bf16[2,4,16,32,128]{4,3,2,1,0:T(8,128)(2,1)S(1)}, bf16[2,4,16,32,128]{4,3,2,1,0:T(8,128)(2,1)}, u32[]{:S(2)}) copy-start(bf16[2,4,16,32,128]{4,3,2,1,0:T(8,128)(2,1)} %noise.3) | copy-start | bytes 3145732
  2.5 0.9 %copy-start.4 = (bf16[4,16,8,128]{3,2,1,0:T(8,128)(2,1)S(1)}, bf16[4,16,8,128]{3,2,1,0:T(8,128)(2,1)}, u32[]{:S(2)}) copy-start(bf16[4,16,8,128]{3,2,1,0:T(8,128)(2,1)} %param.9) | copy-start | bytes 393220
  3.4 26.2 %copy-start.1 = (f32[4,16,32,128]{3,2,1,0:T(8,128)S(1)}, f32[4,16,32,128]{3,2,1,0:T(8,128)}, u32[]{:S(2)}) copy-start(f32[4,16,32,128]{3,2,1,0:T(8,128)} %lat.3) | copy-start | bytes 3145732
  3.4 26.2 %copy-start.3 = (bf16[2,4,16,32,128]{4,3,2,1,0:T(8,128)(2,1)S(1)}, bf16[2,4,16,32,128]{4,3,2,1,0:T(8,128)(2,1)}, u32[]{:S(2)}) copy-start(bf16[2,4,16,32,128]{4,3,2,1,0:T(8,128)(2,1)} %noise.3) | copy-start | bytes 3145732
  4.9 24.8 %collective-permute-start.2 = (bf16[1664,128]{1,0:T(8,128)(2,1)}, bf16[1664,128]{1,0:T(8,128)(2,1)S(1)}, u32[]{:S(2)}, u32[]{:S(2)}) collective-permute-start(bf16[1664,128]{1,0:T(8,128)(2,1)} %get-tuple-element.16), channel_id=1, source_target_pairs={{0,8},{8,0},{16,24},{24,16},{32,40},{40,32},{48,56},{56,48},{64,72... | collective-permute-start | bytes 1277960 | tf_op jit(solution)/shard_map/ppermute | solution.py:341
  4.9 24.8 %collective-permute-start.3 = (bf16[1664,128]{1,0:T(8,128)(2,1)S(1)}, bf16[1664,128]{1,0:T(8,128)(2,1)}, u32[]{:S(2)}, u32[]{:S(2)}) collective-permute-start(bf16[1664,128]{1,0:T(8,128)(2,1)S(1)} %get-tuple-element.17), channel_id=1, source_target_pairs={{8,16},{16,8},{24,32},{32,24},{40,48},{48,40},{56,192},{192,56},{7... | collective-permute-start | bytes 1277960 | tf_op jit(solution)/shard_map/ppermute | solution.py:342
  9.8 4.9 %collective-permute-start = (bf16[4,112,128]{2,1,0:T(8,128)(2,1)S(1)}, bf16[4,112,128]{2,1,0:T(8,128)(2,1)S(1)}, u32[]{:S(2)}, u32[]{:S(2)}) collective-permute-start(bf16[4,112,128]{2,1,0:T(8,128)(2,1)S(1)} %get-tuple-element.14), channel_id=1, source_target_pairs={{0,1},{1,0},{2,3},{3,2},{4,5},{5,4},{6,7},{7,6},{8,9},{9,8},{10,11... | collective-permute-start | bytes 344072 | tf_op jit(solution)/shard_map/ppermute | solution.py:339
  10.9 7.9 %collective-permute-start.1 = (bf16[4,112,128]{2,1,0:T(8,128)(2,1)S(1)}, bf16[4,112,128]{2,1,0:T(8,128)(2,1)S(1)}, u32[]{:S(2)}, u32[]{:S(2)}) collective-permute-start(bf16[4,112,128]{2,1,0:T(8,128)(2,1)S(1)} %get-tuple-element.15), channel_id=1, source_target_pairs={{1,2},{2,1},{3,4},{4,3},{5,6},{6,5},{9,10},{10,9},{11,12},{12,11},... | collective-permute-start | bytes 344072 | tf_op jit(solution)/shard_map/ppermute | solution.py:340
  20.1 3.7 %copy-start.8 = (bf16[128,8]{0,1:T(8,128)(2,1)S(1)}, bf16[128,8]{0,1:T(8,128)(2,1)}, u32[]{:S(2)}) copy-start(bf16[128,8]{0,1:T(8,128)(2,1)} %param.12) | copy-start | bytes 6148
  20.1 5.1 %collective-permute-start.4 = (bf16[336,128]{1,0:T(8,128)(2,1)}, bf16[336,128]{1,0:T(8,128)(2,1)}, u32[]{:S(2)}, u32[]{:S(2)}) collective-permute-start(bf16[336,128]{1,0:T(8,128)(2,1)} %get-tuple-element.18), channel_id=1, source_target_pairs={{0,8},{8,0},{16,24},{24,16},{32,40},{40,32},{48,56},{56,48},{64,72... | collective-permute-start | bytes 258056 | tf_op jit(solution)/shard_map/ppermute | solution.py:345
  20.1 9.6 %collective-permute-start.5 = (bf16[336,128]{1,0:T(8,128)(2,1)}, bf16[336,128]{1,0:T(8,128)(2,1)}, u32[]{:S(2)}, u32[]{:S(2)}) collective-permute-start(bf16[336,128]{1,0:T(8,128)(2,1)} %get-tuple-element.19), channel_id=1, source_target_pairs={{8,16},{16,8},{24,32},{32,24},{40,48},{48,40},{56,192},{192,56},{7... | collective-permute-start | bytes 258056 | tf_op jit(solution)/shard_map/ppermute | solution.py:346
  23.8 1.1 %copy-start.6 = (bf16[3,32,128]{2,1,0:T(8,128)(2,1)S(1)}, bf16[3,32,128]{2,1,0:T(8,128)(2,1)}, u32[]{:S(2)}) copy-start(bf16[3,32,128]{2,1,0:T(8,128)(2,1)} %temporal.1) | copy-start | bytes 73732
  25.0 4.7 %copy-start.5 = (bf16[4,16,8,128]{3,2,1,0:T(8,128)(2,1)S(1)}, bf16[4,16,8,128]{3,2,1,0:T(8,128)(2,1)}, u32[]{:S(2)}) copy-start(bf16[4,16,8,128]{3,2,1,0:T(8,128)(2,1)} %param.9) | copy-start | bytes 393220
  29.6 0.7 %copy-start.7 = (s32[3]{0:T(128)S(1)}, s32[3]{0:T(128)}, u32[]{:S(2)}) copy-start(s32[3]{0:T(128)} %steps.1) | copy-start | bytes 40

commit v2 on v1

v2 whole, which is shorter than its diff:
```python
import jax
import jax.numpy as jnp
from jax import lax
from jax.experimental import pallas as pl
from jax.experimental.pallas import tpu as pltpu
from jax.sharding import PartitionSpec as P

F32 = jnp.float32
BF16 = jnp.bfloat16
VMEM_ALL = 60 << 20
AXES = ("cfg", "gx", "gy")
NCFG, NGX, NGY = 2, 16, 8
ROWS, COLS, C, FF, CK, NT = 4, 16, 32, 128, 8, 128
YROWS = 2 * C + C + 2 * CK
WIDE, MID = COLS + 4, COLS + 2
XROWS = 2 * WIDE * C + MID * C + MID * CK


def linear(cfg, gx, gy):
    return (cfg * NGX + gx) * NGY + gy


def swaps_x(parity):
    pairs = []
    for cfg in range(NCFG):
        for gy in range(NGY):
            for gx in range(parity, NGX - 1, 2):
                other = 1 - cfg if gx == NGX // 2 - 1 else cfg
                a, b = linear(cfg, gx, gy), linear(other, gx + 1, gy)
                pairs += [(a, b), (b, a)]
    return pairs


def swaps_y(parity):
    pairs = []
    for cfg in range(NCFG):
        for gx in range(NGX):
            for gy in range(parity, NGY - 1, 2):
                a, b = linear(cfg, gx, gy), linear(cfg, gx, gy + 1)
                pairs += [(a, b), (b, a)]
    return pairs


def vmem():
    return pl.BlockSpec(memory_space=pltpu.VMEM)


def smem():
    return pl.BlockSpec(memory_space=pltpu.SMEM)


def join16(*parts):
    return jnp.concatenate([p.astype(F32) for p in parts], axis=0).astype(BF16)


def any_space():
    return pl.BlockSpec(memory_space=pl.ANY)


def cells(v):
    return v.astype(F32).reshape(-1, C, NT)


def pack_y_kernel(place, lat, noise, cond, ya, yb, xs, ns, cs, sems):
    copies = []
    for side, (lo, inner, field) in enumerate(((0, 0, 0), (COLS - 2, COLS - 1, (COLS - 2) * CK))):
        copies.append(pltpu.make_async_copy(lat.at[:, lo : lo + 2], xs.at[side], sems.at[3 * side]))
        copies.append(pltpu.make_async_copy(noise.at[0, :, inner], ns.at[side], sems.at[3 * side + 1]))
        copies.append(
            pltpu.make_async_copy(cond.at[:, field : field + 2 * CK, :], cs.at[side], sems.at[3 * side + 2])
        )
    for copy in copies:
        copy.start()
    for copy in copies:
        copy.wait()

    def pack_y(out, side):
        for r in range(ROWS):
            out[r, 0 : 2 * C, :] = xs[side, r].reshape(2 * C, NT).astype(BF16)
            out[r, 2 * C : 3 * C, :] = ns[side, r]
            both = cs[side, r].astype(F32)
            cell = both[CK:] if side else both[0:CK]
            out[r, 3 * C :, :] = join16(cell, cell)

    for parity in range(2):

        @pl.when(place[1] == parity)
        def _():
            pack_y(ya, 1 - parity)
            pack_y(yb, parity)


def pack_y(place, lat, noise, cond):
    y = jax.ShapeDtypeStruct((ROWS, YROWS, NT), BF16)
    return pl.pallas_call(
        pack_y_kernel,
        out_shape=(y, y),
        in_specs=[smem(), any_space(), any_space(), any_space()],
        out_specs=(vmem(),) * 2,
        scratch_shapes=[
            pltpu.VMEM((2, ROWS, 2, C, NT), F32),
            pltpu.VMEM((2, ROWS, C, NT), BF16),
            pltpu.VMEM((2, ROWS, 2 * CK, NT), BF16),
            pltpu.SemaphoreType.DMA((6,)),
        ],
        compiler_params=pltpu.CompilerParams(vmem_limit_bytes=VMEM_ALL),
        cost_estimate=pl.CostEstimate(flops=1 << 16, bytes_accessed=1 << 19, transcendentals=0),
        name="pack_columns",
    )(place, lat, noise, cond)


def halo_columns(place, ya, yb):
    even = place[1] == 0
    return (
        lambda r: jnp.where(even, yb[r], ya[r]),
        lambda r: jnp.where(even, ya[r], yb[r]),
    )


def wide_latent(lat_row, low, high):
    return jnp.concatenate([cells(low[0 : 2 * C]), lat_row, cells(high[0 : 2 * C])], axis=0)


def wide_noise(noise_row, low, high):
    return jnp.concatenate(
        [cells(low[2 * C : 3 * C]), noise_row.astype(F32), cells(high[2 * C : 3 * C])], axis=0
    )


def wide_cond_row(cond_row, low, high):
    return join16(low.astype(F32)[3 * C : 3 * C + CK], cond_row, high.astype(F32)[3 * C : 3 * C + CK])


def pack_x_kernel(place, lat, noise, cond, ya, yb, xa, xb, token):
    lows, highs = halo_columns(place, ya, yb)

    def pack_x(out, top):
        lo, inner = (ROWS - 2, ROWS - 1) if top else (0, 0)
        n = WIDE * C
        for i in range(2):
            low, high = lows(lo + i), highs(lo + i)
            out[i * n : (i + 1) * n, :] = wide_latent(lat[lo + i], low, high).astype(BF16).reshape(n, NT)
            if lo + i == inner:
                out[2 * n : 2 * n + MID * C, :] = (
                    wide_noise(noise[0, inner], low, high).astype(BF16).reshape(MID * C, NT)
                )
                out[2 * n + MID * C :, :] = wide_cond_row(cond[inner], low, high)

    for parity in range(2):

        @pl.when(place[0] == parity)
        def _():
            pack_x(xa, parity == 0)
            pack_x(xb, parity == 1)

    token[...] = jnp.zeros(token.shape, F32)


def pack_x(place, lat, noise, cond, ya, yb):
    x = jax.ShapeDtypeStruct((XROWS, NT), BF16)
    return pl.pallas_call(
        pack_x_kernel,
        out_shape=(x, x, jax.ShapeDtypeStruct((8, NT), F32)),
        in_specs=[smem()] + [vmem()] * 5,
        out_specs=(vmem(),) * 3,
        compiler_params=pltpu.CompilerParams(vmem_limit_bytes=24 << 20),
        cost_estimate=pl.CostEstimate(flops=1 << 18, bytes_accessed=3 << 20, transcendentals=0),
        name="pack_rows",
    )(place, lat, noise, cond, ya, yb)


def weights_kernel(spatial, cond, temporal, wide, wide_cond, wide_temporal):
    blank = jnp.zeros((C, FF), F32)
    for dx in range(3):
        taps = [0.5 * spatial[dx, dy].astype(F32) for dy in range(3)]
        at = slice(dx * 4 * C, (dx + 1) * 4 * C)
        wide[0:FF, at] = jnp.concatenate(taps + [blank], axis=0).T.astype(BF16)
        wide[FF:, at] = jnp.concatenate([blank] + taps, axis=0).T.astype(BF16)
    small = 0.5 * cond[...].astype(F32)
    none = jnp.zeros((FF - CK, FF), F32)
    pair = jnp.concatenate([small, none], axis=0).T[:, 0:CK]
    gap = jnp.zeros((FF, CK), F32)
    wide_cond[0:FF, :] = jnp.concatenate([pair, gap], axis=1).astype(BF16)
    wide_cond[FF:, :] = jnp.concatenate([gap, pair], axis=1).astype(BF16)
    wide_temporal[...] = jnp.zeros(wide_temporal.shape, BF16)
    wide_temporal[0 : 3 * C, 0:FF] = (2.0 * temporal[...].astype(F32)).astype(BF16).reshape(3 * C, FF)
    wide_temporal[3 * C :, FF:] = (2.0 * temporal[...].astype(F32)).astype(BF16).reshape(3 * C, FF)


def widen(spatial, cond, temporal):
    return pl.pallas_call(
        weights_kernel,
        out_shape=(
            jax.ShapeDtypeStruct((2 * FF, 12 * C), BF16),
            jax.ShapeDtypeStruct((2 * FF, 2 * CK), BF16),
            jax.ShapeDtypeStruct((6 * C, 2 * FF), BF16),
        ),
        in_specs=[vmem()] * 3,
        out_specs=(vmem(),) * 3,
        compiler_params=pltpu.CompilerParams(vmem_limit_bytes=16 << 20),
        cost_estimate=pl.CostEstimate(flops=1 << 18, bytes_accessed=1 << 20, transcendentals=0),
        name="widen_weights",
    )(spatial, cond, temporal)


def log_alpha(when):
    shape = (8, 128)
    position = lax.broadcasted_iota(jnp.int32, shape, 0) * 128 + lax.broadcasted_iota(jnp.int32, shape, 1)
    beta = 0.0001 + (0.02 - 0.0001) * position.astype(F32) / 999.0
    logs = jnp.log(1.0 - jnp.minimum(beta, 0.5))
    return jnp.sum(jnp.where(position <= when, logs, 0.0))


def coefficients(now, later):
    a = jnp.exp(jnp.full((1, NT), log_alpha(now), F32))
    p = jnp.exp(jnp.full((1, NT), log_alpha(later), F32))
    sigma = 0.5 * jnp.sqrt((1.0 - p) / (1.0 - a)) * jnp.sqrt(1.0 - a / p)
    keep = jnp.sqrt(p) / jnp.sqrt(a)
    move = jnp.sqrt(1.0 - p - sigma * sigma) - keep * jnp.sqrt(1.0 - a)
    return keep, move, sigma


def silu(v):
    half = 0.5 * v
    return half + half * jnp.tanh(half)


def normalize(x):
    mean = jnp.sum(jnp.sum(x * x, axis=1, keepdims=True), axis=2, keepdims=True) * (1.0 / (C * NT))
    return x * lax.rsqrt(mean + 1e-05)


def block(rows, cond_rows, pairs, wide, wide_cond, wide_temporal):
    windows = [
        jnp.concatenate([row(2 * C * p, 2 * C * p + 4 * C) for row in rows], axis=0) for p in pairs
    ]
    fields = [cond_rows(p) for p in pairs]
    rhs = jnp.concatenate(windows, axis=1) if len(pairs) > 1 else windows[0]
    field = jnp.concatenate(fields, axis=1) if len(pairs) > 1 else fields[0]
    free = jnp.dot(wide[...], rhs, preferred_element_type=F32)
    given = (free + jnp.dot(wide_cond[...], field, preferred_element_type=F32)).astype(BF16)
    free = free.astype(BF16)
    hidden = (given + given * jnp.tanh(given)) * BF16(1.5) - (free + free * jnp.tanh(free))
    taps = jnp.dot(wide_temporal[...], hidden, preferred_element_type=F32)
    time = lax.broadcasted_iota(jnp.int32, (C, NT), 1)
    sums = []
    for q in range(len(pairs)):
        for o in range(2):
            t = taps[3 * C * o : 3 * C * (o + 1), NT * q : NT * (q + 1)]
            before = jnp.where(time == 0, 0.0, pltpu.roll(t[0:C], 1, 1))
            after = jnp.where(time == NT - 1, 0.0, pltpu.roll(t[2 * C :], NT - 1, 1))
            sums.append(before + t[C : 2 * C] + after)
    return sums


def prepare(x, fresh, factors):
    normed = normalize(x)
    act = silu(normed).astype(BF16).reshape(WIDE * C, NT)
    if fresh is None:
        return act, None
    keep, move, sigma = factors
    value = keep * x[1 : MID + 1] + move * normed[1 : MID + 1] + sigma * fresh
    return act, value.reshape(MID * C, NT)


def pick(ref, *lead):
    return lambda lo, hi: ref[(*lead, slice(lo, hi), slice(None))]


def first_step(rows, condx, e, base, move, weights):
    sums = block(
        rows, lambda p: condx[e, 2 * CK * p : 2 * CK * (p + 1), :], list(range(MID // 2)), *weights
    )
    for i, s in enumerate(sums):
        base[e, i * C : (i + 1) * C, :] = base[e, i * C : (i + 1) * C, :] + move * s


def inner_kernel(place, steps, lat, noise, cond, ya, yb, wide, wide_cond, wide_temporal, token, act, base, condx):
    del token
    factors = coefficients(steps[0], steps[1])
    lows, highs = halo_columns(place, ya, yb)
    for r in range(ROWS):
        low, high = lows(r), highs(r)
        act[r], base[r] = prepare(
            wide_latent(lat[r], low, high), wide_noise(noise[0, r], low, high), factors
        )
        condx[r] = wide_cond_row(cond[r], low, high)
    for r in range(1, ROWS - 1):
        first_step(
            [pick(act, r + d) for d in (-1, 0, 1)], condx, r, base, factors[1], (wide, wide_cond, wide_temporal)
        )


def inner(place, steps, lat, noise, cond, ya, yb, weights, token):
    return pl.pallas_call(
        inner_kernel,
        out_shape=(
            jax.ShapeDtypeStruct((ROWS, WIDE * C, NT), BF16),
            jax.ShapeDtypeStruct((ROWS, MID * C, NT), F32),
            jax.ShapeDtypeStruct((ROWS, MID * CK, NT), BF16),
        ),
        in_specs=[smem(), smem()] + [vmem()] * 9,
        out_specs=(vmem(),) * 3,
        compiler_params=pltpu.CompilerParams(vmem_limit_bytes=24 << 20),
        cost_estimate=pl.CostEstimate(flops=1 << 30, bytes_accessed=4 << 20, transcendentals=2 << 20),
        name="inner_rows",
    )(place, steps, lat, noise, cond, ya, yb, *weights, token)


def main_kernel(
    place, steps, noise, cond, xa, xb, act, base_own, condx_own, wide, wide_cond, wide_temporal,
    out, outer, base, condx, act2,
):
    weights = (wide, wide_cond, wide_temporal)
    factors = coefficients(steps[0], steps[1])
    even_x = place[0] == 0
    n = WIDE * C
    for top in (False, True):
        face = lambda lo, hi: jnp.where(even_x == top, xa[lo:hi, :], xb[lo:hi, :])
        near = 0 if top else 1
        for i in range(2):
            fresh = cells(face(2 * n, 2 * n + MID * C)) if i == near else None
            done, value = prepare(cells(face(i * n, (i + 1) * n)), fresh, factors)
            outer[2 * top + i] = done
            if i == near:
                base[2 + top] = value
                condx[2 + top] = face(2 * n + MID * C, XROWS)
    for i, r in enumerate((0, ROWS - 1)):
        base[i] = base_own[r]
        condx[i] = condx_own[r]

    halo = {-2: 0, -1: 1, ROWS: 2, ROWS + 1: 3}
    for r, slot in ((0, 0), (ROWS - 1, 1), (-1, 2), (ROWS, 3)):
        rows = [pick(outer, halo[r + d]) if r + d in halo else pick(act, r + d) for d in (-1, 0, 1)]
        first_step(rows, condx, slot, base, factors[1], weights)

    keep2, move2, sigma2 = coefficients(steps[1], steps[2])
    left = jnp.where(place[3] == 0, 0.0, 1.0)
    right = jnp.where(place[3] == NGY - 1, 0.0, 1.0)
    for e in range(6):
        r = e - 1
        x = (base_own[r] if 0 < r < ROWS - 1 else base[{0: 0, ROWS - 1: 1, -1: 2, ROWS: 3}[r]]).reshape(MID, C, NT)
        normed = normalize(x)
        value = silu(normed)
        value = jnp.concatenate([value[0:1] * left, value[1 : MID - 1], value[MID - 1 :] * right], axis=0)
        if e == 0:
            value = value * jnp.where(place[2] == 0, 0.0, 1.0)
        if e == 5:
            value = value * jnp.where(place[2] == NGX - 1, 0.0, 1.0)
        act2[e] = value.astype(BF16).reshape(MID * C, NT)
        if 0 < e < 5:
            out[r] = (
                keep2 * x[1 : MID - 1] + move2 * normed[1 : MID - 1] + sigma2 * noise[1, r].astype(F32)
            )

    def second(r, carry):
        sums = block(
            [pick(act2, r + d) for d in range(3)],
            lambda p: cond[r, 2 * CK * p : 2 * CK * (p + 1), :],
            list(range(COLS // 2)),
            *weights,
        )
        for i, s in enumerate(sums):
            out[r, i] = out[r, i] + move2 * s
        return carry

    lax.fori_loop(0, ROWS, second, 0)


def sample(place, steps, noise, cond, xa, xb, act, base, condx, weights):
    return pl.pallas_call(
        main_kernel,
        out_shape=jax.ShapeDtypeStruct((ROWS, COLS, C, NT), F32),
        in_specs=[smem(), smem()] + [vmem()] * 10,
        out_specs=vmem(),
        scratch_shapes=[
            pltpu.VMEM((4, WIDE * C, NT), BF16),
            pltpu.VMEM((4, MID * C, NT), F32),
            pltpu.VMEM((4, MID * CK, NT), BF16),
            pltpu.VMEM((6, MID * C, NT), BF16),
        ],
        compiler_params=pltpu.CompilerParams(vmem_limit_bytes=32 << 20),
        cost_estimate=pl.CostEstimate(flops=2 << 30, bytes_accessed=5 << 20, transcendentals=5 << 20),
        name="sample_slab",
    )(place, steps, noise, cond, xa, xb, act, base, condx, *weights)


def on_device(latent, sample_noise, cond_field, timesteps, spatial_weight, cond_weight, temporal_weight):
    gx, gy = lax.axis_index("gx"), lax.axis_index("gy")
    place = jnp.stack([gx % 2, gy % 2, gx, gy]).astype(jnp.int32)
    cond = cond_field.reshape(ROWS, COLS * CK, NT)
    ya, yb = pack_y(place, latent, sample_noise, cond)
    ya = lax.ppermute(ya, AXES, swaps_y(0))
    yb = lax.ppermute(yb, AXES, swaps_y(1))
    weights = widen(jnp.swapaxes(spatial_weight, 2, 3), cond_weight.T, temporal_weight)
    xa, xb, token = pack_x(place, latent, sample_noise, cond, ya, yb)
    xa = lax.ppermute(xa, AXES, swaps_x(0))
    xb = lax.ppermute(xb, AXES, swaps_x(1))
    act, base, condx = inner(place, timesteps, latent, sample_noise, cond, ya, yb, weights, token)
    return sample(place, timesteps, sample_noise, cond, xa, xb, act, base, condx, weights)


def solution(mesh):
    in_specs = (
        P("gx", "gy", None, None),
        P(None, "gx", "gy", None, None),
        P("gx", "gy", None, None),
        P(),
        P(),
        P(),
        P(),
    )
    return jax.shard_map(
        on_device, mesh=mesh, in_specs=in_specs, out_specs=P("gx", "gy", None, None), check_vma=False
    )
```

time: 51.9 us -> 37.6 us (0.72)
  the two profiles are of different devices: /device:TPU:134 before, /device:TPU:121 now
where the time goes in v2:
time: 37.6 us; the launch traced here: 37.5 us
  Pallas kernels  16 us (43%)
  starting transfers between devices  11.2 us (30%)
  waiting for transfers between devices  9.41 us (25%)
  other arithmetic  0.62 us (2%)
    pallas_call x1, Pallas kernels, sample(): pl.pallas_call(main_kernel, out_shape=jax.ShapeDtypeStruct((ROWS, COLS, C...  9.73 us
    ppermute x1, waiting for transfers between devices, on_device(): xb = lax.ppermute(xb, AXES, swaps_x(1))  6.67 us
    ppermute x1, starting transfers between devices, on_device(): yb = lax.ppermute(yb, AXES, swaps_y(1))  5.58 us
    ppermute x1, starting transfers between devices, on_device(): xb = lax.ppermute(xb, AXES, swaps_x(1))  3.94 us
    pallas_call x1, Pallas kernels, inner(): pl.pallas_call(inner_kernel, out_shape=(jax.ShapeDtypeStruct((ROWS, WIDE...  2.8 us
    ppermute x1, waiting for transfers between devices, on_device(): yb = lax.ppermute(yb, AXES, swaps_y(1))  2.74 us
    pallas_call x1, Pallas kernels, pack_y(): pl.pallas_call(pack_y_kernel, out_shape=(y, y), in_specs=[smem(), any_spa...  2.56 us
    ppermute x1, starting transfers between devices, on_device(): xa = lax.ppermute(xa, AXES, swaps_x(0))  1.63 us
  transfers between devices with their start and end apart: 4, of which 2 were waited for; matrix products, arithmetic and copies ran while one was open for 0% of the time, Pallas kernels for 8%

profile of v2, /device:TPU:121, one launch (start us, length us, event | category | flops | bytes accessed | tf_op | source)
XLA Modules:
  0.0 37.5 jit_solution(10428672769609453314)
XLA Ops:
  0.0 0.0 copy-start.1
  0.0 0.0 copy-start
  0.0 0.0 copy-start.2
  0.0 0.6 %pad_add_fusion.place = s32[4]{0:T(128)} fusion(s32[1]{0:T(128)} %bitcast.3, s32[1]{0:T(128)} %bitcast.2, s32[1]{0:T(128)} %bitcast.1, s32[1]{0:T(128)} %bitcast), kind=kLoop, calls=%fused_computation | loop fusion | flops 12 | bytes 32 | tf_op jit(solution)/shard_map/stack | solution.py:390
  0.7 0.0 copy-start.5
  0.7 2.6 %pack_columns.1 = (bf16[4,112,128]{2,1,0:T(8,128)(2,1)}, bf16[4,112,128]{2,1,0:T(8,128)(2,1)}) custom-call(s32[4]{0:T(128)} %pad_add_fusion.place, f32[4,16,32,128]{3,2,1,0:T(8,128)} %lat.5, bf16[2,4,16,32,128]{4,3,2,1,0:T(8,128)(2,1)} %noise.7, bf16[4,128,128]{2,1,0:T(8,128)(2,1)} %bitcast.7), custom_call_target="tpu_custom_call" | custom-call | flops 65536 | bytes 524288 | tf_op jit(solution)/shard_map/pack_columns/pallas_call | solution.py:95
  3.2 0.1 collective-permute-start
  3.3 0.0 copy-start.3
  3.3 0.0 copy-start.4
  3.3 0.0 copy-start.6
  3.4 0.0 copy-start.7
  3.4 5.6 %collective-permute-start.1 = (bf16[4,112,128]{2,1,0:T(8,128)(2,1)}, bf16[4,112,128]{2,1,0:T(8,128)(2,1)S(1)}, u32[]{:S(2)}, u32[]{:S(2)}) collective-permute-start(bf16[4,112,128]{2,1,0:T(8,128)(2,1)} %get-tuple-element.17), channel_id=1, source_target_pairs={{1,2},{2,1},{3,4},{4,3},{5,6},{6,5},{9,10},{10,9},{11,12},{12,11},... | collective-permute-start | bytes 344072 | tf_op jit(solution)/shard_map/ppermute | solution.py:394
  9.0 0.0 collective-permute-done.ya
  9.0 2.7 %collective-permute-done.1.yb = bf16[4,112,128]{2,1,0:T(8,128)(2,1)S(1)} collective-permute-done((bf16[4,112,128]{2,1,0:T(8,128)(2,1)}, bf16[4,112,128]{2,1,0:T(8,128)(2,1)S(1)}, u32[]{:S(2)}, u32[]{:S(2)}) %collective-permute-start.1) | collective-permute-done | bytes 114720 | tf_op jit(solution)/shard_map/ppermute | solution.py:394
  11.7 0.0 copy-done.1
  11.7 0.0 copy-done
  11.7 0.0 copy-done.2
  11.7 0.0 copy-done.5
  11.7 0.7 %pack_rows.1 = (bf16[2000,128]{1,0:T(8,128)(2,1)S(1)}, bf16[2000,128]{1,0:T(8,128)(2,1)S(1)}, f32[8,128]{1,0:T(8,128)S(1)}) custom-call(s32[4]{0:T(128)S(1)} %copy-done.5, f32[4,16,32,128]{3,2,1,0:T(8,128)S(1)} %copy-done, bf16[2,4,16,32,128]{4,3,2,1,0:T(8,128)(2,1)S(1)} %copy-done.1, bf16[4,128,128]{2,1,0:T(8,128)(2,1)S(1)} %bitcast.8, ...), custom_call_target="tpu_custom_call" | custom-call | flops 262144 | bytes 3145728 | tf_op jit(solution)/shard_map/pack_rows/pallas_call | solution.py:161
  12.4 1.6 %collective-permute-start.2 = (bf16[2000,128]{1,0:T(8,128)(2,1)S(1)}, bf16[2000,128]{1,0:T(8,128)(2,1)S(1)}, u32[]{:S(2)}, u32[]{:S(2)}) collective-permute-start(bf16[2000,128]{1,0:T(8,128)(2,1)S(1)} %get-tuple-element.18), channel_id=1, source_target_pairs={{0,8},{8,0},{16,24},{24,16},{32,40},{40,32},{48,56},{56,48},{64,72... | collective-permute-start | bytes 1536008 | tf_op jit(solution)/shard_map/ppermute | solution.py:397
  14.1 3.9 %collective-permute-start.3 = (bf16[2000,128]{1,0:T(8,128)(2,1)S(1)}, bf16[2000,128]{1,0:T(8,128)(2,1)S(1)}, u32[]{:S(2)}, u32[]{:S(2)}) collective-permute-start(bf16[2000,128]{1,0:T(8,128)(2,1)S(1)} %get-tuple-element.19), channel_id=1, source_target_pairs={{8,16},{16,8},{24,32},{32,24},{40,48},{48,40},{56,192},{192,56},{7... | collective-permute-start | bytes 1536008 | tf_op jit(solution)/shard_map/ppermute | solution.py:398
  18.0 0.0 copy-done.3
  18.0 0.0 copy-done.4
  18.0 0.0 copy-done.6
  18.0 0.2 widen_weights.1
  18.2 0.0 copy-done.7
  18.3 2.8 %inner_rows.1 = (bf16[4,640,128]{2,1,0:T(8,128)(2,1)S(1)}, f32[4,576,128]{2,1,0:T(8,128)S(1)}, bf16[4,144,128]{2,1,0:T(8,128)(2,1)S(1)}) custom-call(s32[4]{0:T(128)S(1)} %copy-done.5, s32[3]{0:T(128)S(1)} %copy-done.7, f32[4,16,32,128]{3,2,1,0:T(8,128)S(1)} %copy-done, bf16[2,4,16,32,128]{4,3,2,1,0:T(8,128)(2,1)S(1)} %copy-done.1, ...), custom_call_target="tpu_custom_call" | custom-call | flops 1073741824 | bytes 4194304 | tf_op jit(solution)/shard_map/inner_rows/pallas_call | solution.py:295
  21.1 0.0 collective-permute-done.2.xa
  21.1 6.7 %collective-permute-done.3.xb = bf16[2000,128]{1,0:T(8,128)(2,1)S(1)} collective-permute-done((bf16[2000,128]{1,0:T(8,128)(2,1)S(1)}, bf16[2000,128]{1,0:T(8,128)(2,1)S(1)}, u32[]{:S(2)}, u32[]{:S(2)}) %collective-permute-start.3) | collective-permute-done | bytes 512032 | tf_op jit(solution)/shard_map/ppermute | solution.py:398
  27.7 9.7 %sample_slab.1 = f32[4,16,32,128]{3,2,1,0:T(8,128)} custom-call(s32[4]{0:T(128)S(1)} %copy-done.5, s32[3]{0:T(128)S(1)} %copy-done.7, bf16[2,4,16,32,128]{4,3,2,1,0:T(8,128)(2,1)S(1)} %copy-done.1, bf16[4,128,128]{2,1,0:T(8,128)(2,1)S(1)} %bitcast.10, bf16[2000,128]{1,0:T(8,128)(2,1)S(1)} %collective-permute-done.2.xa, ...), custom_call_target="tpu_custom_call" | custom-call | flops 2147483648 | bytes 5242880 | tf_op jit(solution)/shard_map/sample_slab/pallas_call | solution.py:371
Async XLA Ops:
  0.0 11.7 %copy-start.1 = (bf16[2,4,16,32,128]{4,3,2,1,0:T(8,128)(2,1)S(1)}, bf16[2,4,16,32,128]{4,3,2,1,0:T(8,128)(2,1)}, u32[]{:S(2)}) copy-start(bf16[2,4,16,32,128]{4,3,2,1,0:T(8,128)(2,1)} %noise.7) | copy-start | bytes 3145732
  0.0 11.7 %copy-start = (f32[4,16,32,128]{3,2,1,0:T(8,128)S(1)}, f32[4,16,32,128]{3,2,1,0:T(8,128)}, u32[]{:S(2)}) copy-start(f32[4,16,32,128]{3,2,1,0:T(8,128)} %lat.5) | copy-start | bytes 3145732
  0.0 11.7 %copy-start.2 = (bf16[4,16,8,128]{3,2,1,0:T(8,128)(2,1)S(1)}, bf16[4,16,8,128]{3,2,1,0:T(8,128)(2,1)}, u32[]{:S(2)}) copy-start(bf16[4,16,8,128]{3,2,1,0:T(8,128)(2,1)} %param.9) | copy-start | bytes 393220
  0.7 11.1 %copy-start.5 = (s32[4]{0:T(128)S(1)}, s32[4]{0:T(128)}, u32[]{:S(2)}) copy-start(s32[4]{0:T(128)} %pad_add_fusion.place) | copy-start | bytes 52
  3.2 5.7 %collective-permute-start = (bf16[4,112,128]{2,1,0:T(8,128)(2,1)}, bf16[4,112,128]{2,1,0:T(8,128)(2,1)S(1)}, u32[]{:S(2)}, u32[]{:S(2)}) collective-permute-start(bf16[4,112,128]{2,1,0:T(8,128)(2,1)} %get-tuple-element.16), channel_id=1, source_target_pairs={{0,1},{1,0},{2,3},{3,2},{4,5},{5,4},{6,7},{7,6},{8,9},{9,8},{10,11... | collective-permute-start | bytes 344072 | tf_op jit(solution)/shard_map/ppermute | solution.py:393
  3.3 14.7 %copy-start.3 = (bf16[3,3,128,32]{2,3,1,0:T(8,128)(2,1)S(1)}, bf16[3,3,128,32]{2,3,1,0:T(8,128)(2,1)}, u32[]{:S(2)}) copy-start(bf16[3,3,128,32]{2,3,1,0:T(8,128)(2,1)} %param.11) | copy-start | bytes 221188
  3.3 14.7 %copy-start.4 = (bf16[3,32,128]{2,1,0:T(8,128)(2,1)S(1)}, bf16[3,32,128]{2,1,0:T(8,128)(2,1)}, u32[]{:S(2)}) copy-start(bf16[3,32,128]{2,1,0:T(8,128)(2,1)} %temporal.1) | copy-start | bytes 73732
  3.3 14.7 %copy-start.6 = (bf16[128,8]{0,1:T(8,128)(2,1)S(1)}, bf16[128,8]{0,1:T(8,128)(2,1)}, u32[]{:S(2)}) copy-start(bf16[128,8]{0,1:T(8,128)(2,1)} %param.12) | copy-start | bytes 6148
  3.4 14.9 %copy-start.7 = (s32[3]{0:T(128)S(1)}, s32[3]{0:T(128)}, u32[]{:S(2)}) copy-start(s32[3]{0:T(128)} %steps.3) | copy-start | bytes 40
  3.4 8.3 %collective-permute-start.1 = (bf16[4,112,128]{2,1,0:T(8,128)(2,1)}, bf16[4,112,128]{2,1,0:T(8,128)(2,1)S(1)}, u32[]{:S(2)}, u32[]{:S(2)}) collective-permute-start(bf16[4,112,128]{2,1,0:T(8,128)(2,1)} %get-tuple-element.17), channel_id=1, source_target_pairs={{1,2},{2,1},{3,4},{4,3},{5,6},{6,5},{9,10},{10,9},{11,12},{12,11},... | collective-permute-start | bytes 344072 | tf_op jit(solution)/shard_map/ppermute | solution.py:394
  12.4 8.6 %collective-permute-start.2 = (bf16[2000,128]{1,0:T(8,128)(2,1)S(1)}, bf16[2000,128]{1,0:T(8,128)(2,1)S(1)}, u32[]{:S(2)}, u32[]{:S(2)}) collective-permute-start(bf16[2000,128]{1,0:T(8,128)(2,1)S(1)} %get-tuple-element.18), channel_id=1, source_target_pairs={{0,8},{8,0},{16,24},{24,16},{32,40},{40,32},{48,56},{56,48},{64,72... | collective-permute-start | bytes 1536008 | tf_op jit(solution)/shard_map/ppermute | solution.py:397
  14.1 13.7 %collective-permute-start.3 = (bf16[2000,128]{1,0:T(8,128)(2,1)S(1)}, bf16[2000,128]{1,0:T(8,128)(2,1)S(1)}, u32[]{:S(2)}, u32[]{:S(2)}) collective-permute-start(bf16[2000,128]{1,0:T(8,128)(2,1)S(1)} %get-tuple-element.19), channel_id=1, source_target_pairs={{8,16},{16,8},{24,32},{32,24},{40,48},{48,40},{56,192},{192,56},{7... | collective-permute-start | bytes 1536008 | tf_op jit(solution)/shard_map/ppermute | solution.py:398

commit v3 on v2

--- a/solution.py
+++ b/solution.py
@@ -8,6 +8,7 @@
 F32 = jnp.float32
 BF16 = jnp.bfloat16
 VMEM_ALL = 60 << 20
+VMEM_MOST = 34 << 20
 AXES = ("cfg", "gx", "gy")
 NCFG, NGX, NGY = 2, 16, 8
 ROWS, COLS, C, FF, CK, NT = 4, 16, 32, 128, 8, 128
@@ -61,7 +62,8 @@
     return v.astype(F32).reshape(-1, C, NT)
 
 
-def pack_y_kernel(place, lat, noise, cond, ya, yb, xs, ns, cs, sems):
+def pack_y_kernel(place, lat, noise, cond, ya, yb, token, xs, ns, cs, sems):
+    token[...] = jnp.zeros(token.shape, F32)
     copies = []
     for side, (lo, inner, field) in enumerate(((0, 0, 0), (COLS - 2, COLS - 1, (COLS - 2) * CK))):
         copies.append(pltpu.make_async_copy(lat.at[:, lo : lo + 2], xs.at[side], sems.at[3 * side]))
@@ -94,9 +96,9 @@
     y = jax.ShapeDtypeStruct((ROWS, YROWS, NT), BF16)
     return pl.pallas_call(
         pack_y_kernel,
-        out_shape=(y, y),
+        out_shape=(y, y, jax.ShapeDtypeStruct((8, NT), F32)),
         in_specs=[smem(), any_space(), any_space(), any_space()],
-        out_specs=(vmem(),) * 2,
+        out_specs=(vmem(),) * 3,
         scratch_shapes=[
             pltpu.VMEM((2, ROWS, 2, C, NT), F32),
             pltpu.VMEM((2, ROWS, C, NT), BF16),
@@ -117,21 +119,62 @@
     )
 
 
-def wide_latent(lat_row, low, high):
-    return jnp.concatenate([cells(low[0 : 2 * C]), lat_row, cells(high[0 : 2 * C])], axis=0)
-
-
-def wide_noise(noise_row, low, high):
-    return jnp.concatenate(
-        [cells(low[2 * C : 3 * C]), noise_row.astype(F32), cells(high[2 * C : 3 * C])], axis=0
-    )
+def own_kernel(
+    token, steps, lat, noise, act, base, packed, fresh, fresh2, xs, lat_sems, noise_sems, later_sem
+):
+    del token
+    loads = []
+    for r in range(ROWS):
+        loads.append(
+            (
+                pltpu.make_async_copy(lat.at[r], xs.at[r], lat_sems.at[r]),
+                pltpu.make_async_copy(noise.at[0, r], fresh.at[r], noise_sems.at[r]),
+            )
+        )
+        for load in loads[-1]:
+            load.start()
+    later = pltpu.make_async_copy(noise.at[1], fresh2, later_sem)
+    later.start()
+    factors = coefficients(steps[0], steps[1])
+    for r in range(ROWS):
+        for load in loads[r]:
+            load.wait()
+        x = xs[r]
+        packed[r] = x.astype(BF16).reshape(COLS * C, NT)
+        act[r], base[r] = prepare(x, fresh[r], factors)
+    later.wait()
+
+
+def own(token, steps, lat, noise):
+    n = COLS * C
+    return pl.pallas_call(
+        own_kernel,
+        out_shape=(
+            jax.ShapeDtypeStruct((ROWS, n, NT), BF16),
+            jax.ShapeDtypeStruct((ROWS, n, NT), F32),
+            jax.ShapeDtypeStruct((ROWS, n, NT), BF16),
+            jax.ShapeDtypeStruct((ROWS, COLS, C, NT), BF16),
+            jax.ShapeDtypeStruct((ROWS, COLS, C, NT), BF16),
+        ),
+        in_specs=[vmem(), smem(), any_space(), any_space()],
+        out_specs=(vmem(),) * 5,
+        scratch_shapes=[
+            pltpu.VMEM((ROWS, COLS, C, NT), F32),
+            pltpu.SemaphoreType.DMA((ROWS,)),
+            pltpu.SemaphoreType.DMA((ROWS,)),
+            pltpu.SemaphoreType.DMA,
+        ],
+        compiler_params=pltpu.CompilerParams(vmem_limit_bytes=VMEM_MOST),
+        cost_estimate=pl.CostEstimate(flops=1 << 24, bytes_accessed=4 << 20, transcendentals=1 << 18),
+        name="own_cells",
+    )(token, steps, lat, noise)
 
 
 def wide_cond_row(cond_row, low, high):
     return join16(low.astype(F32)[3 * C : 3 * C + CK], cond_row, high.astype(F32)[3 * C : 3 * C + CK])
 
 
-def pack_x_kernel(place, lat, noise, cond, ya, yb, xa, xb, token):
+def pack_x_kernel(place, packed, fresh, cond, ya, yb, xa, xb, token):
     lows, highs = halo_columns(place, ya, yb)
 
     def pack_x(out, top):
@@ -139,12 +182,15 @@
         n = WIDE * C
         for i in range(2):
             low, high = lows(lo + i), highs(lo + i)
-            out[i * n : (i + 1) * n, :] = wide_latent(lat[lo + i], low, high).astype(BF16).reshape(n, NT)
+            out[i * n : i * n + 2 * C, :] = low[0 : 2 * C]
+            out[i * n + 2 * C : (i + 1) * n - 2 * C, :] = packed[lo + i]
+            out[(i + 1) * n - 2 * C : (i + 1) * n, :] = high[0 : 2 * C]
             if lo + i == inner:
-                out[2 * n : 2 * n + MID * C, :] = (
-                    wide_noise(noise[0, inner], low, high).astype(BF16).reshape(MID * C, NT)
-                )
-                out[2 * n + MID * C :, :] = wide_cond_row(cond[inner], low, high)
+                at, end = 2 * n, 2 * n + MID * C
+                out[at : at + C, :] = low[2 * C : 3 * C]
+                out[at + C : end - C, :] = fresh[inner].reshape(COLS * C, NT)
+                out[end - C : end, :] = high[2 * C : 3 * C]
+                out[end:, :] = wide_cond_row(cond[inner], low, high)
 
     for parity in range(2):
 
@@ -156,7 +202,7 @@
     token[...] = jnp.zeros(token.shape, F32)
 
 
-def pack_x(place, lat, noise, cond, ya, yb):
+def pack_x(place, packed, fresh, cond, ya, yb):
     x = jax.ShapeDtypeStruct((XROWS, NT), BF16)
     return pl.pallas_call(
         pack_x_kernel,
@@ -166,7 +212,7 @@
         compiler_params=pltpu.CompilerParams(vmem_limit_bytes=24 << 20),
         cost_estimate=pl.CostEstimate(flops=1 << 18, bytes_accessed=3 << 20, transcendentals=0),
         name="pack_rows",
-    )(place, lat, noise, cond, ya, yb)
+    )(place, packed, fresh, cond, ya, yb)
 
 
 def weights_kernel(spatial, cond, temporal, wide, wide_cond, wide_temporal):
@@ -230,21 +276,30 @@
     return x * lax.rsqrt(mean + 1e-05)
 
 
-def block(rows, cond_rows, pairs, wide, wide_cond, wide_temporal):
+def spatial_sum(terms, pairs, wide):
     windows = [
-        jnp.concatenate([row(2 * C * p, 2 * C * p + 4 * C) for row in rows], axis=0) for p in pairs
+        jnp.concatenate([row(2 * C * p, 2 * C * p + 4 * C) for _, row in terms], axis=0) for p in pairs
     ]
-    fields = [cond_rows(p) for p in pairs]
-    rhs = jnp.concatenate(windows, axis=1) if len(pairs) > 1 else windows[0]
-    field = jnp.concatenate(fields, axis=1) if len(pairs) > 1 else fields[0]
-    free = jnp.dot(wide[...], rhs, preferred_element_type=F32)
-    given = (free + jnp.dot(wide_cond[...], field, preferred_element_type=F32)).astype(BF16)
+    taps = wide[:, 4 * C * terms[0][0] : 4 * C * (terms[-1][0] + 1)]
+    return jnp.dot(taps, jnp.concatenate(windows, axis=1), preferred_element_type=F32)
+
+
+def cond_pairs(term, first, pairs):
+    cell = lambda i: term[:, NT * (first + i) : NT * (first + i + 1)]
+    return jnp.concatenate(
+        [jnp.concatenate([cell(2 * p), cell(2 * p + 1)], axis=0) for p in range(pairs)], axis=1
+    )
+
+
+def temporal_sum(free, given, wide_temporal):
+    pairs = range(free.shape[1] // NT)
+    given = given.astype(BF16)
     free = free.astype(BF16)
     hidden = (given + given * jnp.tanh(given)) * BF16(1.5) - (free + free * jnp.tanh(free))
     taps = jnp.dot(wide_temporal[...], hidden, preferred_element_type=F32)
     time = lax.broadcasted_iota(jnp.int32, (C, NT), 1)
     sums = []
-    for q in range(len(pairs)):
+    for q in pairs:
         for o in range(2):
             t = taps[3 * C * o : 3 * C * (o + 1), NT * q : NT * (q + 1)]
             before = jnp.where(time == 0, 0.0, pltpu.roll(t[0:C], 1, 1))
@@ -255,66 +310,106 @@
 
 def prepare(x, fresh, factors):
     normed = normalize(x)
-    act = silu(normed).astype(BF16).reshape(WIDE * C, NT)
+    act = silu(normed).astype(BF16).reshape(-1, NT)
     if fresh is None:
         return act, None
     keep, move, sigma = factors
-    value = keep * x[1 : MID + 1] + move * normed[1 : MID + 1] + sigma * fresh
-    return act, value.reshape(MID * C, NT)
+    skip = (x.shape[0] - fresh.shape[0]) // 2
+    part = slice(skip, skip + fresh.shape[0])
+    value = keep * x[part] + move * normed[part] + sigma * fresh.astype(F32)
+    return act, value.reshape(-1, NT)
 
 
 def pick(ref, *lead):
     return lambda lo, hi: ref[(*lead, slice(lo, hi), slice(None))]
 
 
-def first_step(rows, condx, e, base, move, weights):
-    sums = block(
-        rows, lambda p: condx[e, 2 * CK * p : 2 * CK * (p + 1), :], list(range(MID // 2)), *weights
-    )
+def add_sums(sums, base, e, move):
     for i, s in enumerate(sums):
         base[e, i * C : (i + 1) * C, :] = base[e, i * C : (i + 1) * C, :] + move * s
 
 
-def inner_kernel(place, steps, lat, noise, cond, ya, yb, wide, wide_cond, wide_temporal, token, act, base, condx):
+FIRST = range(MID // 2)
+SECOND = range(COLS // 2)
+
+
+def next_act(value, row, place):
+    left = jnp.where(place[3] == 0, 0.0, 1.0)
+    right = jnp.where(place[3] == NGY - 1, 0.0, 1.0)
+    value = jnp.concatenate([value[0:1] * left, value[1 : MID - 1], value[MID - 1 :] * right], axis=0)
+    if row == -1:
+        value = value * jnp.where(place[2] == 0, 0.0, 1.0)
+    if row == ROWS:
+        value = value * jnp.where(place[2] == NGX - 1, 0.0, 1.0)
+    return value.astype(BF16).reshape(MID * C, NT)
+
+
+def inner_kernel(
+    place, steps, act_own, base_own, cond, ya, yb, wide, wide_cond, wide_temporal, token,
+    act, base, term, part1, part2, act2,
+):
     del token
     factors = coefficients(steps[0], steps[1])
     lows, highs = halo_columns(place, ya, yb)
     for r in range(ROWS):
         low, high = lows(r), highs(r)
-        act[r], base[r] = prepare(
-            wide_latent(lat[r], low, high), wide_noise(noise[0, r], low, high), factors
+        x = jnp.concatenate([cells(low[0 : 2 * C]), cells(high[0 : 2 * C])], axis=0)
+        fresh = jnp.concatenate([cells(low[2 * C : 3 * C]), cells(high[2 * C : 3 * C])], axis=0)
+        done, value = prepare(x, fresh, factors)
+        act[r, 0 : 2 * C, :] = done[0 : 2 * C]
+        act[r, 2 * C : (WIDE - 2) * C, :] = act_own[r]
+        act[r, (WIDE - 2) * C :, :] = done[2 * C :]
+        base[r, 0:C, :] = value[0:C]
+        base[r, C : (MID - 1) * C, :] = base_own[r]
+        base[r, (MID - 1) * C :, :] = value[C:]
+        field = wide_cond_row(cond[r], low, high).astype(F32)
+        field = jnp.concatenate([field[CK * i : CK * (i + 1)] for i in range(MID)], axis=1).astype(BF16)
+        term[r] = jnp.dot(wide_cond[0:FF, 0:CK], field, preferred_element_type=F32)
+    for r in range(1, ROWS - 1):
+        free = spatial_sum([(d + 1, pick(act, r + d)) for d in (-1, 0, 1)], FIRST, wide)
+        add_sums(
+            temporal_sum(free, free + cond_pairs(term[r], 0, MID // 2), wide_temporal), base, r, factors[1]
         )
-        condx[r] = wide_cond_row(cond[r], low, high)
-    for r in range(1, ROWS - 1):
-        first_step(
-            [pick(act, r + d) for d in (-1, 0, 1)], condx, r, base, factors[1], (wide, wide_cond, wide_temporal)
-        )
-
-
-def inner(place, steps, lat, noise, cond, ya, yb, weights, token):
+    part1[0] = spatial_sum([(1, pick(act, 0)), (2, pick(act, 1))], FIRST, wide)
+    part1[1] = spatial_sum([(0, pick(act, ROWS - 2)), (1, pick(act, ROWS - 1))], FIRST, wide)
+    part1[2] = spatial_sum([(2, pick(act, 0))], FIRST, wide)
+    part1[3] = spatial_sum([(0, pick(act, ROWS - 1))], FIRST, wide)
+    for i in range(2):
+        act2[i] = next_act(silu(normalize(base[1 + i].reshape(MID, C, NT))), 1 + i, place)
+    one, two = pick(act2, 0), pick(act2, 1)
+    part2[0] = spatial_sum([(2, one)], SECOND, wide)
+    part2[1] = spatial_sum([(1, one), (2, two)], SECOND, wide)
+    part2[2] = spatial_sum([(0, one), (1, two)], SECOND, wide)
+    part2[3] = spatial_sum([(0, two)], SECOND, wide)
+
+
+def inner(place, steps, act, base, cond, ya, yb, weights, token):
     return pl.pallas_call(
         inner_kernel,
         out_shape=(
             jax.ShapeDtypeStruct((ROWS, WIDE * C, NT), BF16),
             jax.ShapeDtypeStruct((ROWS, MID * C, NT), F32),
-            jax.ShapeDtypeStruct((ROWS, MID * CK, NT), BF16),
+            jax.ShapeDtypeStruct((ROWS, FF, MID * NT), F32),
+            jax.ShapeDtypeStruct((4, 2 * FF, MID // 2 * NT), F32),
+            jax.ShapeDtypeStruct((4, 2 * FF, COLS // 2 * NT), F32),
+            jax.ShapeDtypeStruct((2, MID * C, NT), BF16),
         ),
         in_specs=[smem(), smem()] + [vmem()] * 9,
-        out_specs=(vmem(),) * 3,
-        compiler_params=pltpu.CompilerParams(vmem_limit_bytes=24 << 20),
+        out_specs=(vmem(),) * 6,
+        compiler_params=pltpu.CompilerParams(vmem_limit_bytes=VMEM_MOST),
         cost_estimate=pl.CostEstimate(flops=1 << 30, bytes_accessed=4 << 20, transcendentals=2 << 20),
         name="inner_rows",
-    )(place, steps, lat, noise, cond, ya, yb, *weights, token)
+    )(place, steps, act, base, cond, ya, yb, *weights, token)
 
 
 def main_kernel(
-    place, steps, noise, cond, xa, xb, act, base_own, condx_own, wide, wide_cond, wide_temporal,
-    out, outer, base, condx, act2,
+    place, steps, fresh2, xa, xb, act, base_own, term, part1, part2, act2_own, wide, wide_cond, wide_temporal,
+    out, outer, base, act2,
 ):
-    weights = (wide, wide_cond, wide_temporal)
     factors = coefficients(steps[0], steps[1])
     even_x = place[0] == 0
     n = WIDE * C
+    fields = []
     for top in (False, True):
         face = lambda lo, hi: jnp.where(even_x == top, xa[lo:hi, :], xb[lo:hi, :])
         near = 0 if top else 1
@@ -324,80 +419,81 @@
             outer[2 * top + i] = done
             if i == near:
                 base[2 + top] = value
-                condx[2 + top] = face(2 * n + MID * C, XROWS)
+        fields.append(face(2 * n + MID * C, XROWS))
     for i, r in enumerate((0, ROWS - 1)):
         base[i] = base_own[r]
-        condx[i] = condx_own[r]
-
-    halo = {-2: 0, -1: 1, ROWS: 2, ROWS + 1: 3}
-    for r, slot in ((0, 0), (ROWS - 1, 1), (-1, 2), (ROWS, 3)):
-        rows = [pick(outer, halo[r + d]) if r + d in halo else pick(act, r + d) for d in (-1, 0, 1)]
-        first_step(rows, condx, slot, base, factors[1], weights)
+
+    far = (
+        [(0, pick(outer, 1))],
+        [(2, pick(outer, 2))],
+        [(0, pick(outer, 0)), (1, pick(outer, 1))],
+        [(1, pick(outer, 2)), (2, pick(outer, 3))],
+    )
+    for slot in range(4):
+        free = part1[slot] + spatial_sum(far[slot], FIRST, wide)
+        if slot < 2:
+            given = free + cond_pairs(term[(ROWS - 1) * slot], 0, MID // 2)
+        else:
+            field = jnp.concatenate([fields[slot - 2][2 * CK * p : 2 * CK * (p + 1)] for p in FIRST], axis=1)
+            given = free + jnp.dot(wide_cond[...], field, preferred_element_type=F32)
+        add_sums(temporal_sum(free, given, wide_temporal), base, slot, factors[1])
 
     keep2, move2, sigma2 = coefficients(steps[1], steps[2])
-    left = jnp.where(place[3] == 0, 0.0, 1.0)
-    right = jnp.where(place[3] == NGY - 1, 0.0, 1.0)
-    for e in range(6):
-        r = e - 1
-        x = (base_own[r] if 0 < r < ROWS - 1 else base[{0: 0, ROWS - 1: 1, -1: 2, ROWS: 3}[r]]).reshape(MID, C, NT)
+    slots = {0: 0, ROWS - 1: 1, -1: 2, ROWS: 3}
+    for r in range(-1, ROWS + 1):
+        x = (base[slots[r]] if r in slots else base_own[r]).reshape(MID, C, NT)
         normed = normalize(x)
-        value = silu(normed)
-        value = jnp.concatenate([value[0:1] * left, value[1 : MID - 1], value[MID - 1 :] * right], axis=0)
-        if e == 0:
-            value = value * jnp.where(place[2] == 0, 0.0, 1.0)
-        if e == 5:
-            value = value * jnp.where(place[2] == NGX - 1, 0.0, 1.0)
-        act2[e] = value.astype(BF16).reshape(MID * C, NT)
-        if 0 < e < 5:
+        if r in slots:
+            act2[slots[r]] = next_act(silu(normed), r, place)
+        if 0 <= r < ROWS:
             out[r] = (
-                keep2 * x[1 : MID - 1] + move2 * normed[1 : MID - 1] + sigma2 * noise[1, r].astype(F32)
+                keep2 * x[1 : MID - 1] + move2 * normed[1 : MID - 1] + sigma2 * fresh2[r].astype(F32)
             )
 
-    def second(r, carry):
-        sums = block(
-            [pick(act2, r + d) for d in range(3)],
-            lambda p: cond[r, 2 * CK * p : 2 * CK * (p + 1), :],
-            list(range(COLS // 2)),
-            *weights,
-        )
+    near = (
+        [(0, pick(act2, 2)), (1, pick(act2, 0))],
+        [(0, pick(act2, 0))],
+        [(2, pick(act2, 1))],
+        [(1, pick(act2, 1)), (2, pick(act2, 3))],
+    )
+    for r in range(ROWS):
+        free = part2[r] + spatial_sum(near[r], SECOND, wide)
+        sums = temporal_sum(free, free + cond_pairs(term[r], 1, COLS // 2), wide_temporal)
         for i, s in enumerate(sums):
             out[r, i] = out[r, i] + move2 * s
-        return carry
-
-    lax.fori_loop(0, ROWS, second, 0)
-
-
-def sample(place, steps, noise, cond, xa, xb, act, base, condx, weights):
+
+
+def sample(place, steps, fresh2, xa, xb, parts, weights):
     return pl.pallas_call(
         main_kernel,
         out_shape=jax.ShapeDtypeStruct((ROWS, COLS, C, NT), F32),
-        in_specs=[smem(), smem()] + [vmem()] * 10,
+        in_specs=[smem(), smem()] + [vmem()] * 12,
         out_specs=vmem(),
         scratch_shapes=[
             pltpu.VMEM((4, WIDE * C, NT), BF16),
             pltpu.VMEM((4, MID * C, NT), F32),
-            pltpu.VMEM((4, MID * CK, NT), BF16),
-            pltpu.VMEM((6, MID * C, NT), BF16),
+            pltpu.VMEM((4, MID * C, NT), BF16),
         ],
-        compiler_params=pltpu.CompilerParams(vmem_limit_bytes=32 << 20),
+        compiler_params=pltpu.CompilerParams(vmem_limit_bytes=VMEM_MOST),
         cost_estimate=pl.CostEstimate(flops=2 << 30, bytes_accessed=5 << 20, transcendentals=5 << 20),
         name="sample_slab",
-    )(place, steps, noise, cond, xa, xb, act, base, condx, *weights)
+    )(place, steps, fresh2, xa, xb, *parts, *weights)
 
 
 def on_device(latent, sample_noise, cond_field, timesteps, spatial_weight, cond_weight, temporal_weight):
     gx, gy = lax.axis_index("gx"), lax.axis_index("gy")
     place = jnp.stack([gx % 2, gy % 2, gx, gy]).astype(jnp.int32)
     cond = cond_field.reshape(ROWS, COLS * CK, NT)
-    ya, yb = pack_y(place, latent, sample_noise, cond)
+    ya, yb, token = pack_y(place, latent, sample_noise, cond)
     ya = lax.ppermute(ya, AXES, swaps_y(0))
     yb = lax.ppermute(yb, AXES, swaps_y(1))
+    act, base, packed, fresh, fresh2 = own(token, timesteps, latent, sample_noise)
     weights = widen(jnp.swapaxes(spatial_weight, 2, 3), cond_weight.T, temporal_weight)
-    xa, xb, token = pack_x(place, latent, sample_noise, cond, ya, yb)
+    xa, xb, token = pack_x(place, packed, fresh, cond, ya, yb)
     xa = lax.ppermute(xa, AXES, swaps_x(0))
     xb = lax.ppermute(xb, AXES, swaps_x(1))
-    act, base, condx = inner(place, timesteps, latent, sample_noise, cond, ya, yb, weights, token)
-    return sample(place, timesteps, sample_noise, cond, xa, xb, act, base, condx, weights)
+    parts = inner(place, timesteps, act, base, cond, ya, yb, weights, token)
+    return sample(place, timesteps, fresh2, xa, xb, parts, weights)
 
 
 def solution(mesh):

time: 37.6 us -> 39.6 us (1.053)
  local copies, waits for them, and re-layouts: 0.04 us -> 5.37 us
  waiting for transfers between devices: 9.41 us -> 5.66 us
  Pallas kernels: 16 us -> 16.6 us
  starting transfers between devices: 11.2 us -> 10.8 us
    unnamed x16 -> x24, local copies, waits for them, and re-layouts: 0.04 us -> 5.37 us
    ppermute x1, waiting for transfers between devices: 2.74 us -> 0.01 us  [on_device(): yb = lax.ppermute(yb, AXES, swaps_y(1))]
    pallas_call x1, Pallas kernels: 9.73 us -> 7.07 us  [sample(): pl.pallas_call(main_kernel, out_shape=jax.ShapeDtypeStruct((ROWS, COLS, C...]
    pallas_call x1 -> x2, Pallas kernels: 2.56 us -> 4.88 us  [the longest x1 2.56 us: pack_y(): pl.pallas_call(pack_y_kernel, out_shape=(y, y, jax.ShapeDtypeStruct((8, N...]
    ppermute x1, waiting for transfers between devices: 6.67 us -> 5.65 us  [on_device(): xb = lax.ppermute(xb, AXES, swaps_x(1))]
    pallas_call x1, Pallas kernels: 2.8 us -> 3.79 us  [inner(): pl.pallas_call(inner_kernel, out_shape=(jax.ShapeDtypeStruct((ROWS, WIDE...]
  transfers between devices with their start and end apart: 4 -> 4, of which waited for: 2 -> 1; matrix products, arithmetic and copies ran while one was open for 0% -> 0% of each run, Pallas kernels for 8% -> 16%
where the time goes in v3:
time: 39.6 us; the launch traced here: 39.3 us
  Pallas kernels  16.6 us (42%)
  starting transfers between devices  10.8 us (27%)
  waiting for transfers between devices  5.66 us (14%)
  local copies, waits for them, and re-layouts  5.37 us (14%)
  other arithmetic  0.67 us (2%)
    pallas_call x1, Pallas kernels, sample(): pl.pallas_call(main_kernel, out_shape=jax.ShapeDtypeStruct((ROWS, COLS, C...  7.07 us
    ppermute x1, waiting for transfers between devices, on_device(): xb = lax.ppermute(xb, AXES, swaps_x(1))  5.65 us
    ppermute x1, starting transfers between devices, on_device(): yb = lax.ppermute(yb, AXES, swaps_y(1))  5.47 us
    unnamed x24, local copies, waits for them, and re-layouts  5.37 us
    ppermute x1, starting transfers between devices, on_device(): xb = lax.ppermute(xb, AXES, swaps_x(1))  3.94 us
    pallas_call x1, Pallas kernels, inner(): pl.pallas_call(inner_kernel, out_shape=(jax.ShapeDtypeStruct((ROWS, WIDE...  3.79 us
    pallas_call x1, Pallas kernels, pack_y(): pl.pallas_call(pack_y_kernel, out_shape=(y, y, jax.ShapeDtypeStruct((8, N...  2.56 us
    pallas_call x1, Pallas kernels, own(): pl.pallas_call(own_kernel, out_shape=(jax.ShapeDtypeStruct((ROWS, n, NT),...  2.32 us
  transfers between devices with their start and end apart: 4, of which 1 were waited for; matrix products, arithmetic and copies ran while one was open for 0% of the time, Pallas kernels for 16%

profile of v3, /device:TPU:121, one launch (start us, length us, event | category | flops | bytes accessed | tf_op | source)
XLA Modules:
  0.0 39.3 jit_solution(1141773510097405227)
XLA Ops:
  0.0 0.0 copy-start.3
  0.0 0.0 copy-start.10
  0.0 0.0 copy-start.5
  0.0 0.0 copy-start.11
  0.0 0.0 copy-start.4
  0.0 0.7 %pad_add_fusion.place = s32[4]{0:T(128)} fusion(s32[1]{0:T(128)} %bitcast.3, s32[1]{0:T(128)} %bitcast.2, s32[1]{0:T(128)} %bitcast.1, s32[1]{0:T(128)} %bitcast), kind=kLoop, calls=%fused_computation | loop fusion | flops 12 | bytes 32 | tf_op jit(solution)/shard_map/stack | solution.py:485
  0.7 0.0 copy-start.7
  0.7 2.6 %pack_columns.1 = (bf16[4,112,128]{2,1,0:T(8,128)(2,1)}, bf16[4,112,128]{2,1,0:T(8,128)(2,1)}, f32[8,128]{1,0:T(8,128)}) custom-call(s32[4]{0:T(128)} %pad_add_fusion.place, f32[4,16,32,128]{3,2,1,0:T(8,128)} %lat.3, bf16[2,4,16,32,128]{4,3,2,1,0:T(8,128)(2,1)} %noise.3, bf16[4,128,128]{2,1,0:T(8,128)(2,1)} %bitcast.7), custom_call_target="tpu_custom_call" | custom-call | flops 65536 | bytes 524288 | tf_op jit(solution)/shard_map/pack_columns/pallas_call | solution.py:97
  3.3 0.1 collective-permute-start
  3.4 5.5 %collective-permute-start.1 = (bf16[4,112,128]{2,1,0:T(8,128)(2,1)}, bf16[4,112,128]{2,1,0:T(8,128)(2,1)S(1)}, u32[]{:S(2)}, u32[]{:S(2)}) collective-permute-start(bf16[4,112,128]{2,1,0:T(8,128)(2,1)} %get-tuple-element.30), channel_id=1, source_target_pairs={{1,2},{2,1},{3,4},{4,3},{5,6},{6,5},{9,10},{10,9},{11,12},{12,11},... | collective-permute-start | bytes 344072 | tf_op jit(solution)/shard_map/ppermute | solution.py:489
  8.9 0.0 copy-start
  8.9 1.2 %copy-done = f32[4,16,32,128]{3,2,1,0:T(8,128)S(1)} copy-done((f32[4,16,32,128]{3,2,1,0:T(8,128)S(1)}, f32[4,16,32,128]{3,2,1,0:T(8,128)}, u32[]{:S(2)}) %copy-start) | copy-done | bytes 1048600
  10.1 0.0 copy-start.1
  10.1 1.2 %copy-done.1 = bf16[2,4,16,32,128]{4,3,2,1,0:T(8,128)(2,1)S(1)} copy-done((bf16[2,4,16,32,128]{4,3,2,1,0:T(8,128)(2,1)S(1)}, bf16[2,4,16,32,128]{4,3,2,1,0:T(8,128)(2,1)}, u32[]{:S(2)}) %copy-start.1) | copy-done | bytes 1048600
  11.3 0.0 copy-start.8
  11.3 0.7 %copy-done.8 = f32[8,128]{1,0:T(8,128)S(1)} copy-done((f32[8,128]{1,0:T(8,128)S(1)}, f32[8,128]{1,0:T(8,128)}, u32[]{:S(2)}) %copy-start.8) | copy-done | bytes 4120
  12.0 0.0 copy-start.9
  12.0 0.7 %copy-done.9 = s32[3]{0:T(128)S(1)} copy-done((s32[3]{0:T(128)S(1)}, s32[3]{0:T(128)}, u32[]{:S(2)}) %copy-start.9) | copy-done | bytes 36
  12.6 2.3 %own_cells.1 = (bf16[4,512,128]{2,1,0:T(8,128)(2,1)S(1)}, f32[4,512,128]{2,1,0:T(8,128)S(1)}, bf16[4,512,128]{2,1,0:T(8,128)(2,1)S(1)}, bf16[4,16,32,128]{3,2,1,0:T(8,128)(2,1)S(1)}, bf16[4,16,32,128]{3,2,1,0:T(8,128)(2,1)S(1)}) custom-call(f32[8,128]{1,0:T(8,128)S(1)} %copy-done.8, s32[3]{0:T(128)S(1)} %copy-done.9, f32[4,16,32,128]{3,2,1,0:T(8,128)S(1)} %copy-done, ...), custom_call_target="tpu_custom_call" | custom-call | flops 16777216 | bytes 4194304 | tf_op jit(solution)/shard_map/own_cells/pallas_call | solution.py:150
  15.0 0.0 collective-permute-done.ya
  15.0 0.0 collective-permute-done.1.yb
  15.0 0.0 copy-start.2
  15.0 0.9 %copy-done.2 = bf16[4,16,8,128]{3,2,1,0:T(8,128)(2,1)S(1)} copy-done((bf16[4,16,8,128]{3,2,1,0:T(8,128)(2,1)S(1)}, bf16[4,16,8,128]{3,2,1,0:T(8,128)(2,1)}, u32[]{:S(2)}) %copy-start.2) | copy-done | bytes 131096
  15.9 0.0 copy-start.6
  15.9 0.7 %copy-done.6 = s32[4]{0:T(128)S(1)} copy-done((s32[4]{0:T(128)S(1)}, s32[4]{0:T(128)}, u32[]{:S(2)}) %copy-start.6) | copy-done | bytes 40
  16.6 0.6 %pack_rows.1 = (bf16[2000,128]{1,0:T(8,128)(2,1)S(1)}, bf16[2000,128]{1,0:T(8,128)(2,1)S(1)}, f32[8,128]{1,0:T(8,128)S(1)}) custom-call(s32[4]{0:T(128)S(1)} %copy-done.6, bf16[4,512,128]{2,1,0:T(8,128)(2,1)S(1)} %get-tuple-element.27.packed, bf16[4,16,32,128]{3,2,1,0:T(8,128)(2,1)S(1)} %get-tuple-element.28.fresh, bf16[4,128,128]{2,1,0:T(8,128)(2,1)S(1)} %bitcast.8, ...), custom_call_target="tpu_custom_call" | custom-call | flops 262144 | bytes 3145728 | tf_op jit(solution)/shard_map/pack_rows/pallas_call | solution.py:207
  17.2 1.3 %collective-permute-start.2 = (bf16[2000,128]{1,0:T(8,128)(2,1)S(1)}, bf16[2000,128]{1,0:T(8,128)(2,1)S(1)}, u32[]{:S(2)}, u32[]{:S(2)}) collective-permute-start(bf16[2000,128]{1,0:T(8,128)(2,1)S(1)} %get-tuple-element.31), channel_id=1, source_target_pairs={{0,8},{8,0},{16,24},{24,16},{32,40},{40,32},{48,56},{56,48},{64,72... | collective-permute-start | bytes 1536008 | tf_op jit(solution)/shard_map/ppermute | solution.py:493
  18.6 3.9 %collective-permute-start.3 = (bf16[2000,128]{1,0:T(8,128)(2,1)S(1)}, bf16[2000,128]{1,0:T(8,128)(2,1)S(1)}, u32[]{:S(2)}, u32[]{:S(2)}) collective-permute-start(bf16[2000,128]{1,0:T(8,128)(2,1)S(1)} %get-tuple-element.32), channel_id=1, source_target_pairs={{8,16},{16,8},{24,32},{32,24},{40,48},{48,40},{56,192},{192,56},{7... | collective-permute-start | bytes 1536008 | tf_op jit(solution)/shard_map/ppermute | solution.py:494
  22.5 0.0 copy-done.5
  22.5 0.0 copy-done.11
  22.5 0.0 copy-done.4
  22.5 0.2 widen_weights.1
  22.7 0.0 copy-done.3
  22.8 0.0 copy-done.10
  22.8 0.0 copy-done.7
  22.8 3.8 %inner_rows.1 = (bf16[4,640,128]{2,1,0:T(8,128)(2,1)S(1)}, f32[4,576,128]{2,1,0:T(8,128)S(1)}, f32[4,128,2304]{2,1,0:T(8,128)S(1)}, f32[4,256,1152]{2,1,0:T(8,12...) custom-call(s32[4]{0:T(128)S(1)} %copy-done.7, s32[3]{0:T(128)S(1)} %copy-done.10, ...), custom_call_target="tpu_custom_call" | custom-call | flops 1073741824 | bytes 4194304 | tf_op jit(solution)/shard_map/inner_rows/pallas_call | solution.py:387
  26.6 0.0 collective-permute-done.2.xa
  26.6 5.7 %collective-permute-done.3.xb = bf16[2000,128]{1,0:T(8,128)(2,1)S(1)} collective-permute-done((bf16[2000,128]{1,0:T(8,128)(2,1)S(1)}, bf16[2000,128]{1,0:T(8,128)(2,1)S(1)}, u32[]{:S(2)}, u32[]{:S(2)}) %collective-permute-start.3) | collective-permute-done | bytes 512032 | tf_op jit(solution)/shard_map/ppermute | solution.py:494
  32.2 7.1 %sample_slab.1 = f32[4,16,32,128]{3,2,1,0:T(8,128)} custom-call(s32[4]{0:T(128)S(1)} %copy-done.7, s32[3]{0:T(128)S(1)} %copy-done.10, bf16[4,16,32,128]{3,2,1,0:T(8,128)(2,1)S(1)} %get-tuple-element.26.fresh2, bf16[2000,128]{1,0:T(8,128)(2,1)S(1)} %collective-permute-done.2.xa, bf16[2000,128]{1,0:T(8,128)(2,1)S(1)} %collective-permute-done.3.xb, ...), custom_call_target="tpu_custom_call" | custom-call | flops 2147483648 | bytes 5242880 | tf_op jit(solution)/shard_map/sample_slab/pallas_call | solution.py:467
Async XLA Ops:
  0.0 22.7 %copy-start.3 = (bf16[4,16,8,128]{3,2,1,0:T(8,128)(2,1)S(1)}, bf16[4,16,8,128]{3,2,1,0:T(8,128)(2,1)}, u32[]{:S(2)}) copy-start(bf16[4,16,8,128]{3,2,1,0:T(8,128)(2,1)} %param.9) | copy-start | bytes 393220
  0.0 22.8 %copy-start.10 = (s32[3]{0:T(128)S(1)}, s32[3]{0:T(128)}, u32[]{:S(2)}) copy-start(s32[3]{0:T(128)} %steps.5) | copy-start | bytes 40
  0.0 22.5 %copy-start.5 = (bf16[3,32,128]{2,1,0:T(8,128)(2,1)S(1)}, bf16[3,32,128]{2,1,0:T(8,128)(2,1)}, u32[]{:S(2)}) copy-start(bf16[3,32,128]{2,1,0:T(8,128)(2,1)} %temporal.1) | copy-start | bytes 73732
  0.0 22.5 %copy-start.11 = (bf16[128,8]{0,1:T(8,128)(2,1)S(1)}, bf16[128,8]{0,1:T(8,128)(2,1)}, u32[]{:S(2)}) copy-start(bf16[128,8]{0,1:T(8,128)(2,1)} %param.12) | copy-start | bytes 6148
  0.0 22.5 %copy-start.4 = (bf16[3,3,128,32]{2,3,1,0:T(8,128)(2,1)S(1)}, bf16[3,3,128,32]{2,3,1,0:T(8,128)(2,1)}, u32[]{:S(2)}) copy-start(bf16[3,3,128,32]{2,3,1,0:T(8,128)(2,1)} %param.11) | copy-start | bytes 221188
  0.7 22.1 %copy-start.7 = (s32[4]{0:T(128)S(1)}, s32[4]{0:T(128)}, u32[]{:S(2)}) copy-start(s32[4]{0:T(128)} %pad_add_fusion.place) | copy-start | bytes 52
  3.3 11.7 %collective-permute-start = (bf16[4,112,128]{2,1,0:T(8,128)(2,1)}, bf16[4,112,128]{2,1,0:T(8,128)(2,1)S(1)}, u32[]{:S(2)}, u32[]{:S(2)}) collective-permute-start(bf16[4,112,128]{2,1,0:T(8,128)(2,1)} %get-tuple-element.29), channel_id=1, source_target_pairs={{0,1},{1,0},{2,3},{3,2},{4,5},{5,4},{6,7},{7,6},{8,9},{9,8},{10,11... | collective-permute-start | bytes 344072 | tf_op jit(solution)/shard_map/ppermute | solution.py:488
  3.4 11.6 %collective-permute-start.1 = (bf16[4,112,128]{2,1,0:T(8,128)(2,1)}, bf16[4,112,128]{2,1,0:T(8,128)(2,1)S(1)}, u32[]{:S(2)}, u32[]{:S(2)}) collective-permute-start(bf16[4,112,128]{2,1,0:T(8,128)(2,1)} %get-tuple-element.30), channel_id=1, source_target_pairs={{1,2},{2,1},{3,4},{4,3},{5,6},{6,5},{9,10},{10,9},{11,12},{12,11},... | collective-permute-start | bytes 344072 | tf_op jit(solution)/shard_map/ppermute | solution.py:489
  8.9 1.2 %copy-start = (f32[4,16,32,128]{3,2,1,0:T(8,128)S(1)}, f32[4,16,32,128]{3,2,1,0:T(8,128)}, u32[]{:S(2)}) copy-start(f32[4,16,32,128]{3,2,1,0:T(8,128)} %lat.3) | copy-start | bytes 3145732
  10.1 1.2 %copy-start.1 = (bf16[2,4,16,32,128]{4,3,2,1,0:T(8,128)(2,1)S(1)}, bf16[2,4,16,32,128]{4,3,2,1,0:T(8,128)(2,1)}, u32[]{:S(2)}) copy-start(bf16[2,4,16,32,128]{4,3,2,1,0:T(8,128)(2,1)} %noise.3) | copy-start | bytes 3145732
  11.3 0.7 %copy-start.8 = (f32[8,128]{1,0:T(8,128)S(1)}, f32[8,128]{1,0:T(8,128)}, u32[]{:S(2)}) copy-start(f32[8,128]{1,0:T(8,128)} %get-tuple-element.25.token) | copy-start | bytes 12292
  12.0 0.7 %copy-start.9 = (s32[3]{0:T(128)S(1)}, s32[3]{0:T(128)}, u32[]{:S(2)}) copy-start(s32[3]{0:T(128)} %steps.5) | copy-start | bytes 40
  15.0 0.9 %copy-start.2 = (bf16[4,16,8,128]{3,2,1,0:T(8,128)(2,1)S(1)}, bf16[4,16,8,128]{3,2,1,0:T(8,128)(2,1)}, u32[]{:S(2)}) copy-start(bf16[4,16,8,128]{3,2,1,0:T(8,128)(2,1)} %param.9) | copy-start | bytes 393220
  15.9 0.7 %copy-start.6 = (s32[4]{0:T(128)S(1)}, s32[4]{0:T(128)}, u32[]{:S(2)}) copy-start(s32[4]{0:T(128)} %pad_add_fusion.place) | copy-start | bytes 52
  17.2 9.3 %collective-permute-start.2 = (bf16[2000,128]{1,0:T(8,128)(2,1)S(1)}, bf16[2000,128]{1,0:T(8,128)(2,1)S(1)}, u32[]{:S(2)}, u32[]{:S(2)}) collective-permute-start(bf16[2000,128]{1,0:T(8,128)(2,1)S(1)} %get-tuple-element.31), channel_id=1, source_target_pairs={{0,8},{8,0},{16,24},{24,16},{32,40},{40,32},{48,56},{56,48},{64,72... | collective-permute-start | bytes 1536008 | tf_op jit(solution)/shard_map/ppermute | solution.py:493
  18.6 13.7 %collective-permute-start.3 = (bf16[2000,128]{1,0:T(8,128)(2,1)S(1)}, bf16[2000,128]{1,0:T(8,128)(2,1)S(1)}, u32[]{:S(2)}, u32[]{:S(2)}) collective-permute-start(bf16[2000,128]{1,0:T(8,128)(2,1)S(1)} %get-tuple-element.32), channel_id=1, source_target_pairs={{8,16},{16,8},{24,32},{32,24},{40,48},{48,40},{56,192},{192,56},{7... | collective-permute-start | bytes 1536008 | tf_op jit(solution)/shard_map/ppermute | solution.py:494

commit v4 on v3

--- a/solution.py
+++ b/solution.py
@@ -7,7 +7,7 @@
 
 F32 = jnp.float32
 BF16 = jnp.bfloat16
-VMEM_ALL = 60 << 20
+VMEM_ALL = 52 << 20
 VMEM_MOST = 34 << 20
 AXES = ("cfg", "gx", "gy")
 NCFG, NGX, NGY = 2, 16, 8
@@ -119,30 +119,13 @@
     )
 
 
-def own_kernel(
-    token, steps, lat, noise, act, base, packed, fresh, fresh2, xs, lat_sems, noise_sems, later_sem
-):
+def own_kernel(token, steps, lat, noise, act, base, packed):
     del token
-    loads = []
-    for r in range(ROWS):
-        loads.append(
-            (
-                pltpu.make_async_copy(lat.at[r], xs.at[r], lat_sems.at[r]),
-                pltpu.make_async_copy(noise.at[0, r], fresh.at[r], noise_sems.at[r]),
-            )
-        )
-        for load in loads[-1]:
-            load.start()
-    later = pltpu.make_async_copy(noise.at[1], fresh2, later_sem)
-    later.start()
     factors = coefficients(steps[0], steps[1])
     for r in range(ROWS):
-        for load in loads[r]:
-            load.wait()
-        x = xs[r]
+        x = lat[r]
         packed[r] = x.astype(BF16).reshape(COLS * C, NT)
-        act[r], base[r] = prepare(x, fresh[r], factors)
-    later.wait()
+        act[r], base[r] = prepare(x, noise[0, r], factors)
 
 
 def own(token, steps, lat, noise):
@@ -153,18 +136,10 @@
             jax.ShapeDtypeStruct((ROWS, n, NT), BF16),
             jax.ShapeDtypeStruct((ROWS, n, NT), F32),
             jax.ShapeDtypeStruct((ROWS, n, NT), BF16),
-            jax.ShapeDtypeStruct((ROWS, COLS, C, NT), BF16),
-            jax.ShapeDtypeStruct((ROWS, COLS, C, NT), BF16),
         ),
-        in_specs=[vmem(), smem(), any_space(), any_space()],
-        out_specs=(vmem(),) * 5,
-        scratch_shapes=[
-            pltpu.VMEM((ROWS, COLS, C, NT), F32),
-            pltpu.SemaphoreType.DMA((ROWS,)),
-            pltpu.SemaphoreType.DMA((ROWS,)),
-            pltpu.SemaphoreType.DMA,
-        ],
-        compiler_params=pltpu.CompilerParams(vmem_limit_bytes=VMEM_MOST),
+        in_specs=[vmem(), smem(), vmem(), vmem()],
+        out_specs=(vmem(),) * 3,
+        compiler_params=pltpu.CompilerParams(vmem_limit_bytes=24 << 20),
         cost_estimate=pl.CostEstimate(flops=1 << 24, bytes_accessed=4 << 20, transcendentals=1 << 18),
         name="own_cells",
     )(token, steps, lat, noise)
@@ -174,7 +149,7 @@
     return join16(low.astype(F32)[3 * C : 3 * C + CK], cond_row, high.astype(F32)[3 * C : 3 * C + CK])
 
 
-def pack_x_kernel(place, packed, fresh, cond, ya, yb, xa, xb, token):
+def pack_x_kernel(place, packed, noise, cond, ya, yb, xa, xb, token):
     lows, highs = halo_columns(place, ya, yb)
 
     def pack_x(out, top):
@@ -188,7 +163,7 @@
             if lo + i == inner:
                 at, end = 2 * n, 2 * n + MID * C
                 out[at : at + C, :] = low[2 * C : 3 * C]
-                out[at + C : end - C, :] = fresh[inner].reshape(COLS * C, NT)
+                out[at + C : end - C, :] = noise[0, inner].reshape(COLS * C, NT)
                 out[end - C : end, :] = high[2 * C : 3 * C]
                 out[end:, :] = wide_cond_row(cond[inner], low, high)
 
@@ -202,7 +177,7 @@
     token[...] = jnp.zeros(token.shape, F32)
 
 
-def pack_x(place, packed, fresh, cond, ya, yb):
+def pack_x(place, packed, noise, cond, ya, yb):
     x = jax.ShapeDtypeStruct((XROWS, NT), BF16)
     return pl.pallas_call(
         pack_x_kernel,
@@ -212,7 +187,7 @@
         compiler_params=pltpu.CompilerParams(vmem_limit_bytes=24 << 20),
         cost_estimate=pl.CostEstimate(flops=1 << 18, bytes_accessed=3 << 20, transcendentals=0),
         name="pack_rows",
-    )(place, packed, fresh, cond, ya, yb)
+    )(place, packed, noise, cond, ya, yb)
 
 
 def weights_kernel(spatial, cond, temporal, wide, wide_cond, wide_temporal):
@@ -403,7 +378,7 @@
 
 
 def main_kernel(
-    place, steps, fresh2, xa, xb, act, base_own, term, part1, part2, act2_own, wide, wide_cond, wide_temporal,
+    place, steps, noise, xa, xb, act, base_own, term, part1, part2, act2_own, wide, wide_cond, wide_temporal,
     out, outer, base, act2,
 ):
     factors = coefficients(steps[0], steps[1])
@@ -447,7 +422,7 @@
             act2[slots[r]] = next_act(silu(normed), r, place)
         if 0 <= r < ROWS:
             out[r] = (
-                keep2 * x[1 : MID - 1] + move2 * normed[1 : MID - 1] + sigma2 * fresh2[r].astype(F32)
+                keep2 * x[1 : MID - 1] + move2 * normed[1 : MID - 1] + sigma2 * noise[1, r].astype(F32)
             )
 
     near = (
@@ -463,7 +438,7 @@
             out[r, i] = out[r, i] + move2 * s
 
 
-def sample(place, steps, fresh2, xa, xb, parts, weights):
+def sample(place, steps, noise, xa, xb, parts, weights):
     return pl.pallas_call(
         main_kernel,
         out_shape=jax.ShapeDtypeStruct((ROWS, COLS, C, NT), F32),
@@ -477,7 +452,7 @@
         compiler_params=pltpu.CompilerParams(vmem_limit_bytes=VMEM_MOST),
         cost_estimate=pl.CostEstimate(flops=2 << 30, bytes_accessed=5 << 20, transcendentals=5 << 20),
         name="sample_slab",
-    )(place, steps, fresh2, xa, xb, *parts, *weights)
+    )(place, steps, noise, xa, xb, *parts, *weights)
 
 
 def on_device(latent, sample_noise, cond_field, timesteps, spatial_weight, cond_weight, temporal_weight):
@@ -487,13 +462,13 @@
     ya, yb, token = pack_y(place, latent, sample_noise, cond)
     ya = lax.ppermute(ya, AXES, swaps_y(0))
     yb = lax.ppermute(yb, AXES, swaps_y(1))
-    act, base, packed, fresh, fresh2 = own(token, timesteps, latent, sample_noise)
+    act, base, packed = own(token, timesteps, latent, sample_noise)
     weights = widen(jnp.swapaxes(spatial_weight, 2, 3), cond_weight.T, temporal_weight)
-    xa, xb, token = pack_x(place, packed, fresh, cond, ya, yb)
+    xa, xb, token = pack_x(place, packed, sample_noise, cond, ya, yb)
     xa = lax.ppermute(xa, AXES, swaps_x(0))
     xb = lax.ppermute(xb, AXES, swaps_x(1))
     parts = inner(place, timesteps, act, base, cond, ya, yb, weights, token)
-    return sample(place, timesteps, fresh2, xa, xb, parts, weights)
+    return sample(place, timesteps, sample_noise, xa, xb, parts, weights)
 
 
 def solution(mesh):

time: 39.6 us -> 35.4 us (0.89)
  Pallas kernels: 16.6 us -> 14.3 us
  local copies, waits for them, and re-layouts: 5.37 us -> 4.1 us
  other arithmetic: 0.67 us -> 0.08 us
    unnamed x24 -> x20, local copies, waits for them, and re-layouts: 5.37 us -> 4.1 us
    pallas_call x1, Pallas kernels: 2.56 us -> 1.47 us  [pack_y(): pl.pallas_call(pack_y_kernel, out_shape=(y, y, jax.ShapeDtypeStruct((8, N...]
    pallas_call x1, Pallas kernels: 2.32 us -> 1.27 us  [own(): pl.pallas_call(own_kernel, out_shape=(jax.ShapeDtypeStruct((ROWS, n, NT),...]
    another operation x1, other arithmetic: 0.67 us -> 0.08 us  [on_device(): place = jnp.stack([gx % 2, gy % 2, gx, gy]).astype(jnp.int32)]
  transfers between devices with their start and end apart: 4 -> 4, of which waited for: 1 -> 1; matrix products, arithmetic and copies ran while one was open for 0% -> 0% of each run, Pallas kernels for 16% -> 15%
where the time goes in v4:
time: 35.4 us; the launch traced here: 35.2 us
  Pallas kernels  14.3 us (40%)
  starting transfers between devices  10.8 us (31%)
  waiting for transfers between devices  5.67 us (16%)
  local copies, waits for them, and re-layouts  4.1 us (12%)
    pallas_call x1, Pallas kernels, sample(): pl.pallas_call(main_kernel, out_shape=jax.ShapeDtypeStruct((ROWS, COLS, C...  6.97 us
    ppermute x1, waiting for transfers between devices, on_device(): xb = lax.ppermute(xb, AXES, swaps_x(1))  5.66 us
    ppermute x1, starting transfers between devices, on_device(): yb = lax.ppermute(yb, AXES, swaps_y(1))  5.47 us
    unnamed x20, local copies, waits for them, and re-layouts  4.1 us
    ppermute x1, starting transfers between devices, on_device(): xb = lax.ppermute(xb, AXES, swaps_x(1))  3.94 us
    pallas_call x1, Pallas kernels, inner(): pl.pallas_call(inner_kernel, out_shape=(jax.ShapeDtypeStruct((ROWS, WIDE...  3.8 us
    pallas_call x1, Pallas kernels, pack_y(): pl.pallas_call(pack_y_kernel, out_shape=(y, y, jax.ShapeDtypeStruct((8, N...  1.47 us
    ppermute x1, starting transfers between devices, on_device(): xa = lax.ppermute(xa, AXES, swaps_x(0))  1.32 us
  transfers between devices with their start and end apart: 4, of which 1 were waited for; matrix products, arithmetic and copies ran while one was open for 0% of the time, Pallas kernels for 15%

profile of v4, /device:TPU:121, one launch (start us, length us, event | category | flops | bytes accessed | tf_op | source)
XLA Modules:
  0.0 35.2 jit_solution(12398527469737169627)
XLA Ops:
  0.0 0.0 copy-start.1
  0.0 0.1 pad_add_fusion.place
  0.1 0.0 copy-start.2
  0.1 1.3 %copy-done.2 = f32[4,16,32,128]{3,2,1,0:T(8,128)S(1)} copy-done((f32[4,16,32,128]{3,2,1,0:T(8,128)S(1)}, f32[4,16,32,128]{3,2,1,0:T(8,128)}, u32[]{:S(2)}) %copy-start.2) | copy-done | bytes 1048600
  1.4 0.0 copy-start.3
  1.4 0.9 %copy-done.3 = bf16[4,16,8,128]{3,2,1,0:T(8,128)(2,1)S(1)} copy-done((bf16[4,16,8,128]{3,2,1,0:T(8,128)(2,1)S(1)}, bf16[4,16,8,128]{3,2,1,0:T(8,128)(2,1)}, u32[]{:S(2)}) %copy-start.3) | copy-done | bytes 131096
  2.3 0.0 copy-start.5
  2.3 0.0 copy-start.6
  2.3 0.0 copy-start.9
  2.3 0.0 copy-start.4
  2.3 0.0 copy-start.8
  2.3 1.5 %pack_columns.1 = (bf16[4,112,128]{2,1,0:T(8,128)(2,1)S(1)}, bf16[4,112,128]{2,1,0:T(8,128)(2,1)S(1)}, f32[8,128]{1,0:T(8,128)S(1)}) custom-call(s32[4]{0:T(128)S(1)} %pad_add_fusion.place, f32[4,16,32,128]{3,2,1,0:T(8,128)S(1)} %copy-done.2, bf16[2,4,16,32,128]{4,3,2,1,0:T(8,128)(2,1)} %noise.7, bf16[4,128,128]{2,1,0:T(8,128)(2,1)S(1)} %bitcast.7), custom_call_target="tpu_custom_call" | custom-call | flops 65536 | bytes 524288 | tf_op jit(solution)/shard_map/pack_columns/pallas_call | solution.py:97
  3.8 0.1 collective-permute-start
  3.9 5.5 %collective-permute-start.1 = (bf16[4,112,128]{2,1,0:T(8,128)(2,1)S(1)}, bf16[4,112,128]{2,1,0:T(8,128)(2,1)S(1)}, u32[]{:S(2)}, u32[]{:S(2)}) collective-permute-start(bf16[4,112,128]{2,1,0:T(8,128)(2,1)S(1)} %get-tuple-element.26), channel_id=1, source_target_pairs={{1,2},{2,1},{3,4},{4,3},{5,6},{6,5},{9,10},{10,9},{11,12},{12,11},... | collective-permute-start | bytes 344072 | tf_op jit(solution)/shard_map/ppermute | solution.py:464
  9.4 0.0 copy-start
  9.4 1.2 %copy-done = bf16[2,4,16,32,128]{4,3,2,1,0:T(8,128)(2,1)S(1)} copy-done((bf16[2,4,16,32,128]{4,3,2,1,0:T(8,128)(2,1)S(1)}, bf16[2,4,16,32,128]{4,3,2,1,0:T(8,128)(2,1)}, u32[]{:S(2)}) %copy-start) | copy-done | bytes 1048600
  10.6 0.0 copy-start.7
  10.6 0.7 %copy-done.7 = s32[3]{0:T(128)S(1)} copy-done((s32[3]{0:T(128)S(1)}, s32[3]{0:T(128)}, u32[]{:S(2)}) %copy-start.7) | copy-done | bytes 36
  11.2 1.3 %own_cells.1 = (bf16[4,512,128]{2,1,0:T(8,128)(2,1)S(1)}, f32[4,512,128]{2,1,0:T(8,128)S(1)}, bf16[4,512,128]{2,1,0:T(8,128)(2,1)S(1)}) custom-call(f32[8,128]{1,0:T(8,128)S(1)} %get-tuple-element.23.token, s32[3]{0:T(128)S(1)} %copy-done.7, f32[4,16,32,128]{3,2,1,0:T(8,128)S(1)} %copy-done.2, bf16[2,4,16,32,128]{4,3,2,1,0:T(8,128)(2,1)S(1)} %copy-done), custom_call_target="tpu_custom_call" | custom-call | flops 16777216 | bytes 4194304 | tf_op jit(solution)/shard_map/own_cells/pallas_call | solution.py:133
  12.5 0.0 collective-permute-done.ya
  12.5 0.0 collective-permute-done.1.yb
  12.5 0.0 copy-done.1
  12.5 0.6 %pack_rows.1 = (bf16[2000,128]{1,0:T(8,128)(2,1)S(1)}, bf16[2000,128]{1,0:T(8,128)(2,1)S(1)}, f32[8,128]{1,0:T(8,128)S(1)}) custom-call(s32[4]{0:T(128)S(1)} %pad_add_fusion.place, bf16[4,512,128]{2,1,0:T(8,128)(2,1)S(1)} %get-tuple-element.24.packed, bf16[2,4,16,32,128]{4,3,2,1,0:T(8,128)(2,1)S(1)} %copy-done.1, bf16[4,128,128]{2,1,0:T(8,128)(2,1)S(1)} %bitcast.8, ...), custom_call_target="tpu_custom_call" | custom-call | flops 262144 | bytes 3145728 | tf_op jit(solution)/shard_map/pack_rows/pallas_call | solution.py:182
  13.2 1.3 %collective-permute-start.2 = (bf16[2000,128]{1,0:T(8,128)(2,1)S(1)}, bf16[2000,128]{1,0:T(8,128)(2,1)S(1)}, u32[]{:S(2)}, u32[]{:S(2)}) collective-permute-start(bf16[2000,128]{1,0:T(8,128)(2,1)S(1)} %get-tuple-element.27), channel_id=1, source_target_pairs={{0,8},{8,0},{16,24},{24,16},{32,40},{40,32},{48,56},{56,48},{64,72... | collective-permute-start | bytes 1536008 | tf_op jit(solution)/shard_map/ppermute | solution.py:468
  14.5 3.9 %collective-permute-start.3 = (bf16[2000,128]{1,0:T(8,128)(2,1)S(1)}, bf16[2000,128]{1,0:T(8,128)(2,1)S(1)}, u32[]{:S(2)}, u32[]{:S(2)}) collective-permute-start(bf16[2000,128]{1,0:T(8,128)(2,1)S(1)} %get-tuple-element.28), channel_id=1, source_target_pairs={{8,16},{16,8},{24,32},{32,24},{40,48},{48,40},{56,192},{192,56},{7... | collective-permute-start | bytes 1536008 | tf_op jit(solution)/shard_map/ppermute | solution.py:469
  18.5 0.0 copy-done.5
  18.5 0.0 copy-done.6
  18.5 0.0 copy-done.9
  18.5 0.2 widen_weights.1
  18.7 0.0 copy-done.4
  18.7 0.0 copy-done.8
  18.7 3.8 %inner_rows.1 = (bf16[4,640,128]{2,1,0:T(8,128)(2,1)S(1)}, f32[4,576,128]{2,1,0:T(8,128)S(1)}, f32[4,128,2304]{2,1,0:T(8,128)S(1)}, f32[4,256,1152]{2,1,0:T(8,12...) custom-call(s32[4]{0:T(128)S(1)} %pad_add_fusion.place, s32[3]{0:T(128)S(1)} %copy-done.8, ...), custom_call_target="tpu_custom_call" | custom-call | flops 1073741824 | bytes 4194304 | tf_op jit(solution)/shard_map/inner_rows/pallas_call | solution.py:362
  22.5 0.0 collective-permute-done.2.xa
  22.5 5.7 %collective-permute-done.3.xb = bf16[2000,128]{1,0:T(8,128)(2,1)S(1)} collective-permute-done((bf16[2000,128]{1,0:T(8,128)(2,1)S(1)}, bf16[2000,128]{1,0:T(8,128)(2,1)S(1)}, u32[]{:S(2)}, u32[]{:S(2)}) %collective-permute-start.3) | collective-permute-done | bytes 512032 | tf_op jit(solution)/shard_map/ppermute | solution.py:469
  28.2 7.0 %sample_slab.1 = f32[4,16,32,128]{3,2,1,0:T(8,128)} custom-call(s32[4]{0:T(128)S(1)} %pad_add_fusion.place, s32[3]{0:T(128)S(1)} %copy-done.8, bf16[2,4,16,32,128]{4,3,2,1,0:T(8,128)(2,1)S(1)} %copy-done.1, bf16[2000,128]{1,0:T(8,128)(2,1)S(1)} %collective-permute-done.2.xa, bf16[2000,128]{1,0:T(8,128)(2,1)S(1)} %collective-permute-done.3.xb, ...), custom_call_target="tpu_custom_call" | custom-call | flops 2147483648 | bytes 5242880 | tf_op jit(solution)/shard_map/sample_slab/pallas_call | solution.py:442
Async XLA Ops:
  0.0 12.5 %copy-start.1 = (bf16[2,4,16,32,128]{4,3,2,1,0:T(8,128)(2,1)S(1)}, bf16[2,4,16,32,128]{4,3,2,1,0:T(8,128)(2,1)}, u32[]{:S(2)}) copy-start(bf16[2,4,16,32,128]{4,3,2,1,0:T(8,128)(2,1)} %noise.7) | copy-start | bytes 3145732
  0.1 1.3 %copy-start.2 = (f32[4,16,32,128]{3,2,1,0:T(8,128)S(1)}, f32[4,16,32,128]{3,2,1,0:T(8,128)}, u32[]{:S(2)}) copy-start(f32[4,16,32,128]{3,2,1,0:T(8,128)} %lat.3) | copy-start | bytes 3145732
  1.4 0.9 %copy-start.3 = (bf16[4,16,8,128]{3,2,1,0:T(8,128)(2,1)S(1)}, bf16[4,16,8,128]{3,2,1,0:T(8,128)(2,1)}, u32[]{:S(2)}) copy-start(bf16[4,16,8,128]{3,2,1,0:T(8,128)(2,1)} %param.9) | copy-start | bytes 393220
  2.3 16.2 %copy-start.5 = (bf16[3,3,128,32]{2,3,1,0:T(8,128)(2,1)S(1)}, bf16[3,3,128,32]{2,3,1,0:T(8,128)(2,1)}, u32[]{:S(2)}) copy-start(bf16[3,3,128,32]{2,3,1,0:T(8,128)(2,1)} %param.11) | copy-start | bytes 221188
  2.3 16.2 %copy-start.6 = (bf16[3,32,128]{2,1,0:T(8,128)(2,1)S(1)}, bf16[3,32,128]{2,1,0:T(8,128)(2,1)}, u32[]{:S(2)}) copy-start(bf16[3,32,128]{2,1,0:T(8,128)(2,1)} %temporal.1) | copy-start | bytes 73732
  2.3 16.2 %copy-start.9 = (bf16[128,8]{0,1:T(8,128)(2,1)S(1)}, bf16[128,8]{0,1:T(8,128)(2,1)}, u32[]{:S(2)}) copy-start(bf16[128,8]{0,1:T(8,128)(2,1)} %param.12) | copy-start | bytes 6148
  2.3 16.4 %copy-start.4 = (bf16[4,16,8,128]{3,2,1,0:T(8,128)(2,1)S(1)}, bf16[4,16,8,128]{3,2,1,0:T(8,128)(2,1)}, u32[]{:S(2)}) copy-start(bf16[4,16,8,128]{3,2,1,0:T(8,128)(2,1)} %param.9) | copy-start | bytes 393220
  2.3 16.4 %copy-start.8 = (s32[3]{0:T(128)S(1)}, s32[3]{0:T(128)}, u32[]{:S(2)}) copy-start(s32[3]{0:T(128)} %steps.5) | copy-start | bytes 40
  3.8 8.7 %collective-permute-start = (bf16[4,112,128]{2,1,0:T(8,128)(2,1)S(1)}, bf16[4,112,128]{2,1,0:T(8,128)(2,1)S(1)}, u32[]{:S(2)}, u32[]{:S(2)}) collective-permute-start(bf16[4,112,128]{2,1,0:T(8,128)(2,1)S(1)} %get-tuple-element.25), channel_id=1, source_target_pairs={{0,1},{1,0},{2,3},{3,2},{4,5},{5,4},{6,7},{7,6},{8,9},{9,8},{10,11... | collective-permute-start | bytes 344072 | tf_op jit(solution)/shard_map/ppermute | solution.py:463
  3.9 8.6 %collective-permute-start.1 = (bf16[4,112,128]{2,1,0:T(8,128)(2,1)S(1)}, bf16[4,112,128]{2,1,0:T(8,128)(2,1)S(1)}, u32[]{:S(2)}, u32[]{:S(2)}) collective-permute-start(bf16[4,112,128]{2,1,0:T(8,128)(2,1)S(1)} %get-tuple-element.26), channel_id=1, source_target_pairs={{1,2},{2,1},{3,4},{4,3},{5,6},{6,5},{9,10},{10,9},{11,12},{12,11},... | collective-permute-start | bytes 344072 | tf_op jit(solution)/shard_map/ppermute | solution.py:464
  9.4 1.2 %copy-start = (bf16[2,4,16,32,128]{4,3,2,1,0:T(8,128)(2,1)S(1)}, bf16[2,4,16,32,128]{4,3,2,1,0:T(8,128)(2,1)}, u32[]{:S(2)}) copy-start(bf16[2,4,16,32,128]{4,3,2,1,0:T(8,128)(2,1)} %noise.7) | copy-start | bytes 3145732
  10.6 0.7 %copy-start.7 = (s32[3]{0:T(128)S(1)}, s32[3]{0:T(128)}, u32[]{:S(2)}) copy-start(s32[3]{0:T(128)} %steps.5) | copy-start | bytes 40
  13.2 9.3 %collective-permute-start.2 = (bf16[2000,128]{1,0:T(8,128)(2,1)S(1)}, bf16[2000,128]{1,0:T(8,128)(2,1)S(1)}, u32[]{:S(2)}, u32[]{:S(2)}) collective-permute-start(bf16[2000,128]{1,0:T(8,128)(2,1)S(1)} %get-tuple-element.27), channel_id=1, source_target_pairs={{0,8},{8,0},{16,24},{24,16},{32,40},{40,32},{48,56},{56,48},{64,72... | collective-permute-start | bytes 1536008 | tf_op jit(solution)/shard_map/ppermute | solution.py:468
  14.5 13.7 %collective-permute-start.3 = (bf16[2000,128]{1,0:T(8,128)(2,1)S(1)}, bf16[2000,128]{1,0:T(8,128)(2,1)S(1)}, u32[]{:S(2)}, u32[]{:S(2)}) collective-permute-start(bf16[2000,128]{1,0:T(8,128)(2,1)S(1)} %get-tuple-element.28), channel_id=1, source_target_pairs={{8,16},{16,8},{24,32},{32,24},{40,48},{48,40},{56,192},{192,56},{7... | collective-permute-start | bytes 1536008 | tf_op jit(solution)/shard_map/ppermute | solution.py:469

commit v5 on v4

--- a/solution.py
+++ b/solution.py
@@ -149,7 +149,7 @@
     return join16(low.astype(F32)[3 * C : 3 * C + CK], cond_row, high.astype(F32)[3 * C : 3 * C + CK])
 
 
-def pack_x_kernel(place, packed, noise, cond, ya, yb, xa, xb, token):
+def pack_x_kernel(place, packed, noise, cond, ya, yb, xb, xa, token):
     lows, highs = halo_columns(place, ya, yb)
 
     def pack_x(out, top):
@@ -378,7 +378,7 @@
 
 
 def main_kernel(
-    place, steps, noise, xa, xb, act, base_own, term, part1, part2, act2_own, wide, wide_cond, wide_temporal,
+    place, steps, noise, xb, xa, act, base_own, term, part1, part2, act2_own, wide, wide_cond, wide_temporal,
     out, outer, base, act2,
 ):
     factors = coefficients(steps[0], steps[1])
@@ -438,7 +438,7 @@
             out[r, i] = out[r, i] + move2 * s
 
 
-def sample(place, steps, noise, xa, xb, parts, weights):
+def sample(place, steps, noise, xb, xa, parts, weights):
     return pl.pallas_call(
         main_kernel,
         out_shape=jax.ShapeDtypeStruct((ROWS, COLS, C, NT), F32),
@@ -452,7 +452,7 @@
         compiler_params=pltpu.CompilerParams(vmem_limit_bytes=VMEM_MOST),
         cost_estimate=pl.CostEstimate(flops=2 << 30, bytes_accessed=5 << 20, transcendentals=5 << 20),
         name="sample_slab",
-    )(place, steps, noise, xa, xb, *parts, *weights)
+    )(place, steps, noise, xb, xa, *parts, *weights)
 
 
 def on_device(latent, sample_noise, cond_field, timesteps, spatial_weight, cond_weight, temporal_weight):
@@ -464,11 +464,11 @@
     yb = lax.ppermute(yb, AXES, swaps_y(1))
     act, base, packed = own(token, timesteps, latent, sample_noise)
     weights = widen(jnp.swapaxes(spatial_weight, 2, 3), cond_weight.T, temporal_weight)
-    xa, xb, token = pack_x(place, packed, sample_noise, cond, ya, yb)
+    xb, xa, token = pack_x(place, packed, sample_noise, cond, ya, yb)
+    xb = lax.ppermute(xb, AXES, swaps_x(1))
     xa = lax.ppermute(xa, AXES, swaps_x(0))
-    xb = lax.ppermute(xb, AXES, swaps_x(1))
     parts = inner(place, timesteps, act, base, cond, ya, yb, weights, token)
-    return sample(place, timesteps, sample_noise, xa, xb, parts, weights)
+    return sample(place, timesteps, sample_noise, xb, xa, parts, weights)
 
 
 def solution(mesh):

time: 35.4 us -> 34.7 us (0.980)
  the two profiles are of different devices: /device:TPU:121 before, /device:TPU:102 now
where the time goes in v5:
time: 34.7 us; the launch traced here: 34.4 us
  Pallas kernels  14.4 us (41%)
  starting transfers between devices  9.94 us (29%)
  waiting for transfers between devices  5.82 us (17%)
  local copies, waits for them, and re-layouts  4.1 us (12%)
    pallas_call x1, Pallas kernels, sample(): pl.pallas_call(main_kernel, out_shape=jax.ShapeDtypeStruct((ROWS, COLS, C...  6.98 us
    ppermute x1, starting transfers between devices, on_device(): yb = lax.ppermute(yb, AXES, swaps_y(1))  5.93 us
    ppermute x1, waiting for transfers between devices, on_device(): xb = lax.ppermute(xb, AXES, swaps_x(1))  5.81 us
    unnamed x20, local copies, waits for them, and re-layouts  4.1 us
    pallas_call x1, Pallas kernels, inner(): pl.pallas_call(inner_kernel, out_shape=(jax.ShapeDtypeStruct((ROWS, WIDE...  3.8 us
    ppermute x1, starting transfers between devices, on_device(): xb = lax.ppermute(xb, AXES, swaps_x(1))  3.72 us
    pallas_call x1, Pallas kernels, pack_y(): pl.pallas_call(pack_y_kernel, out_shape=(y, y, jax.ShapeDtypeStruct((8, N...  1.47 us
    pallas_call x1, Pallas kernels, own(): pl.pallas_call(own_kernel, out_shape=(jax.ShapeDtypeStruct((ROWS, n, NT),...  1.27 us
  transfers between devices with their start and end apart: 4, of which 1 were waited for; matrix products, arithmetic and copies ran while one was open for 0% of the time, Pallas kernels for 15%

profile of v5, /device:TPU:102, one launch (start us, length us, event | category | flops | bytes accessed | tf_op | source)
XLA Modules:
  0.0 34.4 jit_solution(1303578542225495617)
XLA Ops:
  0.0 0.0 copy-start.1
  0.0 0.1 pad_add_fusion.place
  0.1 0.0 copy-start.2
  0.1 1.3 %copy-done.2 = f32[4,16,32,128]{3,2,1,0:T(8,128)S(1)} copy-done((f32[4,16,32,128]{3,2,1,0:T(8,128)S(1)}, f32[4,16,32,128]{3,2,1,0:T(8,128)}, u32[]{:S(2)}) %copy-start.2) | copy-done | bytes 1048600
  1.4 0.0 copy-start.3
  1.4 0.9 %copy-done.3 = bf16[4,16,8,128]{3,2,1,0:T(8,128)(2,1)S(1)} copy-done((bf16[4,16,8,128]{3,2,1,0:T(8,128)(2,1)S(1)}, bf16[4,16,8,128]{3,2,1,0:T(8,128)(2,1)}, u32[]{:S(2)}) %copy-start.3) | copy-done | bytes 131096
  2.3 0.0 copy-start.5
  2.3 0.0 copy-start.6
  2.3 0.0 copy-start.9
  2.3 0.0 copy-start.4
  2.3 0.0 copy-start.8
  2.3 1.5 %pack_columns.1 = (bf16[4,112,128]{2,1,0:T(8,128)(2,1)S(1)}, bf16[4,112,128]{2,1,0:T(8,128)(2,1)S(1)}, f32[8,128]{1,0:T(8,128)S(1)}) custom-call(s32[4]{0:T(128)S(1)} %pad_add_fusion.place, f32[4,16,32,128]{3,2,1,0:T(8,128)S(1)} %copy-done.2, bf16[2,4,16,32,128]{4,3,2,1,0:T(8,128)(2,1)} %noise.7, bf16[4,128,128]{2,1,0:T(8,128)(2,1)S(1)} %bitcast.7), custom_call_target="tpu_custom_call" | custom-call | flops 65536 | bytes 524288 | tf_op jit(solution)/shard_map/pack_columns/pallas_call | solution.py:97
  3.8 0.2 collective-permute-start
  4.0 5.9 %collective-permute-start.1 = (bf16[4,112,128]{2,1,0:T(8,128)(2,1)S(1)}, bf16[4,112,128]{2,1,0:T(8,128)(2,1)S(1)}, u32[]{:S(2)}, u32[]{:S(2)}) collective-permute-start(bf16[4,112,128]{2,1,0:T(8,128)(2,1)S(1)} %get-tuple-element.26), channel_id=1, source_target_pairs={{1,2},{2,1},{3,4},{4,3},{5,6},{6,5},{9,10},{10,9},{11,12},{12,11},... | collective-permute-start | bytes 344072 | tf_op jit(solution)/shard_map/ppermute | solution.py:464
  9.9 0.0 copy-start
  9.9 1.2 %copy-done = bf16[2,4,16,32,128]{4,3,2,1,0:T(8,128)(2,1)S(1)} copy-done((bf16[2,4,16,32,128]{4,3,2,1,0:T(8,128)(2,1)S(1)}, bf16[2,4,16,32,128]{4,3,2,1,0:T(8,128)(2,1)}, u32[]{:S(2)}) %copy-start) | copy-done | bytes 1048600
  11.2 0.0 copy-start.7
  11.2 0.7 %copy-done.7 = s32[3]{0:T(128)S(1)} copy-done((s32[3]{0:T(128)S(1)}, s32[3]{0:T(128)}, u32[]{:S(2)}) %copy-start.7) | copy-done | bytes 36
  11.8 1.3 %own_cells.1 = (bf16[4,512,128]{2,1,0:T(8,128)(2,1)S(1)}, f32[4,512,128]{2,1,0:T(8,128)S(1)}, bf16[4,512,128]{2,1,0:T(8,128)(2,1)S(1)}) custom-call(f32[8,128]{1,0:T(8,128)S(1)} %get-tuple-element.23.token, s32[3]{0:T(128)S(1)} %copy-done.7, f32[4,16,32,128]{3,2,1,0:T(8,128)S(1)} %copy-done.2, bf16[2,4,16,32,128]{4,3,2,1,0:T(8,128)(2,1)S(1)} %copy-done), custom_call_target="tpu_custom_call" | custom-call | flops 16777216 | bytes 4194304 | tf_op jit(solution)/shard_map/own_cells/pallas_call | solution.py:133
  13.1 0.0 collective-permute-done.ya
  13.1 0.0 collective-permute-done.1.yb
  13.1 0.0 copy-done.1
  13.1 0.6 %pack_rows.1 = (bf16[2000,128]{1,0:T(8,128)(2,1)S(1)}, bf16[2000,128]{1,0:T(8,128)(2,1)S(1)}, f32[8,128]{1,0:T(8,128)S(1)}) custom-call(s32[4]{0:T(128)S(1)} %pad_add_fusion.place, bf16[4,512,128]{2,1,0:T(8,128)(2,1)S(1)} %get-tuple-element.24.packed, bf16[2,4,16,32,128]{4,3,2,1,0:T(8,128)(2,1)S(1)} %copy-done.1, bf16[4,128,128]{2,1,0:T(8,128)(2,1)S(1)} %bitcast.8, ...), custom_call_target="tpu_custom_call" | custom-call | flops 262144 | bytes 3145728 | tf_op jit(solution)/shard_map/pack_rows/pallas_call | solution.py:182
  13.8 3.7 %collective-permute-start.2 = (bf16[2000,128]{1,0:T(8,128)(2,1)S(1)}, bf16[2000,128]{1,0:T(8,128)(2,1)S(1)}, u32[]{:S(2)}, u32[]{:S(2)}) collective-permute-start(bf16[2000,128]{1,0:T(8,128)(2,1)S(1)} %get-tuple-element.27), channel_id=1, source_target_pairs={{8,16},{16,8},{24,32},{32,24},{40,48},{48,40},{56,192},{192,56},{7... | collective-permute-start | bytes 1536008 | tf_op jit(solution)/shard_map/ppermute | solution.py:468
  17.5 0.1 collective-permute-start.3
  17.6 0.0 copy-done.5
  17.6 0.0 copy-done.6
  17.6 0.0 copy-done.9
  17.6 0.2 widen_weights.1
  17.8 0.0 copy-done.4
  17.8 0.0 copy-done.8
  17.8 3.8 %inner_rows.1 = (bf16[4,640,128]{2,1,0:T(8,128)(2,1)S(1)}, f32[4,576,128]{2,1,0:T(8,128)S(1)}, f32[4,128,2304]{2,1,0:T(8,128)S(1)}, f32[4,256,1152]{2,1,0:T(8,12...) custom-call(s32[4]{0:T(128)S(1)} %pad_add_fusion.place, s32[3]{0:T(128)S(1)} %copy-done.8, ...), custom_call_target="tpu_custom_call" | custom-call | flops 1073741824 | bytes 4194304 | tf_op jit(solution)/shard_map/inner_rows/pallas_call | solution.py:362
  21.6 5.8 %collective-permute-done.2.xb = bf16[2000,128]{1,0:T(8,128)(2,1)S(1)} collective-permute-done((bf16[2000,128]{1,0:T(8,128)(2,1)S(1)}, bf16[2000,128]{1,0:T(8,128)(2,1)S(1)}, u32[]{:S(2)}, u32[]{:S(2)}) %collective-permute-start.2) | collective-permute-done | bytes 512032 | tf_op jit(solution)/shard_map/ppermute | solution.py:468
  27.4 0.0 collective-permute-done.3.xa
  27.5 7.0 %sample_slab.1 = f32[4,16,32,128]{3,2,1,0:T(8,128)} custom-call(s32[4]{0:T(128)S(1)} %pad_add_fusion.place, s32[3]{0:T(128)S(1)} %copy-done.8, bf16[2,4,16,32,128]{4,3,2,1,0:T(8,128)(2,1)S(1)} %copy-done.1, bf16[2000,128]{1,0:T(8,128)(2,1)S(1)} %collective-permute-done.2.xb, bf16[2000,128]{1,0:T(8,128)(2,1)S(1)} %collective-permute-done.3.xa, ...), custom_call_target="tpu_custom_call" | custom-call | flops 2147483648 | bytes 5242880 | tf_op jit(solution)/shard_map/sample_slab/pallas_call | solution.py:442
Async XLA Ops:
  0.0 13.1 %copy-start.1 = (bf16[2,4,16,32,128]{4,3,2,1,0:T(8,128)(2,1)S(1)}, bf16[2,4,16,32,128]{4,3,2,1,0:T(8,128)(2,1)}, u32[]{:S(2)}) copy-start(bf16[2,4,16,32,128]{4,3,2,1,0:T(8,128)(2,1)} %noise.7) | copy-start | bytes 3145732
  0.1 1.3 %copy-start.2 = (f32[4,16,32,128]{3,2,1,0:T(8,128)S(1)}, f32[4,16,32,128]{3,2,1,0:T(8,128)}, u32[]{:S(2)}) copy-start(f32[4,16,32,128]{3,2,1,0:T(8,128)} %lat.3) | copy-start | bytes 3145732
  1.4 0.9 %copy-start.3 = (bf16[4,16,8,128]{3,2,1,0:T(8,128)(2,1)S(1)}, bf16[4,16,8,128]{3,2,1,0:T(8,128)(2,1)}, u32[]{:S(2)}) copy-start(bf16[4,16,8,128]{3,2,1,0:T(8,128)(2,1)} %param.9) | copy-start | bytes 393220
  2.3 15.3 %copy-start.5 = (bf16[3,3,128,32]{2,3,1,0:T(8,128)(2,1)S(1)}, bf16[3,3,128,32]{2,3,1,0:T(8,128)(2,1)}, u32[]{:S(2)}) copy-start(bf16[3,3,128,32]{2,3,1,0:T(8,128)(2,1)} %param.11) | copy-start | bytes 221188
  2.3 15.3 %copy-start.6 = (bf16[3,32,128]{2,1,0:T(8,128)(2,1)S(1)}, bf16[3,32,128]{2,1,0:T(8,128)(2,1)}, u32[]{:S(2)}) copy-start(bf16[3,32,128]{2,1,0:T(8,128)(2,1)} %temporal.1) | copy-start | bytes 73732
  2.3 15.3 %copy-start.9 = (bf16[128,8]{0,1:T(8,128)(2,1)S(1)}, bf16[128,8]{0,1:T(8,128)(2,1)}, u32[]{:S(2)}) copy-start(bf16[128,8]{0,1:T(8,128)(2,1)} %param.12) | copy-start | bytes 6148
  2.3 15.5 %copy-start.4 = (bf16[4,16,8,128]{3,2,1,0:T(8,128)(2,1)S(1)}, bf16[4,16,8,128]{3,2,1,0:T(8,128)(2,1)}, u32[]{:S(2)}) copy-start(bf16[4,16,8,128]{3,2,1,0:T(8,128)(2,1)} %param.9) | copy-start | bytes 393220
  2.3 15.5 %copy-start.8 = (s32[3]{0:T(128)S(1)}, s32[3]{0:T(128)}, u32[]{:S(2)}) copy-start(s32[3]{0:T(128)} %steps.5) | copy-start | bytes 40
  3.8 9.3 %collective-permute-start = (bf16[4,112,128]{2,1,0:T(8,128)(2,1)S(1)}, bf16[4,112,128]{2,1,0:T(8,128)(2,1)S(1)}, u32[]{:S(2)}, u32[]{:S(2)}) collective-permute-start(bf16[4,112,128]{2,1,0:T(8,128)(2,1)S(1)} %get-tuple-element.25), channel_id=1, source_target_pairs={{0,1},{1,0},{2,3},{3,2},{4,5},{5,4},{6,7},{7,6},{8,9},{9,8},{10,11... | collective-permute-start | bytes 344072 | tf_op jit(solution)/shard_map/ppermute | solution.py:463
  4.0 9.1 %collective-permute-start.1 = (bf16[4,112,128]{2,1,0:T(8,128)(2,1)S(1)}, bf16[4,112,128]{2,1,0:T(8,128)(2,1)S(1)}, u32[]{:S(2)}, u32[]{:S(2)}) collective-permute-start(bf16[4,112,128]{2,1,0:T(8,128)(2,1)S(1)} %get-tuple-element.26), channel_id=1, source_target_pairs={{1,2},{2,1},{3,4},{4,3},{5,6},{6,5},{9,10},{10,9},{11,12},{12,11},... | collective-permute-start | bytes 344072 | tf_op jit(solution)/shard_map/ppermute | solution.py:464
  9.9 1.2 %copy-start = (bf16[2,4,16,32,128]{4,3,2,1,0:T(8,128)(2,1)S(1)}, bf16[2,4,16,32,128]{4,3,2,1,0:T(8,128)(2,1)}, u32[]{:S(2)}) copy-start(bf16[2,4,16,32,128]{4,3,2,1,0:T(8,128)(2,1)} %noise.7) | copy-start | bytes 3145732
  11.2 0.7 %copy-start.7 = (s32[3]{0:T(128)S(1)}, s32[3]{0:T(128)}, u32[]{:S(2)}) copy-start(s32[3]{0:T(128)} %steps.5) | copy-start | bytes 40
  13.8 13.7 %collective-permute-start.2 = (bf16[2000,128]{1,0:T(8,128)(2,1)S(1)}, bf16[2000,128]{1,0:T(8,128)(2,1)S(1)}, u32[]{:S(2)}, u32[]{:S(2)}) collective-permute-start(bf16[2000,128]{1,0:T(8,128)(2,1)S(1)} %get-tuple-element.27), channel_id=1, source_target_pairs={{8,16},{16,8},{24,32},{32,24},{40,48},{48,40},{56,192},{192,56},{7... | collective-permute-start | bytes 1536008 | tf_op jit(solution)/shard_map/ppermute | solution.py:468
  17.5 10.0 %collective-permute-start.3 = (bf16[2000,128]{1,0:T(8,128)(2,1)S(1)}, bf16[2000,128]{1,0:T(8,128)(2,1)S(1)}, u32[]{:S(2)}, u32[]{:S(2)}) collective-permute-start(bf16[2000,128]{1,0:T(8,128)(2,1)S(1)} %get-tuple-element.28), channel_id=1, source_target_pairs={{0,8},{8,0},{16,24},{24,16},{32,40},{40,32},{48,56},{56,48},{64,72... | collective-permute-start | bytes 1536008 | tf_op jit(solution)/shard_map/ppermute | solution.py:469

commit v6 on v5

--- a/solution.py
+++ b/solution.py
@@ -308,6 +308,11 @@
 SECOND = range(COLS // 2)
 
 
+def next_base(x, normed, fresh, factors):
+    keep, move, sigma = factors
+    return keep * x[1 : MID - 1] + move * normed[1 : MID - 1] + sigma * fresh.astype(F32)
+
+
 def next_act(value, row, place):
     left = jnp.where(place[3] == 0, 0.0, 1.0)
     right = jnp.where(place[3] == NGY - 1, 0.0, 1.0)
@@ -320,8 +325,8 @@
 
 
 def inner_kernel(
-    place, steps, act_own, base_own, cond, ya, yb, wide, wide_cond, wide_temporal, token,
-    act, base, term, part1, part2, act2,
+    place, steps, act_own, base_own, noise, cond, ya, yb, wide, wide_cond, wide_temporal, token,
+    act, base, term, part1, part2, act2, base2,
 ):
     del token
     factors = coefficients(steps[0], steps[1])
@@ -349,8 +354,12 @@
     part1[1] = spatial_sum([(0, pick(act, ROWS - 2)), (1, pick(act, ROWS - 1))], FIRST, wide)
     part1[2] = spatial_sum([(2, pick(act, 0))], FIRST, wide)
     part1[3] = spatial_sum([(0, pick(act, ROWS - 1))], FIRST, wide)
+    later = coefficients(steps[1], steps[2])
     for i in range(2):
-        act2[i] = next_act(silu(normalize(base[1 + i].reshape(MID, C, NT))), 1 + i, place)
+        x = base[1 + i].reshape(MID, C, NT)
+        normed = normalize(x)
+        act2[i] = next_act(silu(normed), 1 + i, place)
+        base2[i] = next_base(x, normed, noise[1, 1 + i], later)
     one, two = pick(act2, 0), pick(act2, 1)
     part2[0] = spatial_sum([(2, one)], SECOND, wide)
     part2[1] = spatial_sum([(1, one), (2, two)], SECOND, wide)
@@ -358,7 +367,7 @@
     part2[3] = spatial_sum([(0, two)], SECOND, wide)
 
 
-def inner(place, steps, act, base, cond, ya, yb, weights, token):
+def inner(place, steps, act, base, noise, cond, ya, yb, weights, token):
     return pl.pallas_call(
         inner_kernel,
         out_shape=(
@@ -368,17 +377,18 @@
             jax.ShapeDtypeStruct((4, 2 * FF, MID // 2 * NT), F32),
             jax.ShapeDtypeStruct((4, 2 * FF, COLS // 2 * NT), F32),
             jax.ShapeDtypeStruct((2, MID * C, NT), BF16),
+            jax.ShapeDtypeStruct((2, COLS, C, NT), F32),
         ),
-        in_specs=[smem(), smem()] + [vmem()] * 9,
-        out_specs=(vmem(),) * 6,
+        in_specs=[smem(), smem()] + [vmem()] * 10,
+        out_specs=(vmem(),) * 7,
         compiler_params=pltpu.CompilerParams(vmem_limit_bytes=VMEM_MOST),
         cost_estimate=pl.CostEstimate(flops=1 << 30, bytes_accessed=4 << 20, transcendentals=2 << 20),
         name="inner_rows",
-    )(place, steps, act, base, cond, ya, yb, *weights, token)
+    )(place, steps, act, base, noise, cond, ya, yb, *weights, token)
 
 
 def main_kernel(
-    place, steps, noise, xb, xa, act, base_own, term, part1, part2, act2_own, wide, wide_cond, wide_temporal,
+    place, steps, noise, xb, xa, act, base_own, term, part1, part2, act2_own, base2_own, wide, wide_cond, wide_temporal,
     out, outer, base, act2,
 ):
     factors = coefficients(steps[0], steps[1])
@@ -413,17 +423,13 @@
             given = free + jnp.dot(wide_cond[...], field, preferred_element_type=F32)
         add_sums(temporal_sum(free, given, wide_temporal), base, slot, factors[1])
 
-    keep2, move2, sigma2 = coefficients(steps[1], steps[2])
-    slots = {0: 0, ROWS - 1: 1, -1: 2, ROWS: 3}
-    for r in range(-1, ROWS + 1):
-        x = (base[slots[r]] if r in slots else base_own[r]).reshape(MID, C, NT)
+    later = coefficients(steps[1], steps[2])
+    for r, slot in ((0, 0), (ROWS - 1, 1), (-1, 2), (ROWS, 3)):
+        x = base[slot].reshape(MID, C, NT)
         normed = normalize(x)
-        if r in slots:
-            act2[slots[r]] = next_act(silu(normed), r, place)
-        if 0 <= r < ROWS:
-            out[r] = (
-                keep2 * x[1 : MID - 1] + move2 * normed[1 : MID - 1] + sigma2 * noise[1, r].astype(F32)
-            )
+        act2[slot] = next_act(silu(normed), r, place)
+        if slot < 2:
+            out[r] = next_base(x, normed, noise[1, r], later)
 
     near = (
         [(0, pick(act2, 2)), (1, pick(act2, 0))],
@@ -435,14 +441,15 @@
         free = part2[r] + spatial_sum(near[r], SECOND, wide)
         sums = temporal_sum(free, free + cond_pairs(term[r], 1, COLS // 2), wide_temporal)
         for i, s in enumerate(sums):
-            out[r, i] = out[r, i] + move2 * s
+            own_part = base2_own[r - 1, i] if 0 < r < ROWS - 1 else out[r, i]
+            out[r, i] = own_part + later[1] * s
 
 
 def sample(place, steps, noise, xb, xa, parts, weights):
     return pl.pallas_call(
         main_kernel,
         out_shape=jax.ShapeDtypeStruct((ROWS, COLS, C, NT), F32),
-        in_specs=[smem(), smem()] + [vmem()] * 12,
+        in_specs=[smem(), smem()] + [vmem()] * 13,
         out_specs=vmem(),
         scratch_shapes=[
             pltpu.VMEM((4, WIDE * C, NT), BF16),
@@ -467,7 +474,7 @@
     xb, xa, token = pack_x(place, packed, sample_noise, cond, ya, yb)
     xb = lax.ppermute(xb, AXES, swaps_x(1))
     xa = lax.ppermute(xa, AXES, swaps_x(0))
-    parts = inner(place, timesteps, act, base, cond, ya, yb, weights, token)
+    parts = inner(place, timesteps, act, base, sample_noise, cond, ya, yb, weights, token)
     return sample(place, timesteps, sample_noise, xb, xa, parts, weights)
 
 

time: 34.7 us -> 34.6 us (level)
  transfers between devices with their start and end apart: 4 -> 4, of which waited for: 1 -> 1; matrix products, arithmetic and copies ran while one was open for 0% -> 0% of each run, Pallas kernels for 15% -> 16%
where the time goes in v6:
time: 34.6 us; the launch traced here: 34.4 us
  Pallas kernels  14.4 us (42%)
  starting transfers between devices  9.94 us (29%)
  waiting for transfers between devices  5.69 us (16%)
  local copies, waits for them, and re-layouts  4.1 us (12%)
    pallas_call x1, Pallas kernels, sample(): pl.pallas_call(main_kernel, out_shape=jax.ShapeDtypeStruct((ROWS, COLS, C...  6.92 us
    ppermute x1, starting transfers between devices, on_device(): yb = lax.ppermute(yb, AXES, swaps_y(1))  5.93 us
    ppermute x1, waiting for transfers between devices, on_device(): xb = lax.ppermute(xb, AXES, swaps_x(1))  5.68 us
    unnamed x20, local copies, waits for them, and re-layouts  4.1 us
    pallas_call x1, Pallas kernels, inner(): pl.pallas_call(inner_kernel, out_shape=(jax.ShapeDtypeStruct((ROWS, WIDE...  3.93 us
    ppermute x1, starting transfers between devices, on_device(): xb = lax.ppermute(xb, AXES, swaps_x(1))  3.72 us
    pallas_call x1, Pallas kernels, pack_y(): pl.pallas_call(pack_y_kernel, out_shape=(y, y, jax.ShapeDtypeStruct((8, N...  1.47 us
    pallas_call x1, Pallas kernels, own(): pl.pallas_call(own_kernel, out_shape=(jax.ShapeDtypeStruct((ROWS, n, NT),...  1.27 us
  transfers between devices with their start and end apart: 4, of which 1 were waited for; matrix products, arithmetic and copies ran while one was open for 0% of the time, Pallas kernels for 16%

profile of v6, /device:TPU:102, one launch (start us, length us, event | category | flops | bytes accessed | tf_op | source)
XLA Modules:
  0.0 34.4 jit_solution(14487733824873150017)
XLA Ops:
  0.0 0.0 copy-start.1
  0.0 0.1 pad_add_fusion.place
  0.1 0.0 copy-start.2
  0.1 1.3 %copy-done.2 = f32[4,16,32,128]{3,2,1,0:T(8,128)S(1)} copy-done((f32[4,16,32,128]{3,2,1,0:T(8,128)S(1)}, f32[4,16,32,128]{3,2,1,0:T(8,128)}, u32[]{:S(2)}) %copy-start.2) | copy-done | bytes 1048600
  1.4 0.0 copy-start.3
  1.4 0.9 %copy-done.3 = bf16[4,16,8,128]{3,2,1,0:T(8,128)(2,1)S(1)} copy-done((bf16[4,16,8,128]{3,2,1,0:T(8,128)(2,1)S(1)}, bf16[4,16,8,128]{3,2,1,0:T(8,128)(2,1)}, u32[]{:S(2)}) %copy-start.3) | copy-done | bytes 131096
  2.3 0.0 copy-start.5
  2.3 0.0 copy-start.6
  2.3 0.0 copy-start.9
  2.3 0.0 copy-start.4
  2.3 0.0 copy-start.8
  2.3 1.5 %pack_columns.1 = (bf16[4,112,128]{2,1,0:T(8,128)(2,1)S(1)}, bf16[4,112,128]{2,1,0:T(8,128)(2,1)S(1)}, f32[8,128]{1,0:T(8,128)S(1)}) custom-call(s32[4]{0:T(128)S(1)} %pad_add_fusion.place, f32[4,16,32,128]{3,2,1,0:T(8,128)S(1)} %copy-done.2, bf16[2,4,16,32,128]{4,3,2,1,0:T(8,128)(2,1)} %noise.9, bf16[4,128,128]{2,1,0:T(8,128)(2,1)S(1)} %bitcast.7), custom_call_target="tpu_custom_call" | custom-call | flops 65536 | bytes 524288 | tf_op jit(solution)/shard_map/pack_columns/pallas_call | solution.py:97
  3.8 0.2 collective-permute-start
  4.0 5.9 %collective-permute-start.1 = (bf16[4,112,128]{2,1,0:T(8,128)(2,1)S(1)}, bf16[4,112,128]{2,1,0:T(8,128)(2,1)S(1)}, u32[]{:S(2)}, u32[]{:S(2)}) collective-permute-start(bf16[4,112,128]{2,1,0:T(8,128)(2,1)S(1)} %get-tuple-element.27), channel_id=1, source_target_pairs={{1,2},{2,1},{3,4},{4,3},{5,6},{6,5},{9,10},{10,9},{11,12},{12,11},... | collective-permute-start | bytes 344072 | tf_op jit(solution)/shard_map/ppermute | solution.py:471
  9.9 0.0 copy-start
  9.9 1.2 %copy-done = bf16[2,4,16,32,128]{4,3,2,1,0:T(8,128)(2,1)S(1)} copy-done((bf16[2,4,16,32,128]{4,3,2,1,0:T(8,128)(2,1)S(1)}, bf16[2,4,16,32,128]{4,3,2,1,0:T(8,128)(2,1)}, u32[]{:S(2)}) %copy-start) | copy-done | bytes 1048600
  11.2 0.0 copy-start.7
  11.2 0.7 %copy-done.7 = s32[3]{0:T(128)S(1)} copy-done((s32[3]{0:T(128)S(1)}, s32[3]{0:T(128)}, u32[]{:S(2)}) %copy-start.7) | copy-done | bytes 36
  11.8 1.3 %own_cells.1 = (bf16[4,512,128]{2,1,0:T(8,128)(2,1)S(1)}, f32[4,512,128]{2,1,0:T(8,128)S(1)}, bf16[4,512,128]{2,1,0:T(8,128)(2,1)S(1)}) custom-call(f32[8,128]{1,0:T(8,128)S(1)} %get-tuple-element.24.token, s32[3]{0:T(128)S(1)} %copy-done.7, f32[4,16,32,128]{3,2,1,0:T(8,128)S(1)} %copy-done.2, bf16[2,4,16,32,128]{4,3,2,1,0:T(8,128)(2,1)S(1)} %copy-done), custom_call_target="tpu_custom_call" | custom-call | flops 16777216 | bytes 4194304 | tf_op jit(solution)/shard_map/own_cells/pallas_call | solution.py:133
  13.1 0.0 collective-permute-done.ya
  13.1 0.0 collective-permute-done.1.yb
  13.1 0.0 copy-done.1
  13.1 0.6 %pack_rows.1 = (bf16[2000,128]{1,0:T(8,128)(2,1)S(1)}, bf16[2000,128]{1,0:T(8,128)(2,1)S(1)}, f32[8,128]{1,0:T(8,128)S(1)}) custom-call(s32[4]{0:T(128)S(1)} %pad_add_fusion.place, bf16[4,512,128]{2,1,0:T(8,128)(2,1)S(1)} %get-tuple-element.25.packed, bf16[2,4,16,32,128]{4,3,2,1,0:T(8,128)(2,1)S(1)} %copy-done.1, bf16[4,128,128]{2,1,0:T(8,128)(2,1)S(1)} %bitcast.8, ...), custom_call_target="tpu_custom_call" | custom-call | flops 262144 | bytes 3145728 | tf_op jit(solution)/shard_map/pack_rows/pallas_call | solution.py:182
  13.8 3.7 %collective-permute-start.2 = (bf16[2000,128]{1,0:T(8,128)(2,1)S(1)}, bf16[2000,128]{1,0:T(8,128)(2,1)S(1)}, u32[]{:S(2)}, u32[]{:S(2)}) collective-permute-start(bf16[2000,128]{1,0:T(8,128)(2,1)S(1)} %get-tuple-element.28), channel_id=1, source_target_pairs={{8,16},{16,8},{24,32},{32,24},{40,48},{48,40},{56,192},{192,56},{7... | collective-permute-start | bytes 1536008 | tf_op jit(solution)/shard_map/ppermute | solution.py:475
  17.5 0.1 collective-permute-start.3
  17.6 0.0 copy-done.5
  17.6 0.0 copy-done.6
  17.6 0.0 copy-done.9
  17.6 0.2 widen_weights.1
  17.8 0.0 copy-done.4
  17.8 0.0 copy-done.8
  17.8 3.9 %inner_rows.1 = (bf16[4,640,128]{2,1,0:T(8,128)(2,1)S(1)}, f32[4,576,128]{2,1,0:T(8,128)S(1)}, f32[4,128,2304]{2,1,0:T(8,128)S(1)}, f32[4,256,1152]{2,1,0:T(8,12...) custom-call(s32[4]{0:T(128)S(1)} %pad_add_fusion.place, ...), custom_call_target="tpu_custom_call" | custom-call | flops 1073741824 | bytes 4194304 | tf_op jit(solution)/shard_map/inner_rows/pallas_call | solution.py:371
  21.8 5.7 %collective-permute-done.2.xb = bf16[2000,128]{1,0:T(8,128)(2,1)S(1)} collective-permute-done((bf16[2000,128]{1,0:T(8,128)(2,1)S(1)}, bf16[2000,128]{1,0:T(8,128)(2,1)S(1)}, u32[]{:S(2)}, u32[]{:S(2)}) %collective-permute-start.2) | collective-permute-done | bytes 512032 | tf_op jit(solution)/shard_map/ppermute | solution.py:475
  27.4 0.0 collective-permute-done.3.xa
  27.5 6.9 %sample_slab.1 = f32[4,16,32,128]{3,2,1,0:T(8,128)} custom-call(s32[4]{0:T(128)S(1)} %pad_add_fusion.place, s32[3]{0:T(128)S(1)} %copy-done.8, bf16[2,4,16,32,128]{4,3,2,1,0:T(8,128)(2,1)S(1)} %copy-done.1, bf16[2000,128]{1,0:T(8,128)(2,1)S(1)} %collective-permute-done.2.xb, bf16[2000,128]{1,0:T(8,128)(2,1)S(1)} %collective-permute-done.3.xa, ...), custom_call_target="tpu_custom_call" | custom-call | flops 2147483648 | bytes 5242880 | tf_op jit(solution)/shard_map/sample_slab/pallas_call | solution.py:449
Async XLA Ops:
  0.0 13.1 %copy-start.1 = (bf16[2,4,16,32,128]{4,3,2,1,0:T(8,128)(2,1)S(1)}, bf16[2,4,16,32,128]{4,3,2,1,0:T(8,128)(2,1)}, u32[]{:S(2)}) copy-start(bf16[2,4,16,32,128]{4,3,2,1,0:T(8,128)(2,1)} %noise.9) | copy-start | bytes 3145732
  0.1 1.3 %copy-start.2 = (f32[4,16,32,128]{3,2,1,0:T(8,128)S(1)}, f32[4,16,32,128]{3,2,1,0:T(8,128)}, u32[]{:S(2)}) copy-start(f32[4,16,32,128]{3,2,1,0:T(8,128)} %lat.3) | copy-start | bytes 3145732
  1.4 0.9 %copy-start.3 = (bf16[4,16,8,128]{3,2,1,0:T(8,128)(2,1)S(1)}, bf16[4,16,8,128]{3,2,1,0:T(8,128)(2,1)}, u32[]{:S(2)}) copy-start(bf16[4,16,8,128]{3,2,1,0:T(8,128)(2,1)} %param.9) | copy-start | bytes 393220
  2.3 15.3 %copy-start.5 = (bf16[3,3,128,32]{2,3,1,0:T(8,128)(2,1)S(1)}, bf16[3,3,128,32]{2,3,1,0:T(8,128)(2,1)}, u32[]{:S(2)}) copy-start(bf16[3,3,128,32]{2,3,1,0:T(8,128)(2,1)} %param.11) | copy-start | bytes 221188
  2.3 15.3 %copy-start.6 = (bf16[3,32,128]{2,1,0:T(8,128)(2,1)S(1)}, bf16[3,32,128]{2,1,0:T(8,128)(2,1)}, u32[]{:S(2)}) copy-start(bf16[3,32,128]{2,1,0:T(8,128)(2,1)} %temporal.1) | copy-start | bytes 73732
  2.3 15.3 %copy-start.9 = (bf16[128,8]{0,1:T(8,128)(2,1)S(1)}, bf16[128,8]{0,1:T(8,128)(2,1)}, u32[]{:S(2)}) copy-start(bf16[128,8]{0,1:T(8,128)(2,1)} %param.12) | copy-start | bytes 6148
  2.3 15.5 %copy-start.4 = (bf16[4,16,8,128]{3,2,1,0:T(8,128)(2,1)S(1)}, bf16[4,16,8,128]{3,2,1,0:T(8,128)(2,1)}, u32[]{:S(2)}) copy-start(bf16[4,16,8,128]{3,2,1,0:T(8,128)(2,1)} %param.9) | copy-start | bytes 393220
  2.3 15.5 %copy-start.8 = (s32[3]{0:T(128)S(1)}, s32[3]{0:T(128)}, u32[]{:S(2)}) copy-start(s32[3]{0:T(128)} %steps.5) | copy-start | bytes 40
  3.8 9.3 %collective-permute-start = (bf16[4,112,128]{2,1,0:T(8,128)(2,1)S(1)}, bf16[4,112,128]{2,1,0:T(8,128)(2,1)S(1)}, u32[]{:S(2)}, u32[]{:S(2)}) collective-permute-start(bf16[4,112,128]{2,1,0:T(8,128)(2,1)S(1)} %get-tuple-element.26), channel_id=1, source_target_pairs={{0,1},{1,0},{2,3},{3,2},{4,5},{5,4},{6,7},{7,6},{8,9},{9,8},{10,11... | collective-permute-start | bytes 344072 | tf_op jit(solution)/shard_map/ppermute | solution.py:470
  4.0 9.1 %collective-permute-start.1 = (bf16[4,112,128]{2,1,0:T(8,128)(2,1)S(1)}, bf16[4,112,128]{2,1,0:T(8,128)(2,1)S(1)}, u32[]{:S(2)}, u32[]{:S(2)}) collective-permute-start(bf16[4,112,128]{2,1,0:T(8,128)(2,1)S(1)} %get-tuple-element.27), channel_id=1, source_target_pairs={{1,2},{2,1},{3,4},{4,3},{5,6},{6,5},{9,10},{10,9},{11,12},{12,11},... | collective-permute-start | bytes 344072 | tf_op jit(solution)/shard_map/ppermute | solution.py:471
  9.9 1.2 %copy-start = (bf16[2,4,16,32,128]{4,3,2,1,0:T(8,128)(2,1)S(1)}, bf16[2,4,16,32,128]{4,3,2,1,0:T(8,128)(2,1)}, u32[]{:S(2)}) copy-start(bf16[2,4,16,32,128]{4,3,2,1,0:T(8,128)(2,1)} %noise.9) | copy-start | bytes 3145732
  11.2 0.7 %copy-start.7 = (s32[3]{0:T(128)S(1)}, s32[3]{0:T(128)}, u32[]{:S(2)}) copy-start(s32[3]{0:T(128)} %steps.5) | copy-start | bytes 40
  13.8 13.7 %collective-permute-start.2 = (bf16[2000,128]{1,0:T(8,128)(2,1)S(1)}, bf16[2000,128]{1,0:T(8,128)(2,1)S(1)}, u32[]{:S(2)}, u32[]{:S(2)}) collective-permute-start(bf16[2000,128]{1,0:T(8,128)(2,1)S(1)} %get-tuple-element.28), channel_id=1, source_target_pairs={{8,16},{16,8},{24,32},{32,24},{40,48},{48,40},{56,192},{192,56},{7... | collective-permute-start | bytes 1536008 | tf_op jit(solution)/shard_map/ppermute | solution.py:475
  17.5 10.0 %collective-permute-start.3 = (bf16[2000,128]{1,0:T(8,128)(2,1)S(1)}, bf16[2000,128]{1,0:T(8,128)(2,1)S(1)}, u32[]{:S(2)}, u32[]{:S(2)}) collective-permute-start(bf16[2000,128]{1,0:T(8,128)(2,1)S(1)} %get-tuple-element.29), channel_id=1, source_target_pairs={{0,8},{8,0},{16,24},{24,16},{32,40},{40,32},{48,56},{56,48},{64,72... | collective-permute-start | bytes 1536008 | tf_op jit(solution)/shard_map/ppermute | solution.py:476
